TPU v7x, 32 devices: a whole 2x2x4 slice. The times are simulated.
32 devices in a mesh: frames: 8 (over z, x), pos: 4 (over y, core).
Axes of the slice: x: 2, y: 2, z: 4, core: 2. Of those that a mesh axis runs over, the one named last changes fastest.
Arguments:
- inputs: bfloat16 [1024, 16, 1024], P('frames', None, 'pos'), may hold values from -6 to 6
- counts: int32 [1024], P('frames'), may hold values from 8 to 16, as said below
- gain_attn: float32 [1024], replicated, may hold values from 0.25 to 1.75
- weight_qkv: bfloat16 [1024, 3, 1024], P(None, None, 'pos'), may hold values from -0.1875 to 0.1875
- weight_out: bfloat16 [1024, 1024], replicated, may hold values from -0.375 to 0.375
- gain_ffn: float32 [16, 1024], P('pos'), may hold values from 0.25 to 1.75
- weight_ffn: bfloat16 [4096, 16, 3, 1024], P('frames', 'pos'), may hold values from -0.1875 to 0.1875
- cotangent: bfloat16 [1024, 16, 1024], P('frames', None, 'pos'), may hold values from -6 to 6
Outputs:
- block_out: bfloat16 [1024, 16, 1024], P('frames', None, 'pos')
- input_grad: bfloat16 [1024, 16, 1024], P('frames', None, 'pos')
- gain_attn_grad: float32 [1024], replicated
- qkv_grad: float32 [1024, 3, 1024], P('frames', None, 'pos')
- out_grad: float32 [1024, 1024], replicated
- gain_ffn_grad: float32 [16, 1024], P('pos', 'frames')
- ffn_grad: float32 [4096, 16, 3, 1024], P('frames', 'pos')
Inputs may be any that keep to these rules, and one draw needn't show every extreme that they name: `counts`: each frame's count is 8 or 16; both occur in every draw.
All inputs are finite; a program needn't handle non-finite values.
Results may differ from a plain program's by a relative error of at most 0.017.
Values may be sent and summed in bfloat16 or wider, within the bound.
No kernel may reach another device: no remote copies, remote signals or barrier semaphores. Data moves between devices by JAX's collectives and lax.ppermute only.
A program may use at most 512 MiB of HBM per device.

v0:
```python
import jax
import jax.numpy as jnp
from jax import lax
from jax.sharding import PartitionSpec as P

HEAD_DIM = 64


epsilon = 1e-05
masked_score = -1e30


def ffn_forward(hidden_norm, weight_piece):
    gate_up = jnp.einsum(
        "fkd,nkjd->fkjn", hidden_norm, weight_piece[:, :, :2], preferred_element_type=jnp.float32
    )
    activated = (jax.nn.silu(gate_up[:, :, 0]) * gate_up[:, :, 1]).astype(jnp.bfloat16)
    return jnp.einsum(
        "fkn,nkd->fkd", activated, weight_piece[:, :, 2], preferred_element_type=jnp.float32
    )


def ffn_backward(hidden_norm, branch_grad, weight_piece):
    gate_up = jnp.einsum(
        "fkd,nkjd->fkjn", hidden_norm, weight_piece[:, :, :2], preferred_element_type=jnp.float32
    )
    gate_val = gate_up[:, :, 0]
    up_val = gate_up[:, :, 1]
    sigmoid_val = jax.nn.sigmoid(gate_val)
    activated = (gate_val * sigmoid_val * up_val).astype(jnp.bfloat16)
    branch_part = jnp.einsum(
        "fkn,nkd->fkd", activated, weight_piece[:, :, 2], preferred_element_type=jnp.float32
    )
    act_grad = jnp.einsum(
        "fkd,nkd->fkn", branch_grad, weight_piece[:, :, 2], preferred_element_type=jnp.float32
    )
    gate_grad = act_grad * up_val * sigmoid_val * (1.0 + gate_val * (1.0 - sigmoid_val))
    up_grad = act_grad * gate_val * sigmoid_val
    pair_grad = jnp.stack([gate_grad, up_grad], 2).astype(jnp.bfloat16)
    norm_part = jnp.einsum(
        "fkjn,nkjd->fkd", pair_grad, weight_piece[:, :, :2], preferred_element_type=jnp.float32
    )
    stored_part = jnp.concatenate([pair_grad, activated[:, :, None]], 2)
    return (norm_part, stored_part, branch_part)


def body(inputs, counts, gain_attn, weight_qkv, weight_out, gain_ffn, weight_ffn, cotangent):
    pos_count = lax.axis_size("pos")
    pos_index = lax.axis_index("pos")
    frame_rows, depth_all, feature_part = inputs.shape
    feature_all = feature_part * pos_count
    per_device = depth_all // pos_count
    local_cols = weight_qkv.shape[2]
    local_heads = local_cols // HEAD_DIM
    positions = jnp.arange(depth_all, dtype=jnp.int32)
    live_mask = (positions[None, :] < counts[:, None]).astype(jnp.float32)
    gathered = lax.all_gather(inputs, "pos", axis=2, tiled=True)
    inputs_full = gathered.astype(jnp.float32)
    scale_attn = lax.rsqrt(jnp.mean(inputs_full * inputs_full, axis=-1, keepdims=True) + epsilon)
    normal_attn = inputs_full * scale_attn
    normed = (normal_attn * gain_attn).astype(jnp.bfloat16)
    project = jnp.einsum(
        "fkd,dje->fkje", normed, weight_qkv, preferred_element_type=jnp.float32
    ).astype(jnp.bfloat16)
    shaped = project.reshape(frame_rows, depth_all, 3, local_heads, HEAD_DIM)
    query_heads = shaped[:, :, 0]
    key_heads = shaped[:, :, 1]
    value_heads = shaped[:, :, 2]
    factor = HEAD_DIM ** (-0.5)
    scores = (
        jnp.einsum("fihe,fjhe->fhij", query_heads, key_heads, preferred_element_type=jnp.float32)
        * factor
    )
    allowed = (
        (positions[None, None, :] <= positions[None, :, None])
        & (positions[None, None, :] < counts[:, None, None])
    )[:, None]
    scores = jnp.where(allowed, scores, masked_score)
    top_score = jnp.max(scores, axis=-1, keepdims=True)
    exp_score = jnp.exp(scores - top_score)
    attn_probs = exp_score / jnp.sum(exp_score, axis=-1, keepdims=True)
    probs_low = attn_probs.astype(jnp.bfloat16)
    head_mixed = jnp.einsum(
        "fhij,fjhe->fihe", probs_low, value_heads, preferred_element_type=jnp.float32
    )
    head_mixed = head_mixed.astype(jnp.bfloat16).reshape(frame_rows, depth_all, local_cols)
    arrived = lax.all_to_all(head_mixed, "pos", split_axis=1, concat_axis=2, tiled=True)
    first_row = pos_index * per_device
    resid_rows = lax.dynamic_slice_in_dim(inputs_full, first_row, per_device, 1)
    live_rows = lax.dynamic_slice_in_dim(live_mask, first_row, per_device, 1)[:, :, None]
    attended = jnp.einsum("fkd,de->fke", arrived, weight_out, preferred_element_type=jnp.float32)
    hidden = resid_rows + attended
    scale_ffn = lax.rsqrt(jnp.mean(hidden * hidden, axis=-1, keepdims=True) + epsilon)
    normal_ffn = hidden * scale_ffn
    hidden_norm = (normal_ffn * gain_ffn[None]).astype(jnp.bfloat16)
    cot_rows = lax.all_to_all(cotangent, "pos", split_axis=1, concat_axis=2, tiled=True)
    branch_grad = cot_rows * live_rows.astype(jnp.bfloat16)
    branch_out = ffn_forward(hidden_norm, lax.all_gather(weight_ffn, "frames", axis=0, tiled=True))
    block_rows = (live_rows * (hidden + branch_out)).astype(jnp.bfloat16)
    block_out = lax.all_to_all(block_rows, "pos", split_axis=2, concat_axis=1, tiled=True)
    norm_part, stored_part, branch_part = ffn_backward(
        hidden_norm, branch_grad, lax.all_gather(weight_ffn, "frames", axis=0, tiled=True)
    )
    gate_term = jnp.einsum(
        "fkjn,fkd->nkjd", stored_part[:, :, :2], hidden_norm, preferred_element_type=jnp.float32
    )
    down_term = jnp.einsum(
        "fkn,fkd->nkd", stored_part[:, :, 2], branch_grad, preferred_element_type=jnp.float32
    )
    ffn_grad = lax.psum_scatter(
        jnp.concatenate([gate_term, down_term[:, :, None]], 2).astype(jnp.bfloat16),
        "frames",
        scatter_dimension=0,
        tiled=True,
    ).astype(jnp.float32)
    scaled_grad = gain_ffn[None] * norm_part
    row_mean = jnp.mean(normal_ffn * scaled_grad, axis=-1, keepdims=True)
    hidden_grad = live_rows * cot_rows.astype(jnp.float32) + scale_ffn * (
        scaled_grad - normal_ffn * row_mean
    )
    hidden_low = hidden_grad.astype(jnp.bfloat16)
    gain_ffn_part = jnp.sum(norm_part * normal_ffn, axis=0)
    out_weight_part = jnp.einsum(
        "fkd,fke->de", arrived, hidden_low, preferred_element_type=jnp.float32
    )
    mixed_grad = jnp.einsum(
        "fke,de->fkd", hidden_low, weight_out, preferred_element_type=jnp.float32
    ).astype(jnp.bfloat16)
    resid_back, mixed_back = (
        lax.all_to_all(hidden_low, "pos", split_axis=2, concat_axis=1, tiled=True),
        lax.all_to_all(mixed_grad, "pos", split_axis=2, concat_axis=1, tiled=True),
    )
    mixed_heads = mixed_back.reshape(frame_rows, depth_all, local_heads, HEAD_DIM)
    probs_grad = jnp.einsum(
        "fihe,fjhe->fhij", mixed_heads, value_heads, preferred_element_type=jnp.float32
    )
    value_grad = jnp.einsum(
        "fhij,fihe->fjhe", probs_low, mixed_heads, preferred_element_type=jnp.float32
    )
    score_grad = attn_probs * (
        probs_grad - jnp.sum(attn_probs * probs_grad, axis=-1, keepdims=True)
    )
    score_low = score_grad.astype(jnp.bfloat16)
    query_grad = (
        jnp.einsum("fhij,fjhe->fihe", score_low, key_heads, preferred_element_type=jnp.float32)
        * factor
    )
    key_grad = (
        jnp.einsum("fhij,fihe->fjhe", score_low, query_heads, preferred_element_type=jnp.float32)
        * factor
    )
    project_grad = jnp.stack([query_grad, key_grad, value_grad], 2)
    project_grad = project_grad.reshape(frame_rows, depth_all, 3, local_cols).astype(jnp.bfloat16)
    qkv_part = jnp.einsum("fkd,fkje->dje", normed, project_grad, preferred_element_type=jnp.float32)
    normed_grad = jnp.einsum(
        "fkje,dje->fkd", project_grad, weight_qkv, preferred_element_type=jnp.float32
    )
    gain_attn_part = jnp.sum(normed_grad * normal_attn, axis=(0, 1))
    scaled_attn = normed_grad * gain_attn
    row_partial = jnp.sum(normal_attn * scaled_attn, axis=-1)
    scaled_local = lax.psum_scatter(
        scaled_attn.astype(jnp.bfloat16), "pos", scatter_dimension=2, tiled=True
    ).astype(jnp.float32)
    row_total = lax.psum(row_partial, "pos")
    normal_local = lax.dynamic_slice_in_dim(normal_attn, pos_index * feature_part, feature_part, 2)
    input_grad = resid_back.astype(jnp.float32) + scale_attn * (
        scaled_local - normal_local * (row_total[:, :, None] / feature_all)
    )
    input_grad = input_grad.astype(jnp.bfloat16)
    shared = (
        lax.psum_scatter(
            qkv_part.astype(jnp.bfloat16), "frames", scatter_dimension=0, tiled=True
        ).astype(jnp.float32),
        lax.psum_scatter(
            gain_ffn_part.astype(jnp.bfloat16), "frames", scatter_dimension=1, tiled=True
        ).astype(jnp.float32),
    )
    replicated = lax.psum((out_weight_part, gain_attn_part), ("frames", "pos"))
    return (block_out, input_grad, replicated[1], shared[0], replicated[0], shared[1], ffn_grad)


def solution(mesh):
    placed = (
        P("frames", None, "pos"),
        P("frames"),
        P(),
        P(None, None, "pos"),
        P(),
        P("pos", None),
        P("frames", "pos", None, None),
        P("frames", None, "pos"),
    )
    return jax.shard_map(
        body,
        mesh=mesh,
        in_specs=placed,
        out_specs=(
            P("frames", None, "pos"),
            P("frames", None, "pos"),
            P(),
            P("frames", None, "pos"),
            P(),
            P("pos", "frames"),
            P("frames", "pos", None, None),
        ),
        check_vma=False,
    )
```

profile of v0, /device:TPU:0, one launch (start us, length us, event | category | flops | bytes accessed | tf_op | source)
XLA Modules:
  0.0 3946.4 jit_solution(8670350155326851712)
XLA Ops:
  10.0 13.4 copy.117
  25.9 4.6 all-to-all-start.2
  31.7 27.4 all-gather.3.cloned.1.call-done
  59.1 3.2 multiply_reduce_fusion.1
  63.0 6.3 convolution_convert_fusion
  69.3 4.8 copy.108
  74.1 3.9 fusion.73
  78.0 4.8 copy.163
  82.8 4.8 copy.164
  87.5 3.5 fusion.29
  91.0 3.6 fusion.74
  94.6 4.7 copy.162
  99.4 5.0 convert_bitcast_fusion.3
  104.4 3.9 copy.114
  108.3 4.7 all-to-all-start
  116.7 6.6 convert_element_type.87
  123.3 4.3 all-to-all-done
  132.6 4.5 multiply_reduce_fusion.4
  137.1 1820.3 %all-gather.5.cloned.1.call-done = bf16[4096,4,3,1024]{3,0,2,1:T(8,128)(2,1)} async-done(((bf16[512,4,3,1024]{3,0,2,1:T(8,128)(2,1)}), bf16[4096,4,3,1024]{3,0,2,1:T(8,128)(2,1)}) %all-gather.5.cloned.1.call-update) | async-done | bytes 100663312 | tf_op jit(solution)/shard_map/all_gather | solution.py:98
  1957.4 18.9 fusion.3
  1976.3 33.6 convolution_bitcast_fusion
  2009.9 14.7 fusion.15
  2024.6 27.2 fusion.21
  2051.8 2.9 add_convert_fusion
  2060.4 3.5 all-to-all-start.4
  2064.9 13.4 all-to-all-done.4
  2078.6 3.7 copy.129
  2082.3 5.6 convert_bitcast_fusion.2
  2095.7 4.1 copy.134
  2102.0 4.0 copy.131
  2106.0 3.1 copy.132
  2113.2 7.4 bitcast_convert_fusion
  2120.7 9.8 fusion.5
  2131.2 16.5 convert_bitcast_fusion.1
  2147.6 30.0 convert_bitcast_fusion
  2177.6 67.9 %pad_maximum_fusion = bf16[4096,4,3,1024]{0,3,2,1:T(8,128)(2,1)} fusion(bf16[4096,4,1,1024]{0,3,2,1:T(8,128)(2,1)} %convert_bitcast_fusion.1, bf16[4096,4,2,1024]{0,3,2,1:T(8,128)(2,1)} %convert_bitcast_fusion), kind=kLoop, calls=%fused_computation.1 | loop fusion | flops 50331648 | bytes 201326592 | tf_op jit(solution)/shard_map/concatenate | solution.py:111
  2246.2 16.2 fusion.23
  2265.0 3.5 all-to-all-start.1
  2268.6 3.3 convolution_bitcast_fusion.1
  2273.3 9.6 all-to-all-done.1
  2282.9 3.5 all-to-all-start.3
  2290.1 10.8 all-to-all-done.3
  2301.5 43.4 %psum.22 = f32[1024]{0:T(1024)} all-reduce(f32[1024]{0:T(1024)S(1)} %copy-done.25), channel_id=1, replica_groups=mesh['frames'=8,'pos'=4] {'frames','pos'}, use_global_device_ids=true, to_apply=%region_10.11 | all-reduce | flops 1024 | bytes 8192 | tf_op jit(solution)/shard_map/psum | solution.py:178
  2344.8 6.2 psum.21
  2356.7 1430.3 %reduce-scatter.11.cloned.1.call-done = bf16[512,4,3,1024]{0,3,2,1:T(8,128)(2,1)} async-done(((bf16[4096,4,3,1024]{0,3,2,1:T(8,128)(2,1)}), bf16[512,4,3,1024]{0,3,2,1:T(8,128)(2,1)}) %reduce-scatter.11.cloned.1.call-update) | async-done | bytes 12582928 | tf_op jit(solution)/shard_map/reduce_scatter | solution.py:110
  3786.9 23.6 copy.145
  3810.5 123.8 %all-reduce.2.cloned.1.call-done = f32[1024,1024]{1,0:T(8,128)} async-done(((f32[1024,1024]{1,0:T(8,128)}), f32[1024,1024]{1,0:T(8,128)}) %all-reduce.2.cloned.1.call-update) | async-done | bytes 4194320 | tf_op jit(solution)/shard_map/psum | solution.py:178
  3934.4 4.8 copy.178
  (113 shorter events, 51.9 us)
Async XLA Ops:
  7.2 125.4 %copy-start = (bf16[1024,1024]{1,0:T(8,128)(2,1)S(1)}, bf16[1024,1024]{1,0:T(8,128)(2,1)}, u32[]{:S(2)}) copy-start(bf16[1024,1024]{1,0:T(8,128)(2,1)} %param.12) | copy-start | bytes 6291460
  7.2 52.0 %all-gather.3.cloned.1.call-start = ((), (), s32[]{:S(2)}) async-start(), calls=%async_computation.9 | async-start | bytes 5242880 | tf_op jit(solution)/shard_map/all_gather | solution.py:57
  9.9 1947.4 %all-gather.5.cloned.1.call-start = ((), (), s32[]{:S(2)}) async-start(), calls=%async_computation.10 | async-start | bytes 113246208 | tf_op jit(solution)/shard_map/all_gather | solution.py:98
  23.3 1.2 copy-start.13
  24.6 5.9 copy-start.26
  24.6 38.4 copy-start.27
  25.9 82.4 %all-to-all-start.2 = ((bf16[128,16,256]{2,0,1:T(8,128)(2,1)}), bf16[128,16,256]{2,0,1:T(8,128)(2,1)S(1)}, u32[]{:S(2)}, u32[]{:S(2)}) async-start(bf16[128,16,256]{2,0,1:T(8,128)(2,1)} %copy.121), calls=%async_computation.2 | async-start | bytes 2097152 | tf_op jit(solution)/shard_map/all_to_all | solution.py:96
  59.1 3.8 copy-start.5
  62.4 0.6 copy-start.19
  87.5 3.5 copy-start.16
  108.3 19.2 all-to-all-start
  113.1 1844.3 %copy-start.17 = (bf16[128,4]{0,1:T(4,128)(2,1)}, bf16[128,4]{0,1:T(4,128)(2,1)S(1)}, u32[]{:S(2)}) copy-start(bf16[128,4]{0,1:T(4,128)(2,1)S(1)} %get-tuple-element.47) | copy-start | bytes 3076
  113.1 1938.6 %copy-start.22 = (f32[128,4]{0,1:T(4,128)}, f32[128,4]{0,1:T(4,128)S(1)}, u32[]{:S(2)}) copy-start(f32[128,4]{0,1:T(4,128)S(1)} %get-tuple-element.48) | copy-start | bytes 6148
  1957.4 18.9 copy-start.12
  2054.7 1.0 copy-start.7
  2060.4 18.0 all-to-all-start.4
  2063.9 222.6 %reduce-scatter.13.cloned.1.call-start = ((), (), s32[]{:S(2)}) async-start(), calls=%async_computation.15 | async-start | bytes 294912
  2064.9 286.2 %reduce-scatter.9.cloned.1.call-start = ((), (), s32[]{:S(2)}) async-start(), calls=%async_computation.12 | async-start | bytes 1769472 | tf_op jit(solution)/shard_map/reduce_scatter | solution.py:171
  2082.3 5.6 copy-start.9
  2082.3 5.6 copy-start.10
  2082.3 5.6 copy-start.11
  2089.5 1.6 copy-start.3
  2091.1 2.6 copy-start.4
  2095.7 10.3 copy-start.6
  2106.0 7.1 copy-start.20
  2106.0 7.1 copy-start.28
  2109.1 4.1 copy-start.15
  2120.6 232.2 %reduce-scatter.7.cloned.1.call-start = ((), (), s32[]{:S(2)}) async-start(), calls=%async_computation.11 | async-start | bytes 5242880 | tf_op jit(solution)/shard_map/reduce_scatter | solution.py:161
  2130.5 0.6 copy-start.18
  2130.6 1656.4 %reduce-scatter.11.cloned.1.call-start = ((), (), s32[]{:S(2)}) async-start(), calls=%async_computation.14 | async-start | bytes 113246208 | tf_op jit(solution)/shard_map/reduce_scatter | solution.py:110
  2131.2 16.5 copy-start.2
  2245.5 0.7 copy-start.23
  2262.4 6.1 copy-start.8
  2262.4 6.1 copy-start.14
  2265.0 18.0 all-to-all-start.1
  2268.5 1665.9 %all-reduce.2.cloned.1.call-start = ((), (), s32[]{:S(2)}) async-start(), calls=%async_computation.13 | async-start | bytes 8388608 | tf_op jit(solution)/shard_map/psum | solution.py:178
  2282.9 18.0 all-to-all-start.3
  2286.5 15.0 copy-start.25
  2286.5 58.4 %copy-start.24 = (f32[128,16]{0,1:T(8,128)S(1)}, f32[128,16]{0,1:T(8,128)}, u32[]{:S(2)}) copy-start(f32[128,16]{0,1:T(8,128)} %get-tuple-element.36) | copy-start | bytes 24580
  2286.5 66.3 %copy-start.21 = (f32[128,16]{0,1:T(8,128)S(1)}, f32[128,16]{0,1:T(8,128)}, u32[]{:S(2)}) copy-start(f32[128,16]{0,1:T(8,128)} %copy-done.19) | copy-start | bytes 24580
  3786.9 152.2 %copy-start.1 = (bf16[1024,1024]{1,0:T(8,128)(2,1)S(1)}, bf16[1024,1024]{1,0:T(8,128)(2,1)}, u32[]{:S(2)}) copy-start(bf16[1024,1024]{1,0:T(8,128)(2,1)} %param.12) | copy-start | bytes 6291460
Sparse Core Ops, SparseCore 0:
  10.1 48.9 all-gather.2
  61.3 1896.0 all-gather.4
  2068.6 61.6 reduce-scatter.12
  2133.6 64.5 reduce-scatter.8
  2201.3 43.4 reduce-scatter.6
  2248.5 1538.3 reduce-scatter.10
  3793.4 140.9 all-reduce.1
where the time goes:
time: 3950 us
  waiting for transfers between devices  3440 us (87%)
  matrix products  196 us (5%)
  local copies, waits for them, and re-layouts  119 us (3%)
  other arithmetic  106 us (3%)
  blocking collectives  49.6 us (1%)
    all_gather x1, waiting for transfers between devices, body(): lax.all_gather(weight_ffn, 'frames', axis=0, tiled=True)  1820 us
    reduce_scatter x1, waiting for transfers between devices, body(): lax.psum_scatter(jnp.concatenate([gate_term, down_term[:, :, None]], 2).a...  1430 us
    psum x1, waiting for transfers between devices, body(): replicated = lax.psum((out_weight_part, gain_attn_part), ('frames', 'pos'))  124 us
  transfers between devices with their start and end apart: 12, of which 8 were waited for; matrix products, arithmetic and copies ran while one was open for 8% of the time, Pallas kernels for 0%

commit v1 on v0

--- a/solution.py
+++ b/solution.py
@@ -8,40 +8,6 @@
 
 epsilon = 1e-05
 masked_score = -1e30
-
-
-def ffn_forward(hidden_norm, weight_piece):
-    gate_up = jnp.einsum(
-        "fkd,nkjd->fkjn", hidden_norm, weight_piece[:, :, :2], preferred_element_type=jnp.float32
-    )
-    activated = (jax.nn.silu(gate_up[:, :, 0]) * gate_up[:, :, 1]).astype(jnp.bfloat16)
-    return jnp.einsum(
-        "fkn,nkd->fkd", activated, weight_piece[:, :, 2], preferred_element_type=jnp.float32
-    )
-
-
-def ffn_backward(hidden_norm, branch_grad, weight_piece):
-    gate_up = jnp.einsum(
-        "fkd,nkjd->fkjn", hidden_norm, weight_piece[:, :, :2], preferred_element_type=jnp.float32
-    )
-    gate_val = gate_up[:, :, 0]
-    up_val = gate_up[:, :, 1]
-    sigmoid_val = jax.nn.sigmoid(gate_val)
-    activated = (gate_val * sigmoid_val * up_val).astype(jnp.bfloat16)
-    branch_part = jnp.einsum(
-        "fkn,nkd->fkd", activated, weight_piece[:, :, 2], preferred_element_type=jnp.float32
-    )
-    act_grad = jnp.einsum(
-        "fkd,nkd->fkn", branch_grad, weight_piece[:, :, 2], preferred_element_type=jnp.float32
-    )
-    gate_grad = act_grad * up_val * sigmoid_val * (1.0 + gate_val * (1.0 - sigmoid_val))
-    up_grad = act_grad * gate_val * sigmoid_val
-    pair_grad = jnp.stack([gate_grad, up_grad], 2).astype(jnp.bfloat16)
-    norm_part = jnp.einsum(
-        "fkjn,nkjd->fkd", pair_grad, weight_piece[:, :, :2], preferred_element_type=jnp.float32
-    )
-    stored_part = jnp.concatenate([pair_grad, activated[:, :, None]], 2)
-    return (norm_part, stored_part, branch_part)
 
 
 def body(inputs, counts, gain_attn, weight_qkv, weight_out, gain_ffn, weight_ffn, cotangent):
@@ -95,24 +61,42 @@
     hidden_norm = (normal_ffn * gain_ffn[None]).astype(jnp.bfloat16)
     cot_rows = lax.all_to_all(cotangent, "pos", split_axis=1, concat_axis=2, tiled=True)
     branch_grad = cot_rows * live_rows.astype(jnp.bfloat16)
-    branch_out = ffn_forward(hidden_norm, lax.all_gather(weight_ffn, "frames", axis=0, tiled=True))
+    grad_all = lax.all_gather(branch_grad, "frames", axis=0, tiled=True)
+    norm_all = lax.all_gather(hidden_norm, "frames", axis=0, tiled=True)
+    gate_up = jnp.einsum(
+        "fkd,nkjd->fkjn", norm_all, weight_ffn[:, :, :2], preferred_element_type=jnp.float32
+    )
+    gate_val = gate_up[:, :, 0]
+    up_val = gate_up[:, :, 1]
+    sigmoid_val = jax.nn.sigmoid(gate_val)
+    activated = (gate_val * sigmoid_val * up_val).astype(jnp.bfloat16)
+    act_grad = jnp.einsum(
+        "fkd,nkd->fkn", grad_all, weight_ffn[:, :, 2], preferred_element_type=jnp.float32
+    )
+    gate_grad = act_grad * up_val * sigmoid_val * (1.0 + gate_val * (1.0 - sigmoid_val))
+    up_grad = act_grad * gate_val * sigmoid_val
+    pair_grad = jnp.stack([gate_grad, up_grad], 2).astype(jnp.bfloat16)
+    norm_sum = jnp.einsum(
+        "fkjn,nkjd->fkd", pair_grad, weight_ffn[:, :, :2], preferred_element_type=jnp.float32
+    ).astype(jnp.bfloat16)
+    norm_part = lax.psum_scatter(norm_sum, "frames", scatter_dimension=0, tiled=True).astype(
+        jnp.float32
+    )
+    branch_sum = jnp.einsum(
+        "fkn,nkd->fkd", activated, weight_ffn[:, :, 2], preferred_element_type=jnp.float32
+    ).astype(jnp.bfloat16)
+    branch_out = lax.psum_scatter(branch_sum, "frames", scatter_dimension=0, tiled=True).astype(
+        jnp.float32
+    )
     block_rows = (live_rows * (hidden + branch_out)).astype(jnp.bfloat16)
     block_out = lax.all_to_all(block_rows, "pos", split_axis=2, concat_axis=1, tiled=True)
-    norm_part, stored_part, branch_part = ffn_backward(
-        hidden_norm, branch_grad, lax.all_gather(weight_ffn, "frames", axis=0, tiled=True)
-    )
     gate_term = jnp.einsum(
-        "fkjn,fkd->nkjd", stored_part[:, :, :2], hidden_norm, preferred_element_type=jnp.float32
+        "fkjn,fkd->nkjd", pair_grad, norm_all, preferred_element_type=jnp.float32
     )
     down_term = jnp.einsum(
-        "fkn,fkd->nkd", stored_part[:, :, 2], branch_grad, preferred_element_type=jnp.float32
+        "fkn,fkd->nkd", activated, grad_all, preferred_element_type=jnp.float32
     )
-    ffn_grad = lax.psum_scatter(
-        jnp.concatenate([gate_term, down_term[:, :, None]], 2).astype(jnp.bfloat16),
-        "frames",
-        scatter_dimension=0,
-        tiled=True,
-    ).astype(jnp.float32)
+    ffn_grad = jnp.concatenate([gate_term, down_term[:, :, None]], 2)
     scaled_grad = gain_ffn[None] * norm_part
     row_mean = jnp.mean(normal_ffn * scaled_grad, axis=-1, keepdims=True)
     hidden_grad = live_rows * cot_rows.astype(jnp.float32) + scale_ffn * (
@@ -175,8 +159,12 @@
             gain_ffn_part.astype(jnp.bfloat16), "frames", scatter_dimension=1, tiled=True
         ).astype(jnp.float32),
     )
-    replicated = lax.psum((out_weight_part, gain_attn_part), ("frames", "pos"))
-    return (block_out, input_grad, replicated[1], shared[0], replicated[0], shared[1], ffn_grad)
+    out_low = lax.psum_scatter(
+        out_weight_part.astype(jnp.bfloat16), ("frames", "pos"), scatter_dimension=0, tiled=True
+    )
+    out_grad = lax.all_gather(out_low, ("frames", "pos"), axis=0, tiled=True).astype(jnp.float32)
+    gain_attn_grad = lax.psum(gain_attn_part, ("frames", "pos"))
+    return (block_out, input_grad, gain_attn_grad, shared[0], out_grad, shared[1], ffn_grad)
 
 
 def solution(mesh):

time: 3950 us -> 1120 us (0.28)
  waiting for transfers between devices: 3440 us -> 693 us
  other arithmetic: 106 us -> 54.9 us
    all_gather x1 -> x3, waiting for transfers between devices: 1820 us -> 218 us  [the longest x1 92.4 us: body(): grad_all = lax.all_gather(branch_grad, 'frames', axis=0, tiled=True)]
    reduce_scatter x1 -> x3, waiting for transfers between devices: 1430 us -> 359 us  [the longest x1 150 us: body(): lax.psum_scatter(branch_sum, 'frames', scatter_dimension=0, tiled=True)]
    psum x1 -> x0, waiting for transfers between devices: 124 us -> none  [body(): replicated = lax.psum((out_weight_part, gain_attn_part), ('frames', 'pos'))]
    concatenate x1, other arithmetic: 67.9 us -> 18.2 us  [body(): ffn_grad = jnp.concatenate([gate_term, down_term[:, :, None]], 2)]
    reduce_scatter x1, waiting for transfers between devices: 0.01 us -> 41.7 us  [body(): lax.psum_scatter(scaled_attn.astype(jnp.bfloat16), 'pos', scatter_dimensi...]
  transfers between devices with their start and end apart: 12 -> 15, of which waited for: 8 -> 12; matrix products, arithmetic and copies ran while one was open for 8% -> 20% of each run, Pallas kernels for 0% -> 0%
where the time goes in v1:
time: 1120 us; the launch traced here: 1110 us
  waiting for transfers between devices  693 us (62%)
  matrix products  169 us (15%)
  local copies, waits for them, and re-layouts  115 us (10%)
  other arithmetic  54.9 us (5%)
  blocking collectives  45.1 us (4%)
  starting transfers between devices  19.3 us (2%)
  between operations  15 us (1%)
    reduce_scatter x1, waiting for transfers between devices, body(): lax.psum_scatter(branch_sum, 'frames', scatter_dimension=0, tiled=True)  150 us
    reduce_scatter x1, waiting for transfers between devices, body(): lax.psum_scatter(norm_sum, 'frames', scatter_dimension=0, tiled=True)  136 us
    all_gather x1, waiting for transfers between devices, body(): grad_all = lax.all_gather(branch_grad, 'frames', axis=0, tiled=True)  92.4 us
    all_gather x1, waiting for transfers between devices, body(): norm_all = lax.all_gather(hidden_norm, 'frames', axis=0, tiled=True)  86.8 us
    reduce_scatter x1, waiting for transfers between devices, body(): lax.psum_scatter(out_weight_part.astype(jnp.bfloat16), ('frames', 'pos'),...  73.2 us
    unnamed x55, local copies, waits for them, and re-layouts  55.2 us
    reduce_scatter x1, waiting for transfers between devices, body(): lax.psum_scatter(scaled_attn.astype(jnp.bfloat16), 'pos', scatter_dimensi...  41.7 us
    all_gather x1, waiting for transfers between devices, body(): lax.all_gather(out_low, ('frames', 'pos'), axis=0, tiled=True)  38.8 us
  transfers between devices with their start and end apart: 15, of which 12 were waited for; matrix products, arithmetic and copies ran while one was open for 20% of the time, Pallas kernels for 0%

profile of v1, /device:TPU:0, one launch (start us, length us, event | category | flops | bytes accessed | tf_op | source)
XLA Modules:
  0.0 1110.7 jit_solution(8024692748807636193)
XLA Ops:
  11.8 36.1 %all-gather.5.cloned.1.call-done = bf16[128,16,1024]{2,0,1:T(8,128)(2,1)} async-done(((bf16[128,16,256]{2,0,1:T(8,128)(2,1)}), bf16[128,16,1024]{2,0,1:T(8,128)(2,1)}) %all-gather.5.cloned.1.call-update) | async-done | bytes 4194320 | tf_op jit(solution)/shard_map/all_gather | solution.py:23
  47.9 3.2 multiply_reduce_fusion.1
  51.4 6.3 convolution_convert_fusion
  57.7 4.6 copy.111
  62.3 4.2 fusion.73
  66.5 4.7 copy.166
  71.2 4.7 copy.168
  75.9 3.7 copy.167
  79.6 3.5 fusion.37
  83.1 5.3 fusion.74
  92.5 3.9 copy.117
  96.4 3.5 all-to-all-start
  100.4 6.7 convert_element_type.106
  107.1 7.3 all-to-all-done
  118.3 3.3 multiply_reduce_fusion.3
  125.7 3.5 all-to-all-start.2
  129.3 14.4 %all-to-all-done.2 = bf16[128,16,256]{2,0,1:T(8,128)(2,1)S(1)} async-done(((bf16[128,16,256]{2,0,1:T(8,128)(2,1)}), bf16[128,16,256]{2,0,1:T(8,128)(2,1)S(1)}, u32[]{:S(2)}, u32[]{:S(2)}) %all-to-all-start.2) | async-done | bytes 1048608 | tf_op jit(solution)/shard_map/all_to_all | solution.py:62
  148.4 8.5 slice.26
  156.9 5.7 slice.29
  162.6 86.8 %all-gather.7.cloned.1.call-done = bf16[1024,4,1024]{2,0,1:T(8,128)(2,1)} async-done(((bf16[128,4,1024]{2,0,1:T(8,128)(2,1)}), bf16[1024,4,1024]{2,0,1:T(8,128)(2,1)}) %all-gather.7.cloned.1.call-update) | async-done | bytes 8388624 | tf_op jit(solution)/shard_map/all_gather | solution.py:65
  249.4 32.9 %convolution_bitcast_fusion.1 = f32[1024,4,2,512]{3,0,2,1:T(8,128)} fusion(bf16[512,4,2,1024]{3,1,2,0:T(4,128)(2,1)} %slice.26, bf16[1024,4,1024]{2,0,1:T(8,128)(2,1)} %all-gather.7.cloned.1.call-done), kind=kOutput, calls=%fused_computation.4 | convolution fusion | flops 8589934592 | bytes 33554432 | tf_op jit(solution)/shard_map/fkd,nkjd->fkjn/dot_general | solution.py:66
  282.3 92.4 %all-gather.9.cloned.1.call-done = bf16[1024,4,1024]{2,0,1:T(8,128)(2,1)} async-done(((bf16[128,4,1024]{2,0,1:T(8,128)(2,1)}), bf16[1024,4,1024]{2,0,1:T(8,128)(2,1)}) %all-gather.9.cloned.1.call-update) | async-done | bytes 8388624 | tf_op jit(solution)/shard_map/all_gather | solution.py:64
  374.7 17.9 %fusion.18 = (bf16[1024,4,1,512]{3,0,1,2:T(8,128)(2,1)}, bf16[1024,4,1,512]{3,0,1,2:T(8,128)(2,1)}, bf16[1024,4,512]{2,0,1:T(8,128)(2,1)}) fusion(f32[1024,4,2,512]{3,0,2,1:T(8,128)} %convolution_bitcast_fusion.1, bf16[1024,4,1024]{2,0,1:T(8,128)(2,1)} %all-gather.9.cloned.1.call-done, bf16[512,4,1,1024]{3,1,2,0:T(4,128)(2,1)} %slice.29), kind=kOutput, calls=%fused_computation.42 | convolution fusion | flops 4328521728 | bytes 41943040 | tf_op jit(solution)/shard_map/fkd,nkd->fkn/dot_general | solution.py:73
  392.7 27.5 %fusion.13 = bf16[1024,4,1024]{2,0,1:T(8,128)(2,1)} fusion(bf16[512,4,2,1024]{3,1,2,0:T(4,128)(2,1)} %slice.26, bf16[1024,4,1,512]{3,0,1,2:T(8,128)(2,1)} %get-tuple-element.40, bf16[1024,4,1,512]{3,0,1,2:T(8,128)(2,1)} %get-tuple-element.39), kind=kOutput, calls=%fused_computation.30 | convolution fusion | flops 8598323200 | bytes 25165824 | tf_op jit(solution)/shard_map/fkjn,nkjd->fkd/dot_general | solution.py:79
  420.6 11.4 %convert_bitcast_fusion = bf16[1024,4,1024]{2,0,1:T(8,128)(2,1)} fusion(bf16[1024,4,512]{2,0,1:T(8,128)(2,1)} %get-tuple-element.41, bf16[512,4,1,1024]{3,1,2,0:T(4,128)(2,1)} %slice.29), kind=kOutput, calls=%fused_computation.24 | convolution fusion | flops 4299161600 | bytes 16777216 | tf_op jit(solution)/shard_map/fkn,nkd->fkd/dot_general | solution.py:85
  432.1 135.9 %reduce-scatter.11.cloned.1.call-done = bf16[128,4,1024]{2,0,1:T(8,128)(2,1)} async-done(((bf16[1024,4,1024]{2,0,1:T(8,128)(2,1)}), bf16[128,4,1024]{2,0,1:T(8,128)(2,1)}) %reduce-scatter.11.cloned.1.call-update) | async-done | bytes 1048592 | tf_op jit(solution)/shard_map/reduce_scatter | solution.py:82
  570.6 149.7 %reduce-scatter.9.cloned.1.call-done = bf16[128,4,1024]{2,0,1:T(8,128)(2,1)} async-done(((bf16[1024,4,1024]{2,0,1:T(8,128)(2,1)}), bf16[128,4,1024]{2,0,1:T(8,128)(2,1)}) %reduce-scatter.9.cloned.1.call-update) | async-done | bytes 1048592 | tf_op jit(solution)/shard_map/reduce_scatter | solution.py:88
  720.3 4.2 fusion.29
  732.0 3.5 all-to-all-start.4
  736.8 15.7 %all-to-all-done.4 = bf16[128,4,1024]{0,1,2:T(4,128)(2,1)S(1)} async-done(((bf16[128,4,1024]{0,1,2:T(4,128)(2,1)}), bf16[128,4,1024]{0,1,2:T(4,128)(2,1)S(1)}, u32[]{:S(2)}, u32[]{:S(2)}) %all-to-all-start.4) | async-done | bytes 1048608 | tf_op jit(solution)/shard_map/all_to_all | solution.py:115
  752.7 3.7 copy.133
  756.4 5.6 convert_bitcast_fusion.1
  769.8 3.2 copy.138
  774.3 3.2 copy.136
  782.7 8.2 bitcast_convert_fusion.2
  791.0 73.2 %reduce-scatter.17.cloned.1.call-done = bf16[32,1024]{1,0:T(8,128)(2,1)} async-done(((bf16[1024,1024]{1,0:T(8,128)(2,1)}), bf16[32,1024]{1,0:T(8,128)(2,1)}) %reduce-scatter.17.cloned.1.call-update) | async-done | bytes 65552 | tf_op jit(solution)/shard_map/reduce_scatter | solution.py:162
  864.3 9.2 fusion.5
  873.5 17.2 %convolution_bitcast_fusion = f32[512,4,2,1024]{0,3,2,1:T(8,128)} fusion(bf16[1024,4,1024]{2,0,1:T(8,128)(2,1)} %all-gather.7.cloned.1.call-done, bf16[1024,4,1,512]{3,0,1,2:T(8,128)(2,1)} %get-tuple-element.40, bf16[1024,4,1,512]{3,0,1,2:T(8,128)(2,1)} %get-tuple-element.39), kind=kOutput, calls=%fused_computation.3 | convolution fusion | flops 8594128896 | bytes 33554432 | tf_op jit(solution)/shard_map/fkjn,fkd->nkjd/dot_general | solution.py:93
  892.2 3.8 all-to-all-start.1
  896.0 12.5 %convolution_bitcast_fusion.2 = f32[512,4,1,1024]{0,3,2,1:T(8,128)} fusion(bf16[1024,4,1024]{2,0,1:T(8,128)(2,1)} %all-gather.9.cloned.1.call-done, bf16[1024,4,512]{2,0,1:T(8,128)(2,1)} %get-tuple-element.41), kind=kOutput, calls=%fused_computation.44 | convolution fusion | flops 4294967296 | bytes 20971520 | tf_op jit(solution)/shard_map/fkn,fkd->nkd/dot_general | solution.py:96
  910.4 3.5 all-to-all-start.3
  913.9 18.2 %pad_maximum_fusion = f32[512,4,3,1024]{0,3,2,1:T(8,128)} fusion(f32[512,4,1,1024]{0,3,2,1:T(8,128)} %convolution_bitcast_fusion.2, f32[512,4,2,1024]{0,3,2,1:T(8,128)} %convolution_bitcast_fusion), kind=kLoop, calls=%fused_computation.1 | loop fusion | flops 6291456 | bytes 50331648 | tf_op jit(solution)/shard_map/concatenate | solution.py:99
  932.2 30.0 %copy.149 = f32[512,4,3,1024]{3,1,2,0:T(4,128)} copy(f32[512,4,3,1024]{0,3,2,1:T(8,128)} %pad_maximum_fusion) | data formatting | bytes 50331648
  967.4 37.3 %psum.15 = f32[1024]{0:T(1024)} all-reduce(f32[1024]{0:T(1024)S(1)} %get-tuple-element.35), channel_id=1, replica_groups=mesh['frames'=8,'pos'=4] {'frames','pos'}, use_global_device_ids=true, to_apply=%region_12.13 | all-reduce | flops 1024 | bytes 8192 | tf_op jit(solution)/shard_map/psum | solution.py:166
  1004.7 7.8 psum.14
  1014.3 38.8 %all-gather.11.cloned.1.call-done = bf16[1024,1024]{1,0:T(8,128)(2,1)} async-done(((bf16[32,1024]{1,0:T(8,128)(2,1)}), bf16[1024,1024]{1,0:T(8,128)(2,1)}) %all-gather.11.cloned.1.call-update) | async-done | bytes 2097168 | tf_op jit(solution)/shard_map/all_gather | solution.py:165
  1053.0 4.1 convert_element_type.136
  1057.1 41.7 %reduce-scatter.13.cloned.1.call-done = bf16[128,16,256]{2,0,1:T(8,128)(2,1)} async-done(((bf16[128,16,1024]{2,0,1:T(8,128)(2,1)}), bf16[128,16,256]{2,0,1:T(8,128)(2,1)}) %reduce-scatter.13.cloned.1.call-update) | async-done | bytes 1048592 | tf_op jit(solution)/shard_map/reduce_scatter | solution.py:145
  (113 shorter events, 63.5 us)
Async XLA Ops:
  7.2 111.2 %copy-start = (bf16[1024,1024]{1,0:T(8,128)(2,1)S(1)}, bf16[1024,1024]{1,0:T(8,128)(2,1)}, u32[]{:S(2)}) copy-start(bf16[1024,1024]{1,0:T(8,128)(2,1)} %param.12) | copy-start | bytes 6291460
  7.2 44.0 %copy-start.22 = (f32[1024]{0:T(1024)S(1)}, f32[1024]{0:T(1024)}, u32[]{:S(2)}) copy-start(f32[1024]{0:T(1024)} %param.10) | copy-start | bytes 12292
  7.2 40.7 %all-gather.5.cloned.1.call-start = ((), (), s32[]{:S(2)}) async-start(), calls=%async_computation.11 | async-start | bytes 5242880 | tf_op jit(solution)/shard_map/all_gather | solution.py:23
  47.9 3.4 copy-start.5
  79.6 3.5 copy-start.20
  83.1 7.2 copy-start.12
  88.4 2.0 copy-start.7
  96.4 18.0 %all-to-all-start = ((bf16[128,16,256]{0,2,1:T(8,128)(2,1)}), bf16[128,16,256]{0,2,1:T(8,128)(2,1)S(1)}, u32[]{:S(2)}, u32[]{:S(2)}) async-start(bf16[128,16,256]{0,2,1:T(8,128)(2,1)} %bitcast.8), calls=%async_computation | async-start | bytes 2097152 | tf_op jit(solution)/shard_map/all_to_all | solution.py:53
  99.9 149.5 %all-gather.7.cloned.1.call-start = ((), (), s32[]{:S(2)}) async-start(), calls=%async_computation.12 | async-start | bytes 9437184 | tf_op jit(solution)/shard_map/all_gather | solution.py:65
  118.3 4.7 copy-start.21
  118.3 6.0 copy-start.15
  121.7 1.4 copy-start.4
  125.7 18.0 %all-to-all-start.2 = ((bf16[128,16,256]{2,0,1:T(8,128)(2,1)}), bf16[128,16,256]{2,0,1:T(8,128)(2,1)S(1)}, u32[]{:S(2)}, u32[]{:S(2)}) async-start(bf16[128,16,256]{2,0,1:T(8,128)(2,1)} %copy.125), calls=%async_computation.3 | async-start | bytes 2097152 | tf_op jit(solution)/shard_map/all_to_all | solution.py:62
  129.2 245.5 %all-gather.9.cloned.1.call-start = ((), (), s32[]{:S(2)}) async-start(), calls=%async_computation.14 | async-start | bytes 9437184 | tf_op jit(solution)/shard_map/all_gather | solution.py:64
  148.4 419.6 %reduce-scatter.11.cloned.1.call-start = ((), (), s32[]{:S(2)}) async-start(), calls=%async_computation.15 | async-start | bytes 9437184 | tf_op jit(solution)/shard_map/reduce_scatter | solution.py:82
  420.2 300.1 %reduce-scatter.9.cloned.1.call-start = ((), (), s32[]{:S(2)}) async-start(), calls=%async_computation.13 | async-start | bytes 9437184 | tf_op jit(solution)/shard_map/reduce_scatter | solution.py:88
  432.1 432.1 %reduce-scatter.17.cloned.1.call-start = ((), (), s32[]{:S(2)}) async-start(), calls=%async_computation.18 | async-start | bytes 2162688 | tf_op jit(solution)/shard_map/reduce_scatter | solution.py:162
  720.3 5.2 copy-start.16
  724.5 1.0 copy-start.9
  732.0 20.4 %all-to-all-start.4 = ((bf16[128,4,1024]{0,1,2:T(4,128)(2,1)}), bf16[128,4,1024]{0,1,2:T(4,128)(2,1)S(1)}, u32[]{:S(2)}, u32[]{:S(2)}) async-start(bf16[128,4,1024]{0,1,2:T(4,128)(2,1)} %copy.130), calls=%async_computation.6 | async-start | bytes 2097152 | tf_op jit(solution)/shard_map/all_to_all | solution.py:115
  735.6 226.6 %reduce-scatter.19.cloned.1.call-start = ((), (), s32[]{:S(2)}) async-start(), calls=%async_computation.20 | async-start | bytes 294912
  736.5 276.0 %reduce-scatter.15.cloned.1.call-start = ((), (), s32[]{:S(2)}) async-start(), calls=%async_computation.17 | async-start | bytes 1769472 | tf_op jit(solution)/shard_map/reduce_scatter | solution.py:155
  756.4 5.6 copy-start.8
  756.4 5.6 copy-start.13
  756.4 5.6 copy-start.14
  763.6 1.6 copy-start.3
  765.2 2.5 copy-start.2
  773.0 5.8 copy-start.6
  782.7 81.6 %copy-start.17 = (bf16[128,16,1,256]{3,0,2,1:T(8,128)(2,1)S(1)}, bf16[128,16,1,256]{3,0,2,1:T(8,128)(2,1)}, u32[]{:S(2)}) copy-start(bf16[128,16,1,256]{3,0,2,1:T(8,128)(2,1)} %copy.141) | copy-start | bytes 3145732
  782.7 81.6 %copy-start.18 = (bf16[128,16,1,256]{3,0,2,1:T(8,128)(2,1)S(1)}, bf16[128,16,1,256]{3,0,2,1:T(8,128)(2,1)}, u32[]{:S(2)}) copy-start(bf16[128,16,1,256]{3,0,2,1:T(8,128)(2,1)} %copy.140) | copy-start | bytes 3145732
  782.7 81.6 %copy-start.19 = (bf16[128,16,1,256]{3,0,2,1:T(8,128)(2,1)S(1)}, bf16[128,16,1,256]{3,0,2,1:T(8,128)(2,1)}, u32[]{:S(2)}) copy-start(bf16[128,16,1,256]{3,0,2,1:T(8,128)(2,1)} %copy.139) | copy-start | bytes 3145732
  791.0 262.1 %all-gather.11.cloned.1.call-start = ((), (), s32[]{:S(2)}) async-start(), calls=%async_computation.19 | async-start | bytes 2162688 | tf_op jit(solution)/shard_map/all_gather | solution.py:165
  864.2 234.6 %reduce-scatter.13.cloned.1.call-start = ((), (), s32[]{:S(2)}) async-start(), calls=%async_computation.16 | async-start | bytes 5242880 | tf_op jit(solution)/shard_map/reduce_scatter | solution.py:145
  873.5 17.2 %copy-start.11 = (bf16[128,4,1024]{2,0,1:T(8,128)(2,1)S(1)}, bf16[128,4,1024]{2,0,1:T(8,128)(2,1)}, u32[]{:S(2)}) copy-start(bf16[128,4,1024]{2,0,1:T(8,128)(2,1)} %get-tuple-element.48) | copy-start | bytes 3145732
  892.2 18.2 %all-to-all-start.1 = ((bf16[128,4,1024]{0,1,2:T(4,128)(2,1)}), bf16[128,4,1024]{0,1,2:T(4,128)(2,1)S(1)}, u32[]{:S(2)}, u32[]{:S(2)}) async-start(bf16[128,4,1024]{0,1,2:T(4,128)(2,1)} %copy.123), calls=%async_computation.2 | async-start | bytes 2097152 | tf_op jit(solution)/shard_map/all_to_all | solution.py:92
  896.0 12.5 %copy-start.10 = (bf16[128,4,1024]{2,0,1:T(8,128)(2,1)S(1)}, bf16[128,4,1024]{2,0,1:T(8,128)(2,1)}, u32[]{:S(2)}) copy-start(bf16[128,4,1024]{2,0,1:T(8,128)(2,1)} %copy-done.9) | copy-start | bytes 3145732
  910.4 55.4 %all-to-all-start.3 = ((bf16[128,4,1024]{0,1,2:T(4,128)(2,1)}), bf16[128,4,1024]{0,1,2:T(4,128)(2,1)S(1)}, u32[]{:S(2)}, u32[]{:S(2)}) async-start(bf16[128,4,1024]{0,1,2:T(4,128)(2,1)} %copy.128), calls=%async_computation.5 | async-start | bytes 2097152 | tf_op jit(solution)/shard_map/all_to_all | solution.py:114
  1098.8 4.6 copy-start.1
Sparse Core Ops, SparseCore 0:
  10.2 37.7 all-gather.4
  124.5 124.8 all-gather.6
  251.6 123.0 all-gather.8
  420.3 147.6 reduce-scatter.10
  571.9 148.3 reduce-scatter.8
  728.2 135.9 reduce-scatter.16
  868.4 57.1 reduce-scatter.18
  930.0 64.6 reduce-scatter.14
  997.6 55.4 all-gather.10
  1055.4 43.3 reduce-scatter.12

commit v2 on v1

v2 whole, which is shorter than its diff:
```python
import functools

import jax
import jax.numpy as jnp
from jax import lax
from jax.experimental import pallas as pl
from jax.experimental.pallas import tpu as pltpu
from jax.sharding import PartitionSpec as P

HEAD_DIM = 64
EPS = 1e-05
MASKED = -1e30
GROUP = 16
STEP = 32
EXTRA = 16
COST = 0.5
VMEM_LIMIT = 56 * 1024 * 1024

f32 = jnp.float32
bf16 = jnp.bfloat16


def dot(a, b, ca, cb):
    return lax.dot_general(a, b, (((ca,), (cb,)), ((), ())), preferred_element_type=f32)


def cost(us):
    us = us * COST
    return pl.CostEstimate(flops=int(us * 1.15e9), bytes_accessed=int(us * 1e6), transcendentals=0)


def params():
    return pltpu.CompilerParams(vmem_limit_bytes=VMEM_LIMIT)


def to_owners(me, rows, depth, local):
    r = lax.broadcasted_iota(jnp.int32, (rows, rows), 0)
    c = lax.broadcasted_iota(jnp.int32, (rows, rows), 1)
    frames = rows // depth
    k = r // frames
    source = (r % frames) * depth + ((k // local) ^ me) * local + k % local
    return jnp.where(c == source, 1.0, 0.0).astype(bf16)


def from_owners(me, rows, depth, local):
    r = lax.broadcasted_iota(jnp.int32, (rows, rows), 0)
    c = lax.broadcasted_iota(jnp.int32, (rows, rows), 1)
    frames = rows // depth
    k = r % depth
    source = (((k // local) ^ me) * local + k % local) * frames + r // depth
    return jnp.where(c == source, 1.0, 0.0).astype(bf16)


def pick(blocks, index):
    out = blocks[0]
    for b in range(1, len(blocks)):
        out = jnp.where(index == b, blocks[b], out)
    return out


def row_to_column(row):
    n = row.shape[1]
    r = lax.broadcasted_iota(jnp.int32, (n, n), 0)
    c = lax.broadcasted_iota(jnp.int32, (n, n), 1)
    return jnp.sum(jnp.where(r == c, row, 0.0), axis=1, keepdims=True)


def column_to_row(column):
    n = column.shape[0]
    r = lax.broadcasted_iota(jnp.int32, (n, n), 0)
    c = lax.broadcasted_iota(jnp.int32, (n, n), 1)
    return jnp.sum(jnp.where(r == c, column, 0.0), axis=0, keepdims=True)


def pair_mask(live_row, half, depth):
    n = live_row.shape[1] // 2
    live = row_to_column(live_row[:, half * n : (half + 1) * n])
    r = lax.broadcasted_iota(jnp.int32, (n, n), 0)
    c = lax.broadcasted_iota(jnp.int32, (n, n), 1)
    allowed = ((r // depth) == (c // depth)) & (r <= c) & (live > 0.5)
    return jnp.concatenate([allowed, allowed], 1)


def split_heads(block):
    lane = lax.broadcasted_iota(jnp.int32, block.shape, 1)
    zero = jnp.zeros_like(block)
    return jnp.concatenate(
        [jnp.where(lane < HEAD_DIM, block, zero), jnp.where(lane >= HEAD_DIM, block, zero)], 0
    )


def join_heads(pair):
    n = pair.shape[0] // 2
    lane = lax.broadcasted_iota(jnp.int32, (n, pair.shape[1]), 1)
    return jnp.where(lane < HEAD_DIM, pair[:n], pair[n:])


def pair_probs(q2, k2, allowed):
    scores = jnp.where(allowed, dot(k2, q2, 1, 1), MASKED)
    e = jnp.exp(scores - jnp.max(scores, axis=0, keepdims=True))
    return e * (1.0 / jnp.sum(e, axis=0, keepdims=True))


def per_step(frames, step):
    return min(step, frames)


def place(back, pieces, f):
    local, _, part = pieces[0].shape
    blocks = [p[:, f].reshape(local * GROUP, part) for p in pieces]
    return dot(back, jnp.concatenate(blocks, 0), 1, 0)


def row_scale(pieces):
    total = None
    for x in pieces:
        xf = x.astype(f32)
        term = jnp.sum(xf * xf, axis=-1, keepdims=True)
        total = term if total is None else total + term
    return lax.rsqrt(total / (pieces[0].shape[1] * len(pieces)) + EPS)


def cot_kernel(count, idx_ref, cot_ref, live_ref, *outs):
    step, depth, part = cot_ref.shape
    rows = GROUP * depth
    local = depth // count
    move = to_owners(idx_ref[0], rows, depth, local)
    for g in range(step // GROUP):
        f = slice(g * GROUP, (g + 1) * GROUP)
        live = row_to_column(live_ref[g])
        masked = (cot_ref[f].reshape(rows, part).astype(f32) * live).astype(bf16)
        moved = dot(move, masked, 1, 0).astype(bf16).reshape(count, local, GROUP, part)
        for j in range(count):
            outs[j][:, f] = moved[j]


def split_cot(idx, cot, live, count):
    frames, depth, part = cot.shape
    local = depth // count
    step = per_step(frames, 64)
    return pl.pallas_call(
        functools.partial(cot_kernel, count),
        grid_spec=pltpu.PrefetchScalarGridSpec(
            num_scalar_prefetch=1,
            grid=(frames // step,),
            in_specs=[
                pl.BlockSpec((step, depth, part), lambda i, s: (i, 0, 0)),
                pl.BlockSpec((step // GROUP, 1, GROUP * depth), lambda i, s: (i, 0, 0)),
            ],
            out_specs=[pl.BlockSpec((local, step, part), lambda i, s: (0, i, 0))] * count,
        ),
        out_shape=[jax.ShapeDtypeStruct((local, frames, part), bf16)] * count,
        compiler_params=params(),
        cost_estimate=cost(4),
    )(idx, cot, live)


def attn_kernel(count, idx_ref, *refs):
    xs = refs[:count]
    w_ref, gain_ref, live_ref = refs[count : count + 3]
    qkv_ref, resid_ref = refs[count + 3 : count + 5]
    outs = refs[count + 5 :]
    me = idx_ref[0]
    step, depth, part = xs[0].shape
    rows = GROUP * depth
    local = depth // count
    half_rows = rows // 2
    move = to_owners(me, rows, depth, local)
    own = move[: local * GROUP]
    for g in range(step // GROUP):
        f = slice(g * GROUP, (g + 1) * GROUP)
        r = slice(g * rows, (g + 1) * rows)
        pieces = [x[f].reshape(rows, part) for x in xs]
        rms = row_scale(pieces)
        acc = [None] * 3
        for j in range(count):
            normed = (pieces[j].astype(f32) * rms * gain_ref[me ^ j]).astype(bf16)
            for c in range(3):
                term = dot(normed, w_ref[c, me ^ j], 1, 0)
                acc[c] = term if acc[c] is None else acc[c] + term
            moved = dot(own, pieces[j], 1, 0).astype(bf16)
            resid_ref[me ^ j, :, f] = moved.reshape(local, GROUP, part)
        q, k, v = [a.astype(bf16) for a in acc]
        qkv_ref[0, r], qkv_ref[1, r], qkv_ref[2, r] = q, k, v
        q = q * (HEAD_DIM**-0.5)
        mixed = []
        for half in range(2):
            allowed = pair_mask(live_ref[g], half, depth)
            sl = slice(half * half_rows, (half + 1) * half_rows)
            cols = []
            for pair in range(part // 128):
                ln = slice(pair * 128, (pair + 1) * 128)
                probs = pair_probs(split_heads(q[sl, ln]), k[sl, ln], allowed).astype(bf16)
                cols.append(join_heads(dot(probs, v[sl, ln], 0, 0)).astype(bf16))
            mixed.append(jnp.concatenate(cols, 1) if len(cols) > 1 else cols[0])
        mixed = jnp.concatenate(mixed, 0)
        moved = dot(move, mixed, 1, 0).astype(bf16).reshape(count, local, GROUP, part)
        for j in range(count):
            outs[j][:, f] = moved[j]


def attention(idx, xs, w, gain, live, chunk, chunks):
    count = len(xs)
    frames, depth, part = xs[0].shape
    local = depth // count
    frames = frames // chunks
    step = per_step(frames, STEP)
    n = frames // step
    base = chunk * n
    rows = step * depth
    return pl.pallas_call(
        functools.partial(attn_kernel, count),
        grid_spec=pltpu.PrefetchScalarGridSpec(
            num_scalar_prefetch=1,
            grid=(n,),
            in_specs=[pl.BlockSpec((step, depth, part), lambda i, s: (i + base, 0, 0))] * count
            + [
                pl.BlockSpec(w.shape, lambda i, s: (0, 0, 0, 0)),
                pl.BlockSpec(gain.shape, lambda i, s: (0, 0, 0)),
                pl.BlockSpec((step // GROUP, 1, GROUP * depth), lambda i, s: (i + base, 0, 0)),
            ],
            out_specs=[
                pl.BlockSpec((3, rows, part), lambda i, s: (0, i, 0)),
                pl.BlockSpec((count, local, step, part), lambda i, s: (0, 0, i, 0)),
            ]
            + [pl.BlockSpec((local, step, part), lambda i, s: (0, i, 0))] * count,
        ),
        out_shape=[
            jax.ShapeDtypeStruct((3, frames * depth, part), bf16),
            jax.ShapeDtypeStruct((count, local, frames, part), bf16),
        ]
        + [jax.ShapeDtypeStruct((local, frames, part), bf16)] * count,
        compiler_params=params(),
        cost_estimate=cost(8),
    )(idx, *xs, w, gain, live)


def half_specs(local, frames, width):
    half = local // 2
    return [
        pl.BlockSpec((1, frames, width), lambda k, *s: (jnp.minimum(k, half - 1), 0, 0)),
        pl.BlockSpec((1, frames, width), lambda k, *s: (jnp.maximum(k - half, 0), 0, 0)),
    ]


def store_half(is_first, first_ref, second_ref, at, value):
    @pl.when(is_first)
    def _():
        first_ref[at] = value

    @pl.when(jnp.logical_not(is_first))
    def _():
        second_ref[at] = value


def load_half(is_first, first_ref, second_ref):
    return jnp.where(is_first, first_ref[0], second_ref[0])


def project_kernel(count, chunks, idx_ref, *refs):
    mixed = refs[: count * chunks]
    resids = refs[count * chunks : (count + 1) * chunks]
    w_ref, gain_ref, hidden_ref, first_ref, second_ref = refs[(count + 1) * chunks :]
    me = idx_ref[0]
    is_first = pl.program_id(0) < pl.num_programs(0) // 2
    size = mixed[0].shape[1]
    for c in range(chunks):
        f = slice(c * size, (c + 1) * size)
        hidden = jnp.concatenate([resids[c][b, 0] for b in range(count)], 1).astype(f32)
        for j in range(count):
            hidden = hidden + dot(mixed[c * count + j][0], w_ref[me ^ j], 1, 0)
        hidden_ref[0, f] = hidden
        rms = lax.rsqrt(jnp.mean(hidden * hidden, axis=-1, keepdims=True) + EPS)
        norm = (hidden * rms * gain_ref[0]).astype(bf16)
        store_half(is_first, first_ref, second_ref, (0, f), norm)


def project(idx, mixed, resids, w, gain):
    chunks, count = len(mixed), len(mixed[0])
    local, size, part = mixed[0][0].shape
    frames, width = size * chunks, part * count
    each = pl.BlockSpec((1, frames, width), lambda k, s: (k, 0, 0))
    return pl.pallas_call(
        functools.partial(project_kernel, count, chunks),
        grid_spec=pltpu.PrefetchScalarGridSpec(
            num_scalar_prefetch=1,
            grid=(local,),
            in_specs=[pl.BlockSpec((1, size, part), lambda k, s: (k, 0, 0))] * (count * chunks)
            + [pl.BlockSpec((count, 1, size, part), lambda k, s: (0, k, 0, 0))] * chunks
            + [
                pl.BlockSpec(w.shape, lambda k, s: (0, 0, 0)),
                pl.BlockSpec((1, 1, width), lambda k, s: (k, 0, 0)),
            ],
            out_specs=[each, *half_specs(local, frames, width)],
        ),
        out_shape=[
            jax.ShapeDtypeStruct((local, frames, width), f32),
            *[jax.ShapeDtypeStruct((local // 2, frames, width), bf16)] * 2,
        ],
        compiler_params=params(),
        cost_estimate=cost(6),
    )(idx, *[m for part_ in mixed for m in part_], *resids, w, gain)


def ffn_kernel(n, *refs):
    norms, grads, w_ref = refs[: 2 * n], refs[2 * n : 4 * n], refs[4 * n]
    dnorms, branches = refs[4 * n + 1 : 6 * n + 1], refs[6 * n + 1 : 8 * n + 1]
    act_ref = refs[-1]
    frames = norms[0].shape[1]
    is_first = pl.program_id(0) < pl.num_programs(0) // 2
    norm = jnp.concatenate([load_half(is_first, *norms[2 * i : 2 * i + 2]) for i in range(n)], 0)
    grad = jnp.concatenate([load_half(is_first, *grads[2 * i : 2 * i + 2]) for i in range(n)], 0)
    gate = dot(norm, w_ref[0, 0], 1, 1)
    up = dot(norm, w_ref[0, 1], 1, 1)
    dact = dot(grad, w_ref[0, 2], 1, 1)
    sig = jax.nn.sigmoid(gate)
    silu = gate * sig
    act = (silu * up).astype(bf16)
    dgate = (dact * up * sig * (1.0 + gate * (1.0 - sig))).astype(bf16)
    dup = (dact * silu).astype(bf16)
    act_ref[0, 0] = dgate
    act_ref[0, 1] = dup
    act_ref[0, 2] = act
    dnorm = (dot(dgate, w_ref[0, 0], 1, 0) + dot(dup, w_ref[0, 1], 1, 0)).astype(bf16)
    branch = dot(act, w_ref[0, 2], 1, 0).astype(bf16)
    for i in range(n):
        rows = slice(i * frames, (i + 1) * frames)
        store_half(is_first, *dnorms[2 * i : 2 * i + 2], 0, dnorm[rows])
        store_half(is_first, *branches[2 * i : 2 * i + 2], 0, branch[rows])


def ffn(norms, grads, w):
    n = len(norms)
    half, frames, width = norms[0][0].shape
    local, _, hidden, _ = w.shape
    specs = half_specs(local, frames, width)
    *out, act = pl.pallas_call(
        functools.partial(ffn_kernel, n),
        grid=(local,),
        in_specs=specs * (2 * n)
        + [pl.BlockSpec((1, 3, hidden, width), lambda k: (k, 0, 0, 0))],
        out_specs=specs * (2 * n)
        + [pl.BlockSpec((1, 3, n * frames, hidden), lambda k: (k, 0, 0, 0))],
        out_shape=[jax.ShapeDtypeStruct((half, frames, width), bf16)] * (4 * n)
        + [jax.ShapeDtypeStruct((local, 3, n * frames, hidden), bf16)],
        compiler_params=params(),
        cost_estimate=cost(3.5 + 5 * n),
    )(*[h for v in norms for h in v], *[h for v in grads for h in v], w)
    pairs = [out[i : i + 2] for i in range(0, 4 * n, 2)]
    return pairs[:n], pairs[n:], act


def weight_kernel(n, row, *refs):
    acts, others, out_ref = refs[:n], refs[n : -1], refs[-1]
    half, frames, _ = others[0].shape
    for k in range(acts[0].shape[0]):
        total, first = None, 0
        for a in acts:
            size = a.shape[2] // frames
            both = [others[2 * (first + i) + k // half][k % half] for i in range(size)]
            first += size
            both = jnp.concatenate(both, 0) if size > 1 else both[0]
            term = dot(a[k, 0], both, 0, 0)
            total = term if total is None else total + term
        out_ref[:, 0, k] = total


def weight_grad(acts, others, row, out):
    n = len(acts)
    half, frames, width = others[0][0].shape
    local, _, _, hidden = acts[0].shape
    chunk = min(128, hidden)
    whole = pl.BlockSpec(
        (half, frames, width), lambda c: (0, 0, 0), pipeline_mode=pl.Buffered(1)
    )
    others = [h for v in others for h in v]
    ins = list(acts) + others
    specs = [
        pl.BlockSpec((local, 1, a.shape[2], chunk), lambda c: (0, row, 0, c)) for a in acts
    ] + [whole] * len(others)
    aliases = {}
    kernel = functools.partial(weight_kernel, n, row)
    if out is not None:
        aliases = {len(ins): 0}
        ins.append(out)
        specs.append(pl.BlockSpec(memory_space=pl.ANY))
        kernel = lambda *refs: weight_kernel(n, row, *refs[:-2], refs[-1])
    return pl.pallas_call(
        kernel,
        grid=(hidden // chunk,),
        in_specs=specs,
        out_specs=pl.BlockSpec((chunk, 1, local, width), lambda c: (c, row, 0, 0)),
        out_shape=jax.ShapeDtypeStruct((hidden, 3, local, width), f32),
        input_output_aliases=aliases,
        compiler_params=params(),
        cost_estimate=cost(12),
    )(*ins)


def add_low(x, y):
    return (x.astype(f32) + y.astype(f32)).astype(bf16)


def merge(x, y, up, down):
    return add_low(x, up), add_low(y, down)


def sum_halves(refs):
    is_first = pl.program_id(0) < pl.num_programs(0) // 2
    total = None
    for i in range(0, len(refs), 2):
        term = load_half(is_first, *refs[i : i + 2]).astype(f32)
        total = term if total is None else total + term
    return total


def resid_kernel(count, idx_ref, *refs):
    hidden_ref, branch_ref, gain_ref, w_ref, low_ref, gsum_ref = refs[6:12]
    dms, dhs = refs[12 : 12 + count], refs[12 + count :]
    me = idx_ref[0]
    part = w_ref.shape[1]
    dnorm = sum_halves(refs[:6])
    hidden = hidden_ref[0]
    rms = lax.rsqrt(jnp.mean(hidden * hidden, axis=-1, keepdims=True) + EPS)
    xhat = hidden * rms
    gsum_ref[0] = jnp.sum(dnorm * xhat, axis=0, keepdims=True)
    u = dnorm * gain_ref[0]
    inner = jnp.mean(xhat * u, axis=-1, keepdims=True)
    low = (branch_ref[0].astype(f32) + rms * (u - xhat * inner)).astype(bf16)
    low_ref[0] = low
    blocks = [low[:, b * part : (b + 1) * part] for b in range(count)]
    for j in range(count):
        dhs[j][0] = pick(blocks, me ^ j)
        dms[j][0] = dot(low, w_ref[me ^ j], 1, 1).astype(bf16)


def resid_grad(idx, recv, own, hidden, branch, gain, w):
    count, part, width = w.shape
    local, frames, _ = hidden.shape
    each = pl.BlockSpec((1, frames, width), lambda k, s: (k, 0, 0))
    return pl.pallas_call(
        functools.partial(resid_kernel, count),
        grid_spec=pltpu.PrefetchScalarGridSpec(
            num_scalar_prefetch=1,
            grid=(local,),
            in_specs=half_specs(local, frames, width) * 3
            + [each] * 2
            + [
                pl.BlockSpec((1, 1, width), lambda k, s: (k, 0, 0)),
                pl.BlockSpec(w.shape, lambda k, s: (0, 0, 0)),
            ],
            out_specs=[each, pl.BlockSpec((1, 1, width), lambda k, s: (k, 0, 0))]
            + [pl.BlockSpec((1, frames, part), lambda k, s: (k, 0, 0))] * (2 * count),
        ),
        out_shape=[
            jax.ShapeDtypeStruct((local, frames, width), bf16),
            jax.ShapeDtypeStruct((local, 1, width), f32),
        ]
        + [jax.ShapeDtypeStruct((local, frames, part), bf16)] * (2 * count),
        compiler_params=params(),
        cost_estimate=cost(8),
    )(idx, *recv, *own, hidden, branch, gain, w)


def attn_back_kernel(count, idx_ref, *refs):
    xs = refs[:count]
    dms = refs[count : 2 * count]
    qkv_ref, w_ref, gain_ref, live_ref = refs[2 * count : 2 * count + 4]
    keep_ref, send_ref, wsum_ref, gsum_ref = refs[2 * count + 4 :]
    me = idx_ref[0]
    step, depth, part = xs[0].shape
    rows = GROUP * depth
    back = from_owners(me, rows, depth, depth // count)
    half_rows = rows // 2
    factor = HEAD_DIM**-0.5

    @pl.when(pl.program_id(0) == 0)
    def _():
        wsum_ref[...] = jnp.zeros_like(wsum_ref)
        gsum_ref[...] = jnp.zeros_like(gsum_ref)

    every, rmss = [[], [], []], []
    for g in range(step // GROUP):
        f = slice(g * GROUP, (g + 1) * GROUP)
        r = slice(g * rows, (g + 1) * rows)
        dmixed = place(back, dms, f).astype(bf16)
        q, k, v = qkv_ref[0, r] * factor, qkv_ref[1, r], qkv_ref[2, r]
        for half in range(2):
            allowed = pair_mask(live_ref[g], half, depth)
            sl = slice(half * half_rows, (half + 1) * half_rows)
            cols = [[], [], []]
            for pair in range(part // 128):
                ln = slice(pair * 128, (pair + 1) * 128)
                q2, k2, v2 = split_heads(q[sl, ln]), k[sl, ln], v[sl, ln]
                dm2 = split_heads(dmixed[sl, ln])
                probs = pair_probs(q2, k2, allowed)
                dprobs = dot(v2, dm2, 1, 1)
                inner = jnp.sum(probs * dprobs, axis=0, keepdims=True)
                ds = (probs * (dprobs - inner)).astype(bf16)
                cols[0].append((join_heads(dot(ds, k2, 0, 0)) * factor).astype(bf16))
                cols[1].append(dot(ds, q2, 1, 0).astype(bf16))
                cols[2].append(dot(probs.astype(bf16), dm2, 1, 0).astype(bf16))
            for c in range(3):
                every[c].append(jnp.concatenate(cols[c], 1) if len(cols[c]) > 1 else cols[c][0])
    dqkv = [jnp.concatenate(p, 0) for p in every]
    rows = step * depth
    pieces = [x[...].reshape(rows, part) for x in xs]
    rms = row_scale(pieces)
    inner = jnp.zeros((rows, 1), f32)
    for j in range(count):
        owner = me ^ j
        xhat = pieces[j].astype(f32) * rms
        scaled = xhat * gain_ref[owner]
        normed = scaled.astype(bf16)
        dn = jnp.zeros((rows, part), f32)
        for c in range(3):
            dn = dn + dot(dqkv[c], w_ref[c, owner], 1, 1)
            wsum_ref[c, owner] += dot(normed, dqkv[c], 0, 0)
        inner = inner + jnp.sum(scaled * dn, axis=-1, keepdims=True)
        gsum_ref[owner] += jnp.sum(dn * xhat, axis=0, keepdims=True)
        (send_ref if j & 1 else keep_ref)[j // 2, :rows] = dn.astype(bf16)
    size = GROUP * depth
    lines = [column_to_row(inner[g * size : (g + 1) * size]) for g in range(step // GROUP)]
    lines = [line[:, i : i + part] for line in lines for i in range(0, size, part)]
    lines.append(jnp.zeros((EXTRA - len(lines), part), f32))
    lines = jnp.concatenate(lines, 0).astype(bf16)
    for i in range(count // 2):
        send_ref[i, rows:] = lines
        keep_ref[i, rows:] = lines


def attention_back(idx, xs, dms, qkv, w, gain, live, chunk, chunks):
    count = len(xs)
    frames, depth, part = xs[0].shape
    local = dms[0].shape[0]
    frames = frames // chunks
    step = per_step(frames, STEP)
    n = frames // step
    base = chunk * n
    rows = step * depth
    lives = pl.BlockSpec((step // GROUP, 1, GROUP * depth), lambda i, s: (i + base, 0, 0))
    return pl.pallas_call(
        functools.partial(attn_back_kernel, count),
        grid_spec=pltpu.PrefetchScalarGridSpec(
            num_scalar_prefetch=1,
            grid=(n,),
            in_specs=[pl.BlockSpec((step, depth, part), lambda i, s: (i + base, 0, 0))] * count
            + [pl.BlockSpec((local, step, part), lambda i, s: (0, i + base, 0))] * count
            + [
                pl.BlockSpec((3, rows, part), lambda i, s: (0, i, 0)),
                pl.BlockSpec(w.shape, lambda i, s: (0, 0, 0, 0)),
                pl.BlockSpec(gain.shape, lambda i, s: (0, 0, 0)),
                lives,
            ],
            out_specs=[pl.BlockSpec((count // 2, rows + EXTRA, part), lambda i, s: (0, i, 0))] * 2
            + [
                pl.BlockSpec(w.shape, lambda i, s: (0, 0, 0, 0)),
                pl.BlockSpec((count, 1, part), lambda i, s: (0, 0, 0)),
            ],
        ),
        out_shape=[jax.ShapeDtypeStruct((count // 2, n * (rows + EXTRA), part), bf16)] * 2
        + [
            jax.ShapeDtypeStruct(w.shape, f32),
            jax.ShapeDtypeStruct((count, 1, part), f32),
        ],
        compiler_params=params(),
        cost_estimate=cost(14),
    )(idx, *xs, *dms, qkv, w, gain, live)


def input_kernel(count, terms_count, idx_ref, *refs):
    xs = refs[:count]
    dhs = refs[count : 2 * count]
    terms = refs[2 * count : 2 * count + terms_count]
    gain_ref, out_ref = refs[2 * count + terms_count :]
    me = idx_ref[0]
    step, depth, part = xs[0].shape
    rows = GROUP * depth
    back = from_owners(me, rows, depth, depth // count)
    sums = terms[0][0, step * depth :].astype(f32)
    for t in terms[1:]:
        sums = sums + t[0, step * depth :].astype(f32)
    lines = rows // part
    for g in range(step // GROUP):
        f = slice(g * GROUP, (g + 1) * GROUP)
        r = slice(g * rows, (g + 1) * rows)
        resid = place(back, dhs, f)
        pieces = [x[f].reshape(rows, part) for x in xs]
        rms = row_scale(pieces)
        xhat = pieces[0].astype(f32) * rms
        dn = terms[0][0, r].astype(f32)
        for t in terms[1:]:
            dn = dn + t[0, r].astype(f32)
        line = [sums[i : i + 1] for i in range(g * lines, (g + 1) * lines)]
        line = jnp.concatenate(line, 1) if lines > 1 else line[0]
        inner = row_to_column(line) / (part * count)
        out = resid + rms * (dn * gain_ref[me] - xhat * inner)
        out_ref[f] = out.astype(bf16).reshape(GROUP, depth, part)


def input_grad(idx, xs, dhs, terms, gain, chunk, chunks):
    count = len(xs)
    frames, depth, part = xs[0].shape
    local = dhs[0].shape[0]
    frames = frames // chunks
    step = per_step(frames, STEP)
    n = frames // step
    base = chunk * n
    rows = step * depth
    return pl.pallas_call(
        functools.partial(input_kernel, count, len(terms)),
        grid_spec=pltpu.PrefetchScalarGridSpec(
            num_scalar_prefetch=1,
            grid=(n,),
            in_specs=[pl.BlockSpec((step, depth, part), lambda i, s: (i + base, 0, 0))] * count
            + [pl.BlockSpec((local, step, part), lambda i, s: (0, i + base, 0))] * count
            + [pl.BlockSpec((1, rows + EXTRA, part), lambda i, s: (0, i, 0))] * len(terms)
            + [pl.BlockSpec(gain.shape, lambda i, s: (0, 0, 0))],
            out_specs=pl.BlockSpec((step, depth, part), lambda i, s: (i, 0, 0)),
        ),
        out_shape=jax.ShapeDtypeStruct((frames, depth, part), bf16),
        compiler_params=params(),
        cost_estimate=cost(4),
    )(idx, *xs, *dhs, *terms, gain)


def block_kernel(count, idx_ref, *refs):
    hidden_ref, live_ref, outs = refs[6], refs[7], refs[8:]
    me = idx_ref[0]
    part = outs[0].shape[2]
    branch = sum_halves(refs[:6])
    rows = ((hidden_ref[0] + branch) * row_to_column(live_ref[0])).astype(bf16)
    blocks = [rows[:, b * part : (b + 1) * part] for b in range(count)]
    for j in range(count):
        outs[j][0] = pick(blocks, me ^ j)


def block_rows(idx, recv, own, hidden, live, count):
    local, frames, width = hidden.shape
    part = width // count
    each = pl.BlockSpec((1, frames, width), lambda k, s: (k, 0, 0))
    return pl.pallas_call(
        functools.partial(block_kernel, count),
        grid_spec=pltpu.PrefetchScalarGridSpec(
            num_scalar_prefetch=1,
            grid=(local,),
            in_specs=half_specs(local, frames, width) * 3
            + [each, pl.BlockSpec((1, 1, frames), lambda k, s: (k, 0, 0))],
            out_specs=[pl.BlockSpec((1, frames, part), lambda k, s: (k, 0, 0))] * count,
        ),
        out_shape=[jax.ShapeDtypeStruct((local, frames, part), bf16)] * count,
        compiler_params=params(),
        cost_estimate=cost(4),
    )(idx, *recv, *own, hidden, live)


def gather_kernel(count, idx_ref, *refs):
    pieces, out_ref = refs[:count], refs[count]
    step, depth, part = out_ref.shape
    back = from_owners(idx_ref[0], GROUP * depth, depth, depth // count)
    for g in range(step // GROUP):
        f = slice(g * GROUP, (g + 1) * GROUP)
        out = place(back, pieces, f)
        out_ref[f] = out.astype(bf16).reshape(GROUP, depth, part)


def gather_block(idx, pieces):
    count = len(pieces)
    local, frames, part = pieces[0].shape
    depth = local * count
    step = per_step(frames, 64)
    return pl.pallas_call(
        functools.partial(gather_kernel, count),
        grid_spec=pltpu.PrefetchScalarGridSpec(
            num_scalar_prefetch=1,
            grid=(frames // step,),
            in_specs=[pl.BlockSpec((local, step, part), lambda i, s: (0, i, 0))] * count,
            out_specs=pl.BlockSpec((step, depth, part), lambda i, s: (i, 0, 0)),
        ),
        out_shape=jax.ShapeDtypeStruct((frames, depth, part), bf16),
        compiler_params=params(),
        cost_estimate=cost(4),
    )(idx, *pieces)


def swap(value, count, bits, axis="pos"):
    return lax.ppermute(value, axis, [(i, i ^ bits) for i in range(count)])


def exchange(pieces):
    count = len(pieces)
    return [pieces[0]] + [swap(pieces[j], count, j) for j in range(1, count)]


def gather_pos(value, count):
    pieces = {0: value}
    bit = count // 2
    while bit:
        for j in list(pieces):
            pieces[j ^ bit] = swap(pieces[j], count, bit)
        bit //= 2
    return [pieces[j] for j in range(count)]


def sum_axis(value, count, axis):
    bit = 1
    while bit < count:
        value = value + swap(value, count, bit, axis)
        bit *= 2
    return value


def after(value, *others):
    return lax.optimization_barrier((value, *others))[0]


def scatter_halves(blocks, bits, axis):
    count = blocks.shape[0]
    blocks = blocks.astype(f32)
    left = list(range(count))
    for bit in bits:
        keep = [i for i, j in enumerate(left) if not j & bit]
        send = [left.index(left[i] ^ bit) for i in keep]
        moved = swap(jnp.stack([blocks[i] for i in send]).astype(bf16), count, bit, axis)
        blocks = jnp.stack([blocks[i] for i in keep]) + moved.astype(f32)
        left = [left[i] for i in keep]
    return blocks[0]


def gather_doubles(value, count, bits, axis):
    blocks, have = value[None], [0]
    for bit in bits:
        blocks = jnp.concatenate([blocks, swap(blocks, count, bit, axis)], 0)
        have = have + [j ^ bit for j in have]
    inverse = jnp.array([have.index(j) for j in range(count)])
    order = jnp.take(inverse, lax.axis_index(axis) ^ jnp.arange(count), mode="clip")
    return jnp.take(blocks, order, axis=0, mode="clip")


def ring_steps(count):
    order = list(range(0, count, 2)) + list(range(count - 1, 0, -2))
    forward = [(order[i], order[(i + 1) % count]) for i in range(count)]
    return forward, [(b, a) for a, b in forward]


def ring_gather(value, steps, count, beside=None):
    forward, back = steps
    far = count // 2
    blocks = [[None, None] for _ in range(count)]
    blocks[0] = list(value)
    x_up, x_down = value
    y_up, y_down = value[1], value[0]
    tie = []
    for s in range(1, far + 1):
        if tie:
            x_up, x_down = after(x_up, *tie), after(x_down, *tie)
            y_up, y_down = after(y_up, *tie), after(y_down, *tie)
        tie = beside(s - 1, blocks) if beside else []
        x_up = blocks[s][0] = lax.ppermute(x_up, "frames", forward)
        x_down = blocks[count - s][1] = lax.ppermute(x_down, "frames", back)
        if s < far:
            y_up = blocks[s][1] = lax.ppermute(y_up, "frames", forward)
            y_down = blocks[count - s][0] = lax.ppermute(y_down, "frames", back)
    if beside:
        beside(far, blocks)
    return blocks


def ring_sum(blocks, steps, count, beside):
    forward, back = steps
    far = count // 2
    y_up = lax.ppermute(blocks[count - far + 1][1], "frames", forward)
    y_down = lax.ppermute(blocks[far - 1][0], "frames", back)
    x_up = lax.ppermute(blocks[far][0], "frames", forward)
    x_down = lax.ppermute(blocks[far][1], "frames", back)
    tie = beside(0, blocks[far])
    for h in range(far - 1, 0, -1):
        ready = []
        if h < far - 1:
            x, y = merge(after(blocks[count - h][1], *tie), blocks[h][0], y_up, y_down)
            y_up = lax.ppermute(x, "frames", forward)
            y_down = lax.ppermute(y, "frames", back)
            ready = [x, y]
        x, y = merge(after(blocks[count - h][0], *tie), blocks[h][1], x_up, x_down)
        x_up = lax.ppermute(x, "frames", forward)
        x_down = lax.ppermute(y, "frames", back)
        tie = beside(far - h, ready + [x, y])
    return [x_up, y_up, y_down, x_down], tie


CHUNKS = 2


def body(inputs, counts, gain_attn, weight_qkv, weight_out, gain_ffn, weight_ffn, cotangent):
    count = lax.axis_size("pos")
    ring = lax.axis_size("frames")
    me = lax.axis_index("pos")
    idx = me.astype(jnp.int32).reshape(1)
    frames, depth, part = inputs.shape
    width = part * count
    local = depth // count
    steps = ring_steps(ring)

    positions = jnp.arange(depth, dtype=jnp.int32)
    live = (positions[None, :] < counts[:, None]).astype(f32)
    live_rows = live.reshape(frames // GROUP, 1, GROUP * depth)
    live_own = lax.dynamic_slice_in_dim(live, me * local, local, 1).T.reshape(local, 1, frames)
    w_qkv = weight_qkv.transpose(1, 0, 2).reshape(3, count, part, part)
    w_out = weight_out.reshape(count, part, width)
    gain1 = gain_attn.reshape(count, 1, part)
    gain2 = gain_ffn.reshape(local, 1, width)

    cot_pieces = split_cot(idx, cotangent, live_rows, count)
    w_ffn = after(weight_ffn, cot_pieces[0]).transpose(1, 2, 0, 3)
    cot_pieces = exchange(cot_pieces)

    order = me ^ jnp.arange(count)
    branch = jnp.take(jnp.stack(cot_pieces), order, axis=0, mode="clip").transpose(1, 2, 0, 3)
    branch = branch.reshape(local, frames, width)
    half = local // 2
    xs = gather_pos(after(inputs, branch, w_ffn), count)

    parts = []

    def beside_grads(step, blocks):
        if 1 <= step <= CHUNKS:
            first = after(xs[0], *blocks[step], *blocks[ring - step])
            parts.append(
                attention(idx, [first] + xs[1:], w_qkv, gain1, live_rows, step - 1, CHUNKS)
            )
        return []

    grads = ring_gather([branch[:half], branch[half:]], steps, ring, beside_grads)
    qkvs = [p[0] for p in parts]
    resids = [p[1] for p in parts]
    mixeds = [exchange(p[2:]) for p in parts]
    hidden, *norm = project(idx, mixeds, resids, w_out, gain2)

    far = ring // 2
    groups = [[0]] + [[s, ring - s] for s in range(1, far)] + [[far]]
    dnorms, branches, acts = [None] * ring, [None] * ring, []

    def beside_norms(step, blocks):
        group = groups[step]
        norms = [list(blocks[d]) for d in group]
        if step:
            norms[0][0] = after(norms[0][0], acts[-1])
        down, forth, act = ffn(norms, [grads[d] for d in group], w_ffn)
        for i, d in enumerate(group):
            dnorms[d], branches[d] = down[i], forth[i]
        acts.append(act)
        return [act]

    norms = ring_gather(norm, steps, ring, beside_norms)

    totals, sets = [], [range(q, min(q + 6, far + 1)) for q in range(0, far + 1, 6)]

    def weights(row, ready):
        for i, chosen in enumerate(sets):
            if row == 0:
                totals.append(None)
            others = [(grads if row == 2 else norms)[d] for q in chosen for d in groups[q]]
            mine = [acts[q] for q in chosen]
            mine[0] = after(mine[0], *ready)
            totals[i] = weight_grad(mine, others, row, totals[i])
        return totals

    def beside_low(step, ready):
        return weights(step - 1, ready) if 1 <= step <= 3 else []

    recv, tie = ring_sum(dnorms, steps, ring, beside_low)
    for d in (far, far - 1, far + 1):
        branches[d] = [after(b, recv[1], recv[2]) for b in branches[d]]
    recv[0] = after(recv[0], *tie)
    low, gsum, *rest = resid_grad(idx, recv, dnorms[0], hidden, branch, gain2, w_out)
    dms = exchange(rest[:count])
    dhs = exchange([rest[count]] + [after(v, *dms) for v in rest[count + 1 :]])

    backs = []

    def beside_block(step, ready):
        if 1 <= step <= CHUNKS:
            c = step - 1
            first = after(dms[0], *ready)
            backs.append(
                attention_back(
                    idx, xs, [first] + dms[1:], qkvs[c], w_qkv, gain1, live_rows, c, CHUNKS
                )
            )
            return backs[-1][:1]
        return []

    recv, _ = ring_sum(branches, steps, ring, beside_block)
    rows = block_rows(idx, recv, branches[0], hidden, live_own, count)
    block_out = gather_block(idx, exchange(rows))

    grad_in, qkv_part, gain_part = [], 0.0, 0.0
    for c in range(CHUNKS):
        keep, send, qkv_c, gain_c = backs[c]
        qkv_part = qkv_part + qkv_c
        gain_part = gain_part + gain_c
        terms = [keep, swap(send, count, 1)]
        bit = 1
        while bit < count // 2:
            total = sum(t.astype(f32) for t in terms).astype(bf16)
            index = [i for i in range(total.shape[0]) if i & 1]
            going = jnp.stack([total[i] for i in index])
            stay = [i for i in range(total.shape[0]) if not i & 1]
            terms = [jnp.stack([t[i] for i in stay]) for t in terms]
            terms.append(swap(going, count, 2 * bit))
            bit *= 2
        grad_in.append(input_grad(idx, xs, dhs, terms, gain1, c, CHUNKS))
    grad_in = jnp.concatenate(grad_in, 0)

    ffn_grad = totals[0]
    for term in totals[1:]:
        ffn_grad = ffn_grad + term
    ffn_grad = ffn_grad.transpose(0, 2, 1, 3)

    mixed_all = [jnp.concatenate([m[j] for m in mixeds], 1) for j in range(count)]
    out_part = jnp.stack(
        [
            jnp.einsum("kfd,kfe->de", m, low, preferred_element_type=f32).astype(bf16)
            for m in mixed_all
        ]
    )
    out_part = after(out_part, *dms)
    bits = [1 << i for i in range((count - 1).bit_length())]
    ring_bits = [1 << i for i in range((ring - 1).bit_length())]
    out_low = scatter_halves(out_part, bits, "pos")
    ring_order = lax.axis_index("frames") ^ jnp.arange(ring)
    out_low = out_low.astype(bf16).reshape(ring, part // ring, width)
    out_low = jnp.take(out_low, ring_order, axis=0, mode="clip")
    out_low = scatter_halves(out_low, ring_bits, "frames")
    out_grad = gather_doubles(out_low.astype(bf16), ring, ring_bits, "frames")
    out_grad = gather_doubles(out_grad, count, bits[::-1], "pos")
    out_grad = out_grad.reshape(width, width).astype(f32)
    rows = width // ring
    qkv_rows = qkv_part.reshape(3, ring, rows, part).transpose(1, 0, 2, 3)
    packed = [
        qkv_rows.reshape(ring, 3 * rows, part),
        jnp.broadcast_to(gain_part.reshape(1, count, part), (ring, count, part)),
    ]
    columns = gsum.reshape(local, ring, rows).transpose(1, 0, 2).reshape(ring, local * rows)
    lines = -(-local * rows // part)
    columns = jnp.pad(columns, ((0, 0), (0, lines * part - local * rows)))
    packed.append(columns.reshape(ring, lines, part))
    packed = jnp.concatenate([p.astype(bf16) for p in packed], 1)
    moved = lax.all_to_all(packed, "frames", 0, 0, tiled=True)
    moved = jnp.sum(moved.astype(f32), axis=0)
    qkv_grad = moved[: 3 * rows].reshape(3, rows, part)
    gain_attn_grad = sum_axis(moved[3 * rows : 3 * rows + count], count, "pos").reshape(width)
    gain_ffn_grad = moved[3 * rows + count :].reshape(-1)[: local * rows].reshape(local, rows)
    return (
        block_out,
        grad_in,
        gain_attn_grad,
        qkv_grad.transpose(1, 0, 2),
        out_grad,
        gain_ffn_grad,
        ffn_grad,
    )


def solution(mesh):
    placed = (
        P("frames", None, "pos"),
        P("frames"),
        P(),
        P(None, None, "pos"),
        P(),
        P("pos", None),
        P("frames", "pos", None, None),
        P("frames", None, "pos"),
    )
    return jax.shard_map(
        body,
        mesh=mesh,
        in_specs=placed,
        out_specs=(
            P("frames", None, "pos"),
            P("frames", None, "pos"),
            P(),
            P("frames", None, "pos"),
            P(),
            P("pos", "frames"),
            P("frames", "pos", None, None),
        ),
        check_vma=False,
    )
```

time: 1120 us -> 603 us (0.54)
  the two profiles are of different devices: /device:TPU:0 before, /device:TPU:10 now
where the time goes in v2:
time: 603 us; the launch traced here: 593 us
  waiting for transfers between devices  203 us (34%)
  Pallas kernels  182 us (30%)
  starting transfers between devices  126 us (21%)
  local copies, waits for them, and re-layouts  42.6 us (7%)
  other arithmetic  33 us (5%)
    ppermute x37, waiting for transfers between devices, swap(): return lax.ppermute(value, axis, [(i, i ^ bits) for i in range(count)])  69.9 us
    pallas_call x5, Pallas kernels, ffn(): pl.pallas_call(functools.partial(ffn_kernel, n), grid=(local,), in_specs=...  62.3 us
    ppermute x37, starting transfers between devices, swap(): return lax.ppermute(value, axis, [(i, i ^ bits) for i in range(count)])  46.1 us
    ppermute x8, waiting for transfers between devices, ring_gather(): x_up = blocks[s][0] = lax.ppermute(x_up, 'frames', forward)  46.1 us
    pallas_call x3, Pallas kernels, weight_grad(): pl.pallas_call(kernel, grid=(hidden // chunk,), in_specs=specs, out_specs...  38.6 us
    pallas_call x2, Pallas kernels, attention_back(): pl.pallas_call(functools.partial(attn_back_kernel, count), grid_spec=pltp...  27.8 us
    pallas_call x2, Pallas kernels, attention(): pl.pallas_call(functools.partial(attn_kernel, count), grid_spec=pltpu.Pre...  20.2 us
    ppermute x6, waiting for transfers between devices, ring_gather(): y_up = blocks[s][1] = lax.ppermute(y_up, 'frames', forward)  19.5 us
  transfers between devices with their start and end apart: 94, of which 32 were waited for; matrix products, arithmetic and copies ran while one was open for 10% of the time, Pallas kernels for 27%

profile of v2, /device:TPU:10, one launch (start us, length us, event | category | flops | bytes accessed | tf_op | source)
XLA Modules:
  0.0 593.4 jit_solution(17632271380164359528)
XLA Ops:
  6.9 13.2 %copy.50 = bf16[512,4,3,1024]{3,0,2,1:T(8,128)(2,1)} copy(bf16[512,4,3,1024]{3,1,2,0:T(4,128)(2,1)} %param.16) | data formatting | bytes 25165824 | tf_op jit(solution)/shard_map/optimization_barrier | solution.py:714
  27.9 10.6 %collective-permute-done.3.refs_4_.refs_7_ = bf16[2,128,1024]{2,1,0:T(8,128)(2,1)S(1)} collective-permute-done((bf16[2,128,1024]{2,1,0:T(8,128)(2,1)S(1)}, bf16[2,128,1024]{2,1,0:T(8,128)(2,1)S(1)}, u32[]{:S(2)}, u32[]{:S(2)}) %collective-permute-start.3) | collective-permute-done | bytes 524320 | tf_op jit(solution)/shard_map/ppermute | solution.py:759
  39.0 10.8 %collective-permute-done.4.refs_5_.refs_8_ = bf16[2,128,1024]{2,1,0:T(8,128)(2,1)S(1)} collective-permute-done((bf16[2,128,1024]{2,1,0:T(8,128)(2,1)S(1)}, bf16[2,128,1024]{2,1,0:T(8,128)(2,1)S(1)}, u32[]{:S(2)}, u32[]{:S(2)}) %collective-permute-start.4) | collective-permute-done | bytes 524320 | tf_op jit(solution)/shard_map/ppermute | solution.py:762
  52.3 8.8 %collective-permute-done.13.refs_4_.refs_11_ = bf16[2,128,1024]{2,1,0:T(8,128)(2,1)} collective-permute-done((bf16[2,128,1024]{2,1,0:T(8,128)(2,1)S(1)}, bf16[2,128,1024]{2,1,0:T(8,128)(2,1)}, u32[]{:S(2)}, u32[]{:S(2)}) %collective-permute-start.13) | collective-permute-done | bytes 524320 | tf_op jit(solution)/shard_map/ppermute | solution.py:759
  62.7 8.7 %collective-permute-done.14.refs_5_.refs_12_ = bf16[2,128,1024]{2,1,0:T(8,128)(2,1)S(1)} collective-permute-done((bf16[2,128,1024]{2,1,0:T(8,128)(2,1)S(1)}, bf16[2,128,1024]{2,1,0:T(8,128)(2,1)S(1)}, u32[]{:S(2)}, u32[]{:S(2)}) %collective-permute-start.14) | collective-permute-done | bytes 524320 | tf_op jit(solution)/shard_map/ppermute | solution.py:762
  71.4 4.2 collective-permute-done.16.refs_7_.refs_14_
  77.4 10.1 %shard_map.155 = (bf16[3,1024,256]{2,1,0:T(8,128)(2,1)}, bf16[4,4,64,256]{3,2,1,0:T(8,128)(2,1)}, bf16[4,64,256]{2,1,0:T(8,128)(2,1)}, bf16[4,64,256]{2,1,0:T(8,...) custom-call(s32[1]{0:T(128)} %bitcast.idx_ref, bf16[128,16,256]{2,1,0:T(8,128)(2,1)} %refs_0_.5, ...), custom_call_target="tpu_custom_call" | custom-call | flops 4600000000 | bytes 4000000 | tf_op jit(solution)/shard_map/pallas_call | solution.py:211
  89.5 10.1 %shard_map.154 = (bf16[3,1024,256]{2,1,0:T(8,128)(2,1)}, bf16[4,4,64,256]{3,2,1,0:T(8,128)(2,1)}, bf16[4,64,256]{2,1,0:T(8,128)(2,1)}, bf16[4,64,256]{2,1,0:T(8,...) custom-call(s32[1]{0:T(128)} %bitcast.idx_ref, bf16[128,16,256]{2,1,0:T(8,128)(2,1)} %refs_0_.5, ...), custom_call_target="tpu_custom_call" | custom-call | flops 4600000000 | bytes 4000000 | tf_op jit(solution)/shard_map/pallas_call | solution.py:211
  102.2 4.4 collective-permute-done.11.refs_2_
  108.5 7.9 %shard_map.156 = (f32[4,128,1024]{2,1,0:T(8,128)}, bf16[2,128,1024]{2,1,0:T(8,128)(2,1)}, bf16[2,128,1024]{2,1,0:T(8,128)(2,1)}) custom-call(s32[1]{0:T(128)} %bitcast.idx_ref, bf16[4,64,256]{2,1,0:T(8,128)(2,1)} %get-tuple-element.131.refs_0_, bf16[4,64,256]{2,1,0:T(8,128)(2,1)} %copy-done.62, bf16[4,64,256]{2,1,0:T(8,128)(2,1)} %copy-done.63, ...), custom_call_target="tpu_custom_call" | custom-call | flops 3449999872 | bytes 3000000 | tf_op jit(solution)/shard_map/pallas_call | solution.py:283
  121.5 11.1 %shard_map.157 = (bf16[2,128,1024]{2,1,0:T(8,128)(2,1)}, bf16[2,128,1024]{2,1,0:T(8,128)(2,1)}, bf16[2,128,1024]{2,1,0:T(8,128)(2,1)}, bf16[2,128,1024]{2,1,0:T(8,128)(2,1)}, bf16[4,3,128,512]{3,2,1,0:T(8,128)(2,1)}) custom-call(bf16[2,128,1024]{2,1,0:T(8,128)(2,1)} %get-tuple-element.142.refs_0_.refs_5_, ...), custom_call_target="tpu_custom_call" | custom-call | flops 4887499776 | bytes 4250000 | tf_op jit(solution)/shard_map/pallas_call | solution.py:337
  134.2 8.4 %collective-permute-done.22.refs_2_.refs_9_ = bf16[2,128,1024]{2,1,0:T(8,128)(2,1)S(1)} collective-permute-done((bf16[2,128,1024]{2,1,0:T(8,128)(2,1)}, bf16[2,128,1024]{2,1,0:T(8,128)(2,1)S(1)}, u32[]{:S(2)}, u32[]{:S(2)}) %collective-permute-start.22) | collective-permute-done | bytes 524320 | tf_op jit(solution)/shard_map/ppermute | solution.py:763
  145.3 13.4 %shard_map.158 = (bf16[2,128,1024]{2,1,0:T(8,128)(2,1)}, bf16[2,128,1024]{2,1,0:T(8,128)(2,1)}, bf16[2,128,1024]{2,1,0:T(8,128)(2,1)}, bf16[2,128,1024]{2,1,0:T(...) custom-call(bf16[2,128,1024]{2,1,0:T(8,128)(2,1)} %copy-done.6, ...), custom_call_target="tpu_custom_call" | custom-call | flops 7762500096 | bytes 6750000 | tf_op jit(solution)/shard_map/pallas_call | solution.py:337
  160.3 17.2 %collective-permute-done.24.refs_0_.refs_11_ = bf16[2,128,1024]{2,1,0:T(8,128)(2,1)} collective-permute-done((bf16[2,128,1024]{2,1,0:T(8,128)(2,1)S(1)}, bf16[2,128,1024]{2,1,0:T(8,128)(2,1)}, u32[]{:S(2)}, u32[]{:S(2)}) %collective-permute-start.24) | collective-permute-done | bytes 524320 | tf_op jit(solution)/shard_map/ppermute | solution.py:759
  185.1 7.5 %collective-permute-done.28.refs_0_.refs_15_ = bf16[2,128,1024]{2,1,0:T(8,128)(2,1)S(1)} collective-permute-done((bf16[2,128,1024]{2,1,0:T(8,128)(2,1)}, bf16[2,128,1024]{2,1,0:T(8,128)(2,1)S(1)}, u32[]{:S(2)}, u32[]{:S(2)}) %collective-permute-start.28) | collective-permute-done | bytes 524320 | tf_op jit(solution)/shard_map/ppermute | solution.py:759
  193.0 13.4 %shard_map.159 = (bf16[2,128,1024]{2,1,0:T(8,128)(2,1)}, bf16[2,128,1024]{2,1,0:T(8,128)(2,1)}, bf16[2,128,1024]{2,1,0:T(8,128)(2,1)}, bf16[2,128,1024]{2,1,0:T(...) custom-call(bf16[2,128,1024]{2,1,0:T(8,128)(2,1)} %collective-permut, ...), custom_call_target="tpu_custom_call" | custom-call | flops 7762500096 | bytes 6750000 | tf_op jit(solution)/shard_map/pallas_call | solution.py:337
  210.2 7.2 %collective-permute-done.30.refs_2_.refs_17_ = bf16[2,128,1024]{2,1,0:T(8,128)(2,1)S(1)} collective-permute-done((bf16[2,128,1024]{2,1,0:T(8,128)(2,1)S(1)}, bf16[2,128,1024]{2,1,0:T(8,128)(2,1)S(1)}, u32[]{:S(2)}, u32[]{:S(2)}) %collective-permute-start.30) | collective-permute-done | bytes 524320 | tf_op jit(solution)/shard_map/ppermute | solution.py:763
  219.0 13.3 %shard_map.160 = (bf16[2,128,1024]{2,1,0:T(8,128)(2,1)}, bf16[2,128,1024]{2,1,0:T(8,128)(2,1)}, bf16[2,128,1024]{2,1,0:T(8,128)(2,1)}, bf16[2,128,1024]{2,1,0:T(...) custom-call(bf16[2,128,1024]{2,1,0:T(8,128)(2,1)} %copy-done.12, ...), custom_call_target="tpu_custom_call" | custom-call | flops 7762500096 | bytes 6750000 | tf_op jit(solution)/shard_map/pallas_call | solution.py:337
  236.0 3.8 collective-permute-done.37.refs_1_.refs_20_
  240.7 11.0 %shard_map.161 = (bf16[2,128,1024]{2,1,0:T(8,128)(2,1)}, bf16[2,128,1024]{2,1,0:T(8,128)(2,1)}, bf16[2,128,1024]{2,1,0:T(8,128)(2,1)}, bf16[2,128,1024]{2,1,0:T(8,128)(2,1)}, bf16[4,3,128,512]{3,2,1,0:T(8,128)(2,1)}) custom-call(bf16[2,128,1024]{2,1,0:T(8,128)(2,1)} %copy-done.16, bf16[2,128,1024]{2,1,0:T(8,128)(2,1)} %copy-done.15, ...), custom_call_target="tpu_custom_call" | custom-call | flops 4887499776 | bytes 4250000 | tf_op jit(solution)/shard_map/pallas_call | solution.py:337
  258.3 8.5 %collective-permute-done.41 = bf16[2,128,1024]{2,1,0:T(8,128)(2,1)S(1)} collective-permute-done((bf16[2,128,1024]{2,1,0:T(8,128)(2,1)}, bf16[2,128,1024]{2,1,0:T(8,128)(2,1)S(1)}, u32[]{:S(2)}, u32[]{:S(2)}) %collective-permute-start.41) | collective-permute-done | bytes 524320 | tf_op jit(solution)/shard_map/ppermute | solution.py:775
  268.8 9.0 %collective-permute-done.40 = bf16[2,128,1024]{2,1,0:T(8,128)(2,1)S(1)} collective-permute-done((bf16[2,128,1024]{2,1,0:T(8,128)(2,1)}, bf16[2,128,1024]{2,1,0:T(8,128)(2,1)S(1)}, u32[]{:S(2)}, u32[]{:S(2)}) %collective-permute-start.40) | collective-permute-done | bytes 524320 | tf_op jit(solution)/shard_map/ppermute | solution.py:774
  278.5 12.9 %shard_map.162.refs_21_ = f32[512,3,4,1024]{3,2,1,0:T(4,128)} custom-call(bf16[4,3,128,512]{3,2,1,0:T(8,128)(2,1)} %get-tuple-element.181.refs_0_, bf16[4,3,256,512]{3,2,1,0:T(8,128)(2,1)} %get-tuple-element.148.refs_1_, bf16[4,3,256,512]{3,2,1,0:T(8,128)(2,1)} %get-tuple-element.154.refs_2_, bf16[4,3,256,512]{3,2,1,0:T(8,128)(2,1)} %get-tuple-element.160.refs_3_, ...), custom_call_target="tpu_custom_call" | custom-call | flops 6899999744 | bytes 6000000 | tf_op jit(solution)/shard_map/pallas_call | solution.py:388
  296.5 12.8 %shard_map.163.refs_21_ = f32[512,3,4,1024]{3,2,1,0:T(4,128)} custom-call(bf16[4,3,128,512]{3,2,1,0:T(8,128)(2,1)} %get-tuple-element.181.refs_0_, bf16[4,3,256,512]{3,2,1,0:T(8,128)(2,1)} %get-tuple-element.148.refs_1_, bf16[4,3,256,512]{3,2,1,0:T(8,128)(2,1)} %get-tuple-element.154.refs_2_, ...), custom_call_target="tpu_custom_call", output_to_operand_aliasing={{}: (21, {})} | custom-call | flops 6899999744 | bytes 6000000 | tf_op jit(solution)/shard_map/pallas_call | solution.py:388
  310.2 5.4 collective-permute-done.46
  318.1 8.7 %collective-permute-done.51.refs_1_ = bf16[2,128,1024]{2,1,0:T(8,128)(2,1)S(1)} collective-permute-done((bf16[2,128,1024]{2,1,0:T(8,128)(2,1)S(1)}, bf16[2,128,1024]{2,1,0:T(8,128)(2,1)S(1)}, u32[]{:S(2)}, u32[]{:S(2)}) %collective-permute-start.51) | collective-permute-done | bytes 524320 | tf_op jit(solution)/shard_map/ppermute | solution.py:781
  330.3 12.8 %shard_map.164 = f32[512,3,4,1024]{3,2,1,0:T(4,128)} custom-call(bf16[4,3,128,512]{3,2,1,0:T(8,128)(2,1)} %get-tuple-element.181.refs_0_, bf16[4,3,256,512]{3,2,1,0:T(8,128)(2,1)} %get-tuple-element.148.refs_1_, bf16[4,3,256,512]{3,2,1,0:T(8,128)(2,1)} %get-tuple-element.154.refs_2_, ...), custom_call_target="tpu_custom_call", output_to_operand_aliasing={{}: (21, {})} | custom-call | flops 6899999744 | bytes 6000000 | tf_op jit(solution)/shard_map/pallas_call | solution.py:388
  344.5 8.2 %shard_map.165 = (bf16[4,128,1024]{2,1,0:T(8,128)(2,1)}, f32[4,1,1024]{2,1,0:T(1,128)}, bf16[4,128,256]{2,1,0:T(8,128)(2,1)}, bf16[4,128,256]{2,1,0:T(8,128)(2,1...) custom-call(s32[1]{0:T(128)} %bitcast.idx_ref, ...), custom_call_target="tpu_custom_call" | custom-call | flops 4600000000 | bytes 4000000 | tf_op jit(solution)/shard_map/pallas_call | solution.py:441
  367.5 4.4 collective-permute-done.58.refs_7_
  372.8 13.9 %shard_map.166 = (bf16[2,1056,256]{2,1,0:T(8,128)(2,1)}, bf16[2,1056,256]{2,1,0:T(8,128)(2,1)}, f32[3,4,256,256]{3,2,1,0:T(8,128)}, f32[4,1,256]{2,1,0:T(1,128)}) custom-call(s32[1]{0:T(128)} %bitcast.idx_ref, bf16[128,16,256]{2,1,0:T(8,128)(2,1)} %refs_0_.5, bf16[128,16,256]{2,1,0:T(8,128)(2,1)} %copy-done.76, bf16[128,16,256]{2,1,0:T(8,128)(2,1)} %copy-done.75, ...), custom_call_target="tpu_custom_call" | custom-call | flops 8049999872 | bytes 7000000 | tf_op jit(solution)/shard_map/pallas_call | solution.py:542
  394.7 13.9 %shard_map.167 = (bf16[2,1056,256]{2,1,0:T(8,128)(2,1)}, bf16[2,1056,256]{2,1,0:T(8,128)(2,1)}, f32[3,4,256,256]{3,2,1,0:T(8,128)}, f32[4,1,256]{2,1,0:T(1,128)}) custom-call(s32[1]{0:T(128)} %bitcast.idx_ref, bf16[128,16,256]{2,1,0:T(8,128)(2,1)} %refs_0_.5, bf16[128,16,256]{2,1,0:T(8,128)(2,1)} %copy-done.76, bf16[128,16,256]{2,1,0:T(8,128)(2,1)} %copy-done.75, ...), custom_call_target="tpu_custom_call" | custom-call | flops 8049999872 | bytes 7000000 | tf_op jit(solution)/shard_map/pallas_call | solution.py:542
  414.9 6.3 %all-to-all-start = ((bf16[8,390,256]{2,1,0:T(8,128)(2,1)}), bf16[8,390,256]{2,1,0:T(8,128)(2,1)S(1)}, u32[]{:S(2)}, u32[]{:S(2)}) async-start(bf16[8,390,256]{2,1,0:T(8,128)(2,1)} %pad_maximum_fusion.2), calls=%async_computation | async-start | bytes 3211264 | tf_op jit(solution)/shard_map/all_to_all | solution.py:949
  431.7 9.7 %collective-permute-done.85 = bf16[4,32,1024]{2,1,0:T(8,128)(2,1)S(1)} collective-permute-done((bf16[4,32,1024]{2,1,0:T(8,128)(2,1)S(1)}, bf16[4,32,1024]{2,1,0:T(8,128)(2,1)S(1)}, u32[]{:S(2)}, u32[]{:S(2)}) %collective-permute-start.85) | collective-permute-done | bytes 262176 | tf_op jit(solution)/shard_map/ppermute | solution.py:687
  441.5 14.1 %collective-permute-start.86 = (bf16[2,32,1024]{2,1,0:T(8,128)(2,1)S(1)}, bf16[2,32,1024]{2,1,0:T(8,128)(2,1)S(1)}, u32[]{:S(2)}, u32[]{:S(2)}) collective-permute-start(bf16[2,32,1024]{2,1,0:T(8,128)(2,1)S(1)} %pad_maximum_fusion.10), channel_id=1, source_target_pairs={{0,8},{4,12},{8,0},{12,4},{16,24},{20,28},{24,16},{28,20},{1,9},{5... | collective-permute-start | bytes 393224 | tf_op jit(solution)/shard_map/ppermute | solution.py:687
  455.6 5.0 collective-permute-done.86
  466.5 4.2 collective-permute-start.68
  472.1 3.0 collective-permute-done.88
  475.1 11.5 %collective-permute-start.66 = (bf16[2,128,1024]{2,1,0:T(8,128)(2,1)S(1)}, bf16[2,128,1024]{2,1,0:T(8,128)(2,1)S(1)}, u32[]{:S(2)}, u32[]{:S(2)}) collective-permute-start(bf16[2,128,1024]{2,1,0:T(8,128)(2,1)S(1)} %add_convert_fusion.5), channel_id=1, source_target_pairs={{0,8},{8,16},{16,24},{24,28},{28,20},{20,12},{12,4},{4,0},{1,9},{9... | collective-permute-start | bytes 1572872 | tf_op jit(solution)/shard_map/ppermute | solution.py:781
  488.0 10.6 %collective-permute-done.89 = bf16[2,32,1024]{2,1,0:T(8,128)(2,1)S(1)} collective-permute-done((bf16[2,32,1024]{2,1,0:T(8,128)(2,1)S(1)}, bf16[2,32,1024]{2,1,0:T(8,128)(2,1)S(1)}, u32[]{:S(2)}, u32[]{:S(2)}) %collective-permute-start.89) | collective-permute-done | bytes 131104 | tf_op jit(solution)/shard_map/ppermute | solution.py:687
  501.2 3.5 collective-permute-start.90
  509.6 9.2 %collective-permute-done.70.refs_3_ = bf16[2,128,1024]{2,1,0:T(8,128)(2,1)S(1)} collective-permute-done((bf16[2,128,1024]{2,1,0:T(8,128)(2,1)S(1)}, bf16[2,128,1024]{2,1,0:T(8,128)(2,1)S(1)}, u32[]{:S(2)}, u32[]{:S(2)}) %collective-permute-start.70) | collective-permute-done | bytes 524320 | tf_op jit(solution)/shard_map/ppermute | solution.py:786
  522.2 4.7 shard_map.168
  538.3 3.1 collective-permute-done.73.refs_3_
  544.4 8.8 %collective-permute-done.91 = bf16[1,8,32,1024]{3,2,1,0:T(8,128)(2,1)S(1)} collective-permute-done((bf16[1,8,32,1024]{3,2,1,0:T(8,128)(2,1)S(1)}, bf16[1,8,32,1024]{3,2,1,0:T(8,128)(2,1)S(1)}, u32[]{:S(2)}, u32[]{:S(2)}) %collective-permute-start.91) | collective-permute-done | bytes 524320 | tf_op jit(solution)/shard_map/ppermute | solution.py:687
  558.6 5.8 collective-permute-done.75.refs_6_
  565.2 3.5 shard_map.170
  569.0 6.8 %collective-permute-done.80.refs_10_ = bf16[1,1056,256]{2,1,0:T(8,128)(2,1)} collective-permute-done((bf16[1,1056,256]{2,1,0:T(8,128)(2,1)}, bf16[1,1056,256]{2,1,0:T(8,128)(2,1)}, u32[]{:S(2)}, u32[]{:S(2)}) %collective-permute-start.80) | collective-permute-done | bytes 540704 | tf_op jit(solution)/shard_map/ppermute | solution.py:687
  575.8 3.5 shard_map.171
  (446 shorter events, 171.8 us)
Async XLA Ops:
  22.1 27.7 %collective-permute-start.8 = (bf16[128,16,256]{2,1,0:T(8,128)(2,1)S(1)}, bf16[128,16,256]{2,1,0:T(8,128)(2,1)S(1)}, u32[]{:S(2)}, u32[]{:S(2)}) collective-permute-start(bf16[128,16,256]{2,1,0:T(8,128)(2,1)S(1)} %copy-done.74), channel_id=1, source_target_pairs={{0,2},{1,3},{2,0},{3,1},{4,6},{5,7},{6,4},{7,5},{8,10},{9,11},{10,... | collective-permute-start | bytes 3145736 | tf_op jit(solution)/shard_map/ppermute | solution.py:687
  24.3 25.5 %collective-permute-start.4 = (bf16[2,128,1024]{2,1,0:T(8,128)(2,1)S(1)}, bf16[2,128,1024]{2,1,0:T(8,128)(2,1)S(1)}, u32[]{:S(2)}, u32[]{:S(2)}) collective-permute-start(bf16[2,128,1024]{2,1,0:T(8,128)(2,1)S(1)} %bitcast.108), channel_id=1, source_target_pairs={{0,8},{8,16},{16,24},{24,28},{28,20},{20,12},{12,4},{4,0},{1,9},{9... | collective-permute-start | bytes 1572872 | tf_op jit(solution)/shard_map/ppermute | solution.py:762
  24.9 25.4 %collective-permute-start.5 = (bf16[2,128,1024]{2,1,0:T(8,128)(2,1)S(1)}, bf16[2,128,1024]{2,1,0:T(8,128)(2,1)S(1)}, u32[]{:S(2)}, u32[]{:S(2)}) collective-permute-start(bf16[2,128,1024]{2,1,0:T(8,128)(2,1)S(1)} %bitcast.105), channel_id=1, source_target_pairs={{8,0},{16,8},{24,16},{28,24},{20,28},{12,20},{4,12},{0,4},{9,1},{1... | collective-permute-start | bytes 1572872 | tf_op jit(solution)/shard_map/ppermute | solution.py:763
  26.4 24.4 %collective-permute-start.6 = (bf16[2,128,1024]{2,1,0:T(8,128)(2,1)S(1)}, bf16[2,128,1024]{2,1,0:T(8,128)(2,1)S(1)}, u32[]{:S(2)}, u32[]{:S(2)}) collective-permute-start(bf16[2,128,1024]{2,1,0:T(8,128)(2,1)S(1)} %bitcast.109), channel_id=1, source_target_pairs={{8,0},{16,8},{24,16},{28,24},{20,28},{12,20},{4,12},{0,4},{9,1},{1... | collective-permute-start | bytes 1572872 | tf_op jit(solution)/shard_map/ppermute | solution.py:760
  49.8 25.8 %collective-permute-start.7 = (bf16[128,16,256]{2,1,0:T(8,128)(2,1)S(1)}, bf16[128,16,256]{2,1,0:T(8,128)(2,1)S(1)}, u32[]{:S(2)}, u32[]{:S(2)}) collective-permute-start(bf16[128,16,256]{2,1,0:T(8,128)(2,1)S(1)} %copy-done.74), channel_id=1, source_target_pairs={{0,1},{1,0},{2,3},{3,2},{4,5},{5,4},{6,7},{7,6},{8,9},{9,8},{10,11... | collective-permute-start | bytes 3145736 | tf_op jit(solution)/shard_map/ppermute | solution.py:687
  49.8 25.9 %collective-permute-start.9 = (bf16[128,16,256]{2,1,0:T(8,128)(2,1)S(1)}, bf16[128,16,256]{2,1,0:T(8,128)(2,1)S(1)}, u32[]{:S(2)}, u32[]{:S(2)}) collective-permute-start(bf16[128,16,256]{2,1,0:T(8,128)(2,1)S(1)} %collective-permute-done.8.refs_2_), channel_id=1, source_target_pairs={{0,1},{1,0},{2,3},{3,2},{4,5},{5,4},{6,7},{7,6},{8,9},{9,8},{10,11... | collective-permute-start | bytes 3145736 | tf_op jit(solution)/shard_map/ppermute | solution.py:687
  118.5 24.1 %collective-permute-start.22 = (bf16[2,128,1024]{2,1,0:T(8,128)(2,1)}, bf16[2,128,1024]{2,1,0:T(8,128)(2,1)S(1)}, u32[]{:S(2)}, u32[]{:S(2)}) collective-permute-start(bf16[2,128,1024]{2,1,0:T(8,128)(2,1)} %get-tuple-element.142.refs_0_.refs_5_), channel_id=1, source_target_pairs={{8,0},{16,8},{24,16},{28,24},{20,28},{12,20},{4,12},{0,4},{9,1},{1... | collective-permute-start | bytes 1572872 | tf_op jit(solution)/shard_map/ppermute | solution.py:763
  120.1 24.2 %collective-permute-start.21 = (bf16[2,128,1024]{2,1,0:T(8,128)(2,1)}, bf16[2,128,1024]{2,1,0:T(8,128)(2,1)S(1)}, u32[]{:S(2)}, u32[]{:S(2)}) collective-permute-start(bf16[2,128,1024]{2,1,0:T(8,128)(2,1)} %get-tuple-element.143.refs_1_.refs_6_), channel_id=1, source_target_pairs={{0,8},{8,16},{16,24},{24,28},{28,20},{20,12},{12,4},{4,0},{1,9},{9... | collective-permute-start | bytes 1572872 | tf_op jit(solution)/shard_map/ppermute | solution.py:762
  120.5 61.3 %collective-permute-start.32 = (bf16[2,128,1024]{2,1,0:T(8,128)(2,1)}, bf16[2,128,1024]{2,1,0:T(8,128)(2,1)}, u32[]{:S(2)}, u32[]{:S(2)}) collective-permute-start(bf16[2,128,1024]{2,1,0:T(8,128)(2,1)} %collective-permute-done.13.refs_4_.refs_11_), channel_id=1, source_target_pairs={{0,8},{8,16},{16,24},{24,28},{28,20},{20,12},{12,4},{4,0},{1,9},{9... | collective-permute-start | bytes 1572872 | tf_op jit(solution)/shard_map/ppermute | solution.py:759
  132.7 26.0 %collective-permute-start.27 = (bf16[2,128,1024]{2,1,0:T(8,128)(2,1)S(1)}, bf16[2,128,1024]{2,1,0:T(8,128)(2,1)S(1)}, u32[]{:S(2)}, u32[]{:S(2)}) collective-permute-start(bf16[2,128,1024]{2,1,0:T(8,128)(2,1)S(1)} %collective-permute-done.23.refs_3_.refs_10_), channel_id=1, source_target_pairs={{8,0},{16,8},{24,16},{28,24},{20,28},{12,20},{4,12},{0,4},{9,1},{1... | collective-permute-start | bytes 1572872 | tf_op jit(solution)/shard_map/ppermute | solution.py:760
  142.6 37.2 %collective-permute-start.26 = (bf16[2,128,1024]{2,1,0:T(8,128)(2,1)S(1)}, bf16[2,128,1024]{2,1,0:T(8,128)(2,1)S(1)}, u32[]{:S(2)}, u32[]{:S(2)}) collective-permute-start(bf16[2,128,1024]{2,1,0:T(8,128)(2,1)S(1)} %collective-permute-done.22.refs_2_.refs_9_), channel_id=1, source_target_pairs={{8,0},{16,8},{24,16},{28,24},{20,28},{12,20},{4,12},{0,4},{9,1},{1... | collective-permute-start | bytes 1572872 | tf_op jit(solution)/shard_map/ppermute | solution.py:763
  144.3 37.2 %collective-permute-start.25 = (bf16[2,128,1024]{2,1,0:T(8,128)(2,1)S(1)}, bf16[2,128,1024]{2,1,0:T(8,128)(2,1)}, u32[]{:S(2)}, u32[]{:S(2)}) collective-permute-start(bf16[2,128,1024]{2,1,0:T(8,128)(2,1)S(1)} %collective-permute-done.21.refs_1_.refs_8_), channel_id=1, source_target_pairs={{0,8},{8,16},{16,24},{24,28},{28,20},{20,12},{12,4},{4,0},{1,9},{9... | collective-permute-start | bytes 1572872 | tf_op jit(solution)/shard_map/ppermute | solution.py:762
  144.7 32.8 %collective-permute-start.24 = (bf16[2,128,1024]{2,1,0:T(8,128)(2,1)S(1)}, bf16[2,128,1024]{2,1,0:T(8,128)(2,1)}, u32[]{:S(2)}, u32[]{:S(2)}) collective-permute-start(bf16[2,128,1024]{2,1,0:T(8,128)(2,1)S(1)} %collective-permute-done.20.refs_0_.refs_7_), channel_id=1, source_target_pairs={{0,8},{8,16},{16,24},{24,28},{28,20},{20,12},{12,4},{4,0},{1,9},{9... | collective-permute-start | bytes 1572872 | tf_op jit(solution)/shard_map/ppermute | solution.py:759
  158.7 24.7 %collective-permute-start.31 = (bf16[2,128,1024]{2,1,0:T(8,128)(2,1)S(1)}, bf16[2,128,1024]{2,1,0:T(8,128)(2,1)S(1)}, u32[]{:S(2)}, u32[]{:S(2)}) collective-permute-start(bf16[2,128,1024]{2,1,0:T(8,128)(2,1)S(1)} %collective-permute-done.27.refs_3_.refs_14_), channel_id=1, source_target_pairs={{8,0},{16,8},{24,16},{28,24},{20,28},{12,20},{4,12},{0,4},{9,1},{1... | collective-permute-start | bytes 1572872 | tf_op jit(solution)/shard_map/ppermute | solution.py:760
  179.9 26.6 %collective-permute-start.35 = (bf16[2,128,1024]{2,1,0:T(8,128)(2,1)}, bf16[2,128,1024]{2,1,0:T(8,128)(2,1)S(1)}, u32[]{:S(2)}, u32[]{:S(2)}) collective-permute-start(bf16[2,128,1024]{2,1,0:T(8,128)(2,1)} %copy-done.27), channel_id=1, source_target_pairs={{8,0},{16,8},{24,16},{28,24},{20,28},{12,20},{4,12},{0,4},{9,1},{1... | collective-permute-start | bytes 1572872 | tf_op jit(solution)/shard_map/ppermute | solution.py:760
  181.4 25.6 %collective-permute-start.33 = (bf16[2,128,1024]{2,1,0:T(8,128)(2,1)}, bf16[2,128,1024]{2,1,0:T(8,128)(2,1)S(1)}, u32[]{:S(2)}, u32[]{:S(2)}) collective-permute-start(bf16[2,128,1024]{2,1,0:T(8,128)(2,1)} %copy-done.25), channel_id=1, source_target_pairs={{0,8},{8,16},{16,24},{24,28},{28,20},{20,12},{12,4},{4,0},{1,9},{9... | collective-permute-start | bytes 1572872 | tf_op jit(solution)/shard_map/ppermute | solution.py:762
  181.9 26.6 %collective-permute-start.34 = (bf16[2,128,1024]{2,1,0:T(8,128)(2,1)}, bf16[2,128,1024]{2,1,0:T(8,128)(2,1)S(1)}, u32[]{:S(2)}, u32[]{:S(2)}) collective-permute-start(bf16[2,128,1024]{2,1,0:T(8,128)(2,1)} %copy-done.26), channel_id=1, source_target_pairs={{8,0},{16,8},{24,16},{28,24},{20,28},{12,20},{4,12},{0,4},{9,1},{1... | collective-permute-start | bytes 1572872 | tf_op jit(solution)/shard_map/ppermute | solution.py:763
  183.5 33.9 %collective-permute-start.30 = (bf16[2,128,1024]{2,1,0:T(8,128)(2,1)S(1)}, bf16[2,128,1024]{2,1,0:T(8,128)(2,1)S(1)}, u32[]{:S(2)}, u32[]{:S(2)}) collective-permute-start(bf16[2,128,1024]{2,1,0:T(8,128)(2,1)S(1)} %collective-permute-done.26.refs_2_.refs_13_), channel_id=1, source_target_pairs={{8,0},{16,8},{24,16},{28,24},{20,28},{12,20},{4,12},{0,4},{9,1},{1... | collective-permute-start | bytes 1572872 | tf_op jit(solution)/shard_map/ppermute | solution.py:763
  192.5 25.4 %collective-permute-start.29 = (bf16[2,128,1024]{2,1,0:T(8,128)(2,1)}, bf16[2,128,1024]{2,1,0:T(8,128)(2,1)S(1)}, u32[]{:S(2)}, u32[]{:S(2)}) collective-permute-start(bf16[2,128,1024]{2,1,0:T(8,128)(2,1)} %collective-permute-done.25.refs_1_.refs_12_), channel_id=1, source_target_pairs={{0,8},{8,16},{16,24},{24,28},{28,20},{20,12},{12,4},{4,0},{1,9},{9... | collective-permute-start | bytes 1572872 | tf_op jit(solution)/shard_map/ppermute | solution.py:762
  206.4 29.5 %collective-permute-start.38 = (bf16[2,128,1024]{2,1,0:T(8,128)(2,1)}, bf16[2,128,1024]{2,1,0:T(8,128)(2,1)S(1)}, u32[]{:S(2)}, u32[]{:S(2)}) collective-permute-start(bf16[2,128,1024]{2,1,0:T(8,128)(2,1)} %collective-permute-done.32.refs_4_.refs_15_), channel_id=1, source_target_pairs={{0,8},{8,16},{16,24},{24,28},{28,20},{20,12},{12,4},{4,0},{1,9},{9... | collective-permute-start | bytes 1572872 | tf_op jit(solution)/shard_map/ppermute | solution.py:759
  207.0 29.0 %collective-permute-start.39 = (bf16[2,128,1024]{2,1,0:T(8,128)(2,1)S(1)}, bf16[2,128,1024]{2,1,0:T(8,128)(2,1)S(1)}, u32[]{:S(2)}, u32[]{:S(2)}) collective-permute-start(bf16[2,128,1024]{2,1,0:T(8,128)(2,1)S(1)} %collective-permute-done.35.refs_7_.refs_18_), channel_id=1, source_target_pairs={{8,0},{16,8},{24,16},{28,24},{20,28},{12,20},{4,12},{0,4},{9,1},{1... | collective-permute-start | bytes 1572872 | tf_op jit(solution)/shard_map/ppermute | solution.py:760
  208.5 31.3 %collective-permute-start.37 = (bf16[2,128,1024]{2,1,0:T(8,128)(2,1)S(1)}, bf16[2,128,1024]{2,1,0:T(8,128)(2,1)S(1)}, u32[]{:S(2)}, u32[]{:S(2)}) collective-permute-start(bf16[2,128,1024]{2,1,0:T(8,128)(2,1)S(1)} %collective-permute-done.31.refs_3_.refs_18_), channel_id=1, source_target_pairs={{8,0},{16,8},{24,16},{28,24},{20,28},{12,20},{4,12},{0,4},{9,1},{1... | collective-permute-start | bytes 1572872 | tf_op jit(solution)/shard_map/ppermute | solution.py:760
  254.5 36.9 %collective-permute-start.42 = (bf16[2,128,1024]{2,1,0:T(8,128)(2,1)}, bf16[2,128,1024]{2,1,0:T(8,128)(2,1)S(1)}, u32[]{:S(2)}, u32[]{:S(2)}) collective-permute-start(bf16[2,128,1024]{2,1,0:T(8,128)(2,1)} %get-tuple-element.169), channel_id=1, source_target_pairs={{0,8},{8,16},{16,24},{24,28},{28,20},{20,12},{12,4},{4,0},{1,9},{9... | collective-permute-start | bytes 1572872 | tf_op jit(solution)/shard_map/ppermute | solution.py:772
  256.7 35.5 %collective-permute-start.49 = (bf16[2,128,1024]{2,1,0:T(8,128)(2,1)S(1)}, bf16[2,128,1024]{2,1,0:T(8,128)(2,1)S(1)}, u32[]{:S(2)}, u32[]{:S(2)}) collective-permute-start(bf16[2,128,1024]{2,1,0:T(8,128)(2,1)S(1)} %add_convert_fusion.19), channel_id=1, source_target_pairs={{8,0},{16,8},{24,16},{28,24},{20,28},{12,20},{4,12},{0,4},{9,1},{1... | collective-permute-start | bytes 1572872 | tf_op jit(solution)/shard_map/ppermute | solution.py:782
  267.0 27.0 %collective-permute-start.45 = (bf16[2,128,1024]{2,1,0:T(8,128)(2,1)S(1)}, bf16[2,128,1024]{2,1,0:T(8,128)(2,1)S(1)}, u32[]{:S(2)}, u32[]{:S(2)}) collective-permute-start(bf16[2,128,1024]{2,1,0:T(8,128)(2,1)S(1)} %add_convert_fusion.21), channel_id=1, source_target_pairs={{8,0},{16,8},{24,16},{28,24},{20,28},{12,20},{4,12},{0,4},{9,1},{1... | collective-permute-start | bytes 1572872 | tf_op jit(solution)/shard_map/ppermute | solution.py:786
  292.4 25.6 %collective-permute-start.52 = (bf16[2,128,1024]{2,1,0:T(8,128)(2,1)S(1)}, bf16[2,128,1024]{2,1,0:T(8,128)(2,1)S(1)}, u32[]{:S(2)}, u32[]{:S(2)}) collective-permute-start(bf16[2,128,1024]{2,1,0:T(8,128)(2,1)S(1)} %add_convert_fusion.14), channel_id=1, source_target_pairs={{8,0},{16,8},{24,16},{28,24},{20,28},{12,20},{4,12},{0,4},{9,1},{1... | collective-permute-start | bytes 1572872 | tf_op jit(solution)/shard_map/ppermute | solution.py:782
  315.7 27.5 %collective-permute-start.47 = (bf16[2,128,1024]{2,1,0:T(8,128)(2,1)S(1)}, bf16[2,128,1024]{2,1,0:T(8,128)(2,1)S(1)}, u32[]{:S(2)}, u32[]{:S(2)}) collective-permute-start(bf16[2,128,1024]{2,1,0:T(8,128)(2,1)S(1)} %add_convert_fusion.16), channel_id=1, source_target_pairs={{0,8},{8,16},{16,24},{24,28},{28,20},{20,12},{12,4},{4,0},{1,9},{9... | collective-permute-start | bytes 1572872 | tf_op jit(solution)/shard_map/ppermute | solution.py:785
  316.6 27.2 %collective-permute-start.53 = (bf16[2,128,1024]{2,1,0:T(8,128)(2,1)S(1)}, bf16[2,128,1024]{2,1,0:T(8,128)(2,1)S(1)}, u32[]{:S(2)}, u32[]{:S(2)}) collective-permute-start(bf16[2,128,1024]{2,1,0:T(8,128)(2,1)S(1)} %add_convert_fusion.13), channel_id=1, source_target_pairs={{8,0},{16,8},{24,16},{28,24},{20,28},{12,20},{4,12},{0,4},{9,1},{1... | collective-permute-start | bytes 1572872 | tf_op jit(solution)/shard_map/ppermute | solution.py:786
  326.8 28.0 %collective-permute-start.55 = (bf16[2,128,1024]{2,1,0:T(8,128)(2,1)}, bf16[2,128,1024]{2,1,0:T(8,128)(2,1)S(1)}, u32[]{:S(2)}, u32[]{:S(2)}) collective-permute-start(bf16[2,128,1024]{2,1,0:T(8,128)(2,1)} %get-tuple-element.195), channel_id=1, source_target_pairs={{8,0},{16,8},{24,16},{28,24},{20,28},{12,20},{4,12},{0,4},{9,1},{1... | collective-permute-start | bytes 1572872 | tf_op jit(solution)/shard_map/ppermute | solution.py:775
  328.3 34.3 %collective-permute-start.60 = (bf16[2,128,1024]{2,1,0:T(8,128)(2,1)}, bf16[2,128,1024]{2,1,0:T(8,128)(2,1)S(1)}, u32[]{:S(2)}, u32[]{:S(2)}) collective-permute-start(bf16[2,128,1024]{2,1,0:T(8,128)(2,1)} %get-tuple-element.207), channel_id=1, source_target_pairs={{8,0},{16,8},{24,16},{28,24},{20,28},{12,20},{4,12},{0,4},{9,1},{1... | collective-permute-start | bytes 1572872 | tf_op jit(solution)/shard_map/ppermute | solution.py:773
  329.9 26.4 %collective-permute-start.54 = (bf16[2,128,1024]{2,1,0:T(8,128)(2,1)}, bf16[2,128,1024]{2,1,0:T(8,128)(2,1)S(1)}, u32[]{:S(2)}, u32[]{:S(2)}) collective-permute-start(bf16[2,128,1024]{2,1,0:T(8,128)(2,1)} %get-tuple-element.191), channel_id=1, source_target_pairs={{0,8},{8,16},{16,24},{24,28},{28,20},{20,12},{12,4},{4,0},{1,9},{9... | collective-permute-start | bytes 1572872 | tf_op jit(solution)/shard_map/ppermute | solution.py:774
  343.2 45.7 %collective-permute-start.59 = (bf16[2,128,1024]{2,1,0:T(8,128)(2,1)}, bf16[2,128,1024]{2,1,0:T(8,128)(2,1)S(1)}, u32[]{:S(2)}, u32[]{:S(2)}) collective-permute-start(bf16[2,128,1024]{2,1,0:T(8,128)(2,1)} %get-tuple-element.204), channel_id=1, source_target_pairs={{0,8},{8,16},{16,24},{24,28},{28,20},{20,12},{12,4},{4,0},{1,9},{9... | collective-permute-start | bytes 1572872 | tf_op jit(solution)/shard_map/ppermute | solution.py:772
  356.3 34.4 %collective-permute-start.62 = (bf16[2,128,1024]{2,1,0:T(8,128)(2,1)}, bf16[2,128,1024]{2,1,0:T(8,128)(2,1)S(1)}, u32[]{:S(2)}, u32[]{:S(2)}) collective-permute-start(bf16[2,128,1024]{2,1,0:T(8,128)(2,1)} %add_convert_fusion.11), channel_id=1, source_target_pairs={{8,0},{16,8},{24,16},{28,24},{20,28},{12,20},{4,12},{0,4},{9,1},{1... | collective-permute-start | bytes 1572872 | tf_op jit(solution)/shard_map/ppermute | solution.py:786
  365.2 26.8 %collective-permute-start.61 = (bf16[2,128,1024]{2,1,0:T(8,128)(2,1)}, bf16[2,128,1024]{2,1,0:T(8,128)(2,1)S(1)}, u32[]{:S(2)}, u32[]{:S(2)}) collective-permute-start(bf16[2,128,1024]{2,1,0:T(8,128)(2,1)} %add_convert_fusion.12), channel_id=1, source_target_pairs={{0,8},{8,16},{16,24},{24,28},{28,20},{20,12},{12,4},{4,0},{1,9},{9... | collective-permute-start | bytes 1572872 | tf_op jit(solution)/shard_map/ppermute | solution.py:785
  365.7 62.0 %collective-permute-start.67 = (bf16[2,128,1024]{2,1,0:T(8,128)(2,1)}, bf16[2,128,1024]{2,1,0:T(8,128)(2,1)}, u32[]{:S(2)}, u32[]{:S(2)}) collective-permute-start(bf16[2,128,1024]{2,1,0:T(8,128)(2,1)} %add_convert_fusion.9), channel_id=1, source_target_pairs={{8,0},{16,8},{24,16},{28,24},{20,28},{12,20},{4,12},{0,4},{9,1},{1... | collective-permute-start | bytes 1572872 | tf_op jit(solution)/shard_map/ppermute | solution.py:782
  372.5 36.1 %collective-permute-start.83 = (bf16[2,256,1024]{2,1,0:T(8,128)(2,1)S(1)}, bf16[2,256,1024]{2,1,0:T(8,128)(2,1)S(1)}, u32[]{:S(2)}, u32[]{:S(2)}) collective-permute-start(bf16[2,256,1024]{2,1,0:T(8,128)(2,1)S(1)} %pad_maximum_fusion.5), channel_id=1, source_target_pairs={{0,1},{1,0},{2,3},{3,2},{4,5},{5,4},{6,7},{7,6},{8,9},{9,8},{10,11... | collective-permute-start | bytes 3145736 | tf_op jit(solution)/shard_map/ppermute | solution.py:687
  388.9 112.3 %collective-permute-start.77 = (bf16[2,1056,256]{2,1,0:T(8,128)(2,1)}, bf16[2,1056,256]{2,1,0:T(8,128)(2,1)}, u32[]{:S(2)}, u32[]{:S(2)}) collective-permute-start(bf16[2,1056,256]{2,1,0:T(8,128)(2,1)} %get-tuple-element.232), channel_id=1, source_target_pairs={{0,1},{1,0},{2,3},{3,2},{4,5},{5,4},{6,7},{7,6},{8,9},{9,8},{10,11... | collective-permute-start | bytes 3244040 | tf_op jit(solution)/shard_map/ppermute | solution.py:687
  390.7 70.0 %collective-permute-start.65 = (bf16[2,128,1024]{2,1,0:T(8,128)(2,1)}, bf16[2,128,1024]{2,1,0:T(8,128)(2,1)}, u32[]{:S(2)}, u32[]{:S(2)}) collective-permute-start(bf16[2,128,1024]{2,1,0:T(8,128)(2,1)} %add_convert_fusion.10), channel_id=1, source_target_pairs={{0,8},{8,16},{16,24},{24,28},{28,20},{20,12},{12,4},{4,0},{1,9},{9... | collective-permute-start | bytes 1572872 | tf_op jit(solution)/shard_map/ppermute | solution.py:781
  392.1 78.7 %collective-permute-start.69 = (bf16[2,128,1024]{2,1,0:T(8,128)(2,1)}, bf16[2,128,1024]{2,1,0:T(8,128)(2,1)}, u32[]{:S(2)}, u32[]{:S(2)}) collective-permute-start(bf16[2,128,1024]{2,1,0:T(8,128)(2,1)} %add_convert_fusion.7), channel_id=1, source_target_pairs={{8,0},{16,8},{24,16},{28,24},{20,28},{12,20},{4,12},{0,4},{9,1},{1... | collective-permute-start | bytes 1572872 | tf_op jit(solution)/shard_map/ppermute | solution.py:786
  414.9 153.8 %all-to-all-start = ((bf16[8,390,256]{2,1,0:T(8,128)(2,1)}), bf16[8,390,256]{2,1,0:T(8,128)(2,1)S(1)}, u32[]{:S(2)}, u32[]{:S(2)}) async-start(bf16[8,390,256]{2,1,0:T(8,128)(2,1)} %pad_maximum_fusion.2), calls=%async_computation | async-start | bytes 3211264 | tf_op jit(solution)/shard_map/all_to_all | solution.py:949
  424.8 61.9 %collective-permute-start.63 = (bf16[2,128,1024]{2,1,0:T(8,128)(2,1)}, bf16[2,128,1024]{2,1,0:T(8,128)(2,1)}, u32[]{:S(2)}, u32[]{:S(2)}) collective-permute-start(bf16[2,128,1024]{2,1,0:T(8,128)(2,1)} %add_convert_fusion.8), channel_id=1, source_target_pairs={{0,8},{8,16},{16,24},{24,28},{28,20},{20,12},{12,4},{4,0},{1,9},{9... | collective-permute-start | bytes 1572872 | tf_op jit(solution)/shard_map/ppermute | solution.py:785
  460.6 69.3 %collective-permute-start.79 = (bf16[2,1056,256]{2,1,0:T(8,128)(2,1)}, bf16[2,1056,256]{2,1,0:T(8,128)(2,1)}, u32[]{:S(2)}, u32[]{:S(2)}) collective-permute-start(bf16[2,1056,256]{2,1,0:T(8,128)(2,1)} %get-tuple-element.233), channel_id=1, source_target_pairs={{0,1},{1,0},{2,3},{3,2},{4,5},{5,4},{6,7},{7,6},{8,9},{9,8},{10,11... | collective-permute-start | bytes 3244040 | tf_op jit(solution)/shard_map/ppermute | solution.py:687
  466.5 34.3 %collective-permute-start.68 = (bf16[2,128,1024]{2,1,0:T(8,128)(2,1)S(1)}, bf16[2,128,1024]{2,1,0:T(8,128)(2,1)S(1)}, u32[]{:S(2)}, u32[]{:S(2)}) collective-permute-start(bf16[2,128,1024]{2,1,0:T(8,128)(2,1)S(1)} %add_convert_fusion.4), channel_id=1, source_target_pairs={{8,0},{16,8},{24,16},{28,24},{20,28},{12,20},{4,12},{0,4},{9,1},{1... | collective-permute-start | bytes 1572872 | tf_op jit(solution)/shard_map/ppermute | solution.py:782
  475.1 32.7 %collective-permute-start.66 = (bf16[2,128,1024]{2,1,0:T(8,128)(2,1)S(1)}, bf16[2,128,1024]{2,1,0:T(8,128)(2,1)S(1)}, u32[]{:S(2)}, u32[]{:S(2)}) collective-permute-start(bf16[2,128,1024]{2,1,0:T(8,128)(2,1)S(1)} %add_convert_fusion.5), channel_id=1, source_target_pairs={{0,8},{8,16},{16,24},{24,28},{28,20},{20,12},{12,4},{4,0},{1,9},{9... | collective-permute-start | bytes 1572872 | tf_op jit(solution)/shard_map/ppermute | solution.py:781
  501.2 27.7 %collective-permute-start.90 = (bf16[4,32,1024]{2,1,0:T(8,128)(2,1)S(1)}, bf16[4,32,1024]{2,1,0:T(8,128)(2,1)S(1)}, u32[]{:S(2)}, u32[]{:S(2)}) collective-permute-start(bf16[4,32,1024]{2,1,0:T(8,128)(2,1)S(1)} %pad_maximum_fusion.9), channel_id=1, source_target_pairs={{0,16},{4,20},{8,24},{12,28},{16,0},{20,4},{24,8},{28,12},{1,17},{... | collective-permute-start | bytes 786440 | tf_op jit(solution)/shard_map/ppermute | solution.py:687
  507.8 56.6 %collective-permute-start.78 = (bf16[1,1056,256]{2,1,0:T(8,128)(2,1)S(1)}, bf16[1,1056,256]{2,1,0:T(8,128)(2,1)}, u32[]{:S(2)}, u32[]{:S(2)}) collective-permute-start(bf16[1,1056,256]{2,1,0:T(8,128)(2,1)S(1)} %add_convert_fusion.2), channel_id=1, source_target_pairs={{0,2},{1,3},{2,0},{3,1},{4,6},{5,7},{6,4},{7,5},{8,10},{9,11},{10,... | collective-permute-start | bytes 1622024 | tf_op jit(solution)/shard_map/ppermute | solution.py:687
  536.4 28.0 %collective-permute-start.75 = (bf16[4,128,256]{2,1,0:T(8,128)(2,1)S(1)}, bf16[4,128,256]{2,1,0:T(8,128)(2,1)S(1)}, u32[]{:S(2)}, u32[]{:S(2)}) collective-permute-start(bf16[4,128,256]{2,1,0:T(8,128)(2,1)S(1)} %copy-done.87), channel_id=1, source_target_pairs={{0,2},{1,3},{2,0},{3,1},{4,6},{5,7},{6,4},{7,5},{8,10},{9,11},{10,... | collective-permute-start | bytes 786440 | tf_op jit(solution)/shard_map/ppermute | solution.py:687
  558.2 27.0 %collective-permute-start.92 = (bf16[2,8,32,1024]{3,2,1,0:T(8,128)(2,1)}, bf16[2,8,32,1024]{3,2,1,0:T(8,128)(2,1)}, u32[]{:S(2)}, u32[]{:S(2)}) collective-permute-start(bf16[2,8,32,1024]{3,2,1,0:T(8,128)(2,1)} %pad_maximum_fusion.6), channel_id=1, source_target_pairs={{0,1},{1,0},{2,3},{3,2},{4,5},{5,4},{6,7},{7,6},{8,9},{9,8},{10,11... | collective-permute-start | bytes 3145736 | tf_op jit(solution)/shard_map/ppermute | solution.py:687
  (140 other events, 1827.1 us)

commit v3 on v2

--- a/solution.py
+++ b/solution.py
@@ -13,7 +13,7 @@
 GROUP = 16
 STEP = 32
 EXTRA = 16
-COST = 0.5
+COST = 0.0001
 VMEM_LIMIT = 56 * 1024 * 1024
 
 f32 = jnp.float32
@@ -260,9 +260,8 @@
 def project_kernel(count, chunks, idx_ref, *refs):
     mixed = refs[: count * chunks]
     resids = refs[count * chunks : (count + 1) * chunks]
-    w_ref, gain_ref, hidden_ref, first_ref, second_ref = refs[(count + 1) * chunks :]
+    w_ref, gain_ref, hidden_ref, norm_ref = refs[(count + 1) * chunks :]
     me = idx_ref[0]
-    is_first = pl.program_id(0) < pl.num_programs(0) // 2
     size = mixed[0].shape[1]
     for c in range(chunks):
         f = slice(c * size, (c + 1) * size)
@@ -271,8 +270,7 @@
             hidden = hidden + dot(mixed[c * count + j][0], w_ref[me ^ j], 1, 0)
         hidden_ref[0, f] = hidden
         rms = lax.rsqrt(jnp.mean(hidden * hidden, axis=-1, keepdims=True) + EPS)
-        norm = (hidden * rms * gain_ref[0]).astype(bf16)
-        store_half(is_first, first_ref, second_ref, (0, f), norm)
+        norm_ref[0, f] = (hidden * rms * gain_ref[0]).astype(bf16)
 
 
 def project(idx, mixed, resids, w, gain):
@@ -291,25 +289,39 @@
                 pl.BlockSpec(w.shape, lambda k, s: (0, 0, 0)),
                 pl.BlockSpec((1, 1, width), lambda k, s: (k, 0, 0)),
             ],
-            out_specs=[each, *half_specs(local, frames, width)],
+            out_specs=[each, each],
         ),
         out_shape=[
             jax.ShapeDtypeStruct((local, frames, width), f32),
-            *[jax.ShapeDtypeStruct((local // 2, frames, width), bf16)] * 2,
+            jax.ShapeDtypeStruct((local, frames, width), bf16),
         ],
         compiler_params=params(),
         cost_estimate=cost(6),
     )(idx, *[m for part_ in mixed for m in part_], *resids, w, gain)
 
 
-def ffn_kernel(n, *refs):
-    norms, grads, w_ref = refs[: 2 * n], refs[2 * n : 4 * n], refs[4 * n]
-    dnorms, branches = refs[4 * n + 1 : 6 * n + 1], refs[6 * n + 1 : 8 * n + 1]
+def load_block(is_first, refs):
+    return refs[0][0] if len(refs) == 1 else load_half(is_first, *refs)
+
+
+def block_parts(block):
+    return list(block) if isinstance(block, tuple) else [block]
+
+
+def ffn_kernel(sizes, idx_ref, *refs):
+    n = len(sizes) // 2
+    ins = sum(sizes)
+    w_ref = refs[ins]
+    dnorms, branches = refs[ins + 1 : ins + 1 + 2 * n], refs[ins + 1 + 2 * n : ins + 1 + 3 * n]
     act_ref = refs[-1]
-    frames = norms[0].shape[1]
     is_first = pl.program_id(0) < pl.num_programs(0) // 2
-    norm = jnp.concatenate([load_half(is_first, *norms[2 * i : 2 * i + 2]) for i in range(n)], 0)
-    grad = jnp.concatenate([load_half(is_first, *grads[2 * i : 2 * i + 2]) for i in range(n)], 0)
+    blocks, at = [], 0
+    for size in sizes:
+        blocks.append(load_block(is_first, refs[at : at + size]))
+        at += size
+    frames = blocks[0].shape[0]
+    norm = jnp.concatenate(blocks[:n], 0)
+    grad = jnp.concatenate(blocks[n:], 0)
     gate = dot(norm, w_ref[0, 0], 1, 1)
     up = dot(norm, w_ref[0, 1], 1, 1)
     dact = dot(grad, w_ref[0, 2], 1, 1)
@@ -326,38 +338,54 @@
     for i in range(n):
         rows = slice(i * frames, (i + 1) * frames)
         store_half(is_first, *dnorms[2 * i : 2 * i + 2], 0, dnorm[rows])
-        store_half(is_first, *branches[2 * i : 2 * i + 2], 0, branch[rows])
-
-
-def ffn(norms, grads, w):
+        branches[i][0] = branch[rows]
+
+
+def ffn(idx, norms, grads, w):
     n = len(norms)
-    half, frames, width = norms[0][0].shape
-    local, _, hidden, _ = w.shape
-    specs = half_specs(local, frames, width)
+    blocks = [block_parts(v) for v in (*norms, *grads)]
+    local, _, hidden, width = w.shape
+    frames = blocks[0][0].shape[1]
+    halves = half_specs(local, frames, width)
+    whole = [pl.BlockSpec((1, frames, width), lambda k, s: (k, 0, 0))]
     *out, act = pl.pallas_call(
-        functools.partial(ffn_kernel, n),
-        grid=(local,),
-        in_specs=specs * (2 * n)
-        + [pl.BlockSpec((1, 3, hidden, width), lambda k: (k, 0, 0, 0))],
-        out_specs=specs * (2 * n)
-        + [pl.BlockSpec((1, 3, n * frames, hidden), lambda k: (k, 0, 0, 0))],
-        out_shape=[jax.ShapeDtypeStruct((half, frames, width), bf16)] * (4 * n)
+        functools.partial(ffn_kernel, [len(v) for v in blocks]),
+        grid_spec=pltpu.PrefetchScalarGridSpec(
+            num_scalar_prefetch=1,
+            grid=(local,),
+            in_specs=[x for v in blocks for x in (whole if len(v) == 1 else halves)]
+            + [pl.BlockSpec((1, 3, hidden, width), lambda k, s: (k, 0, 0, 0))],
+            out_specs=halves * n
+            + whole * n
+            + [pl.BlockSpec((1, 3, n * frames, hidden), lambda k, s: (k, 0, 0, 0))],
+        ),
+        out_shape=[jax.ShapeDtypeStruct((local // 2, frames, width), bf16)] * (2 * n)
+        + [jax.ShapeDtypeStruct((local, frames, width), bf16)] * n
         + [jax.ShapeDtypeStruct((local, 3, n * frames, hidden), bf16)],
         compiler_params=params(),
         cost_estimate=cost(3.5 + 5 * n),
-    )(*[h for v in norms for h in v], *[h for v in grads for h in v], w)
-    pairs = [out[i : i + 2] for i in range(0, 4 * n, 2)]
-    return pairs[:n], pairs[n:], act
-
-
-def weight_kernel(n, row, *refs):
-    acts, others, out_ref = refs[:n], refs[n : -1], refs[-1]
-    half, frames, _ = others[0].shape
-    for k in range(acts[0].shape[0]):
+    )(idx, *[x for v in blocks for x in v], w)
+    pairs = [out[i : i + 2] for i in range(0, 2 * n, 2)]
+    return pairs, out[2 * n :], act
+
+
+def weight_kernel(n, row, sizes, idx_ref, *refs):
+    acts, out_ref = refs[:n], refs[-1]
+    local = acts[0].shape[0]
+    others, at = [], n
+    for size in sizes:
+        others.append(refs[at : at + size])
+        at += size
+    frames = others[0][0].shape[1]
+
+    def entry(block, k):
+        return block[k // block[0].shape[0]][k % block[0].shape[0]]
+
+    for k in range(local):
         total, first = None, 0
         for a in acts:
             size = a.shape[2] // frames
-            both = [others[2 * (first + i) + k // half][k % half] for i in range(size)]
+            both = [entry(others[first + i], k) for i in range(size)]
             first += size
             both = jnp.concatenate(both, 0) if size > 1 else both[0]
             term = dot(a[k, 0], both, 0, 0)
@@ -365,44 +393,95 @@
         out_ref[:, 0, k] = total
 
 
-def weight_grad(acts, others, row, out):
+def weight_grad(idx, acts, others, row, out):
     n = len(acts)
-    half, frames, width = others[0][0].shape
     local, _, _, hidden = acts[0].shape
     chunk = min(128, hidden)
-    whole = pl.BlockSpec(
-        (half, frames, width), lambda c: (0, 0, 0), pipeline_mode=pl.Buffered(1)
-    )
-    others = [h for v in others for h in v]
-    ins = list(acts) + others
+    others = [block_parts(v) for v in others]
+    width = others[0][0].shape[2]
+    ins = list(acts) + [x for v in others for x in v]
     specs = [
-        pl.BlockSpec((local, 1, a.shape[2], chunk), lambda c: (0, row, 0, c)) for a in acts
-    ] + [whole] * len(others)
+        pl.BlockSpec((local, 1, a.shape[2], chunk), lambda c, s: (0, row, 0, c)) for a in acts
+    ] + [
+        pl.BlockSpec(x.shape, lambda c, s: (0, 0, 0), pipeline_mode=pl.Buffered(1))
+        for v in others
+        for x in v
+    ]
     aliases = {}
-    kernel = functools.partial(weight_kernel, n, row)
+    kernel = functools.partial(weight_kernel, n, row, [len(v) for v in others])
     if out is not None:
-        aliases = {len(ins): 0}
+        aliases = {1 + len(ins): 0}
         ins.append(out)
         specs.append(pl.BlockSpec(memory_space=pl.ANY))
-        kernel = lambda *refs: weight_kernel(n, row, *refs[:-2], refs[-1])
     return pl.pallas_call(
         kernel,
-        grid=(hidden // chunk,),
-        in_specs=specs,
-        out_specs=pl.BlockSpec((chunk, 1, local, width), lambda c: (c, row, 0, 0)),
+        grid_spec=pltpu.PrefetchScalarGridSpec(
+            num_scalar_prefetch=1,
+            grid=(hidden // chunk,),
+            in_specs=specs,
+            out_specs=pl.BlockSpec((chunk, 1, local, width), lambda c, s: (c, row, 0, 0)),
+        ),
         out_shape=jax.ShapeDtypeStruct((hidden, 3, local, width), f32),
         input_output_aliases=aliases,
         compiler_params=params(),
         cost_estimate=cost(12),
-    )(*ins)
+    )(idx, *ins)
 
 
 def add_low(x, y):
     return (x.astype(f32) + y.astype(f32)).astype(bf16)
 
 
-def merge(x, y, up, down):
-    return add_low(x, up), add_low(y, down)
+def merge_kernel(n, idx_ref, *refs):
+    for i in range(n):
+        refs[2 * n + i][...] = add_low(refs[i][...], refs[n + i][...])
+
+
+def merge(idx, mine, moved):
+    n = len(mine)
+    half, frames, width = mine[0].shape
+    each = pl.BlockSpec((1, frames, width), lambda k, s: (k, 0, 0))
+    return pl.pallas_call(
+        functools.partial(merge_kernel, n),
+        grid_spec=pltpu.PrefetchScalarGridSpec(
+            num_scalar_prefetch=1,
+            grid=(half,),
+            in_specs=[each] * (2 * n),
+            out_specs=[each] * n,
+        ),
+        out_shape=[jax.ShapeDtypeStruct(mine[0].shape, bf16)] * n,
+        compiler_params=params(),
+        cost_estimate=cost(1.2 * n),
+    )(idx, *mine, *moved)
+
+
+def whole_kernel(half, idx_ref, f_ref, b_ref, up_ref, down_ref, fo_ref, bo_ref):
+    if half is None:
+        fo_ref[...] = add_low(f_ref[...], up_ref[...])
+        bo_ref[...] = add_low(b_ref[...], down_ref[...])
+        return
+    is_first = pl.program_id(0) < half
+    fo_ref[...] = jnp.where(is_first, add_low(f_ref[...], up_ref[...]), f_ref[...])
+    bo_ref[...] = jnp.where(is_first, b_ref[...], add_low(b_ref[...], down_ref[...]))
+
+
+def merge_whole(idx, f, b, up, down):
+    local, frames, width = f.shape
+    half = None if up.shape == f.shape else local // 2
+    each = pl.BlockSpec((1, frames, width), lambda k, s: (k, 0, 0))
+    moved = half_specs(local, frames, width) if half else [each] * 2
+    return pl.pallas_call(
+        functools.partial(whole_kernel, half),
+        grid_spec=pltpu.PrefetchScalarGridSpec(
+            num_scalar_prefetch=1,
+            grid=(local,),
+            in_specs=[each, each, *moved],
+            out_specs=[each, each],
+        ),
+        out_shape=[jax.ShapeDtypeStruct(f.shape, bf16)] * 2,
+        compiler_params=params(),
+        cost_estimate=cost(4),
+    )(idx, f, b, up, down)
 
 
 def sum_halves(refs):
@@ -462,11 +541,11 @@
     )(idx, *recv, *own, hidden, branch, gain, w)
 
 
-def attn_back_kernel(count, idx_ref, *refs):
+def attn_back_kernel(count, ring, idx_ref, *refs):
     xs = refs[:count]
     dms = refs[count : 2 * count]
     qkv_ref, w_ref, gain_ref, live_ref = refs[2 * count : 2 * count + 4]
-    keep_ref, send_ref, wsum_ref, gsum_ref = refs[2 * count + 4 :]
+    keep_ref, send_ref, wlow_ref, gsum_ref, wsum_ref = refs[2 * count + 4 :]
     me = idx_ref[0]
     step, depth, part = xs[0].shape
     rows = GROUP * depth
@@ -528,24 +607,33 @@
         send_ref[i, rows:] = lines
         keep_ref[i, rows:] = lines
 
-
-def attention_back(idx, xs, dms, qkv, w, gain, live, chunk, chunks):
+    @pl.when(pl.program_id(0) == pl.num_programs(0) - 1)
+    def _():
+        size = part * count // ring
+        for i in range(ring):
+            block, line = i * size // part, i * size % part
+            for c in range(3):
+                wlow_ref[i, c * size : (c + 1) * size] = wsum_ref[
+                    c, block, line : line + size
+                ].astype(bf16)
+
+
+def attention_back(idx, xs, dms, qkv, w, gain, live, ring):
     count = len(xs)
     frames, depth, part = xs[0].shape
     local = dms[0].shape[0]
-    frames = frames // chunks
     step = per_step(frames, STEP)
     n = frames // step
-    base = chunk * n
     rows = step * depth
-    lives = pl.BlockSpec((step // GROUP, 1, GROUP * depth), lambda i, s: (i + base, 0, 0))
-    return pl.pallas_call(
-        functools.partial(attn_back_kernel, count),
+    low_shape = (ring, 3 * part * count // ring, part)
+    lives = pl.BlockSpec((step // GROUP, 1, GROUP * depth), lambda i, s: (i, 0, 0))
+    return pl.pallas_call(
+        functools.partial(attn_back_kernel, count, ring),
         grid_spec=pltpu.PrefetchScalarGridSpec(
             num_scalar_prefetch=1,
             grid=(n,),
-            in_specs=[pl.BlockSpec((step, depth, part), lambda i, s: (i + base, 0, 0))] * count
-            + [pl.BlockSpec((local, step, part), lambda i, s: (0, i + base, 0))] * count
+            in_specs=[pl.BlockSpec((step, depth, part), lambda i, s: (i, 0, 0))] * count
+            + [pl.BlockSpec((local, step, part), lambda i, s: (0, i, 0))] * count
             + [
                 pl.BlockSpec((3, rows, part), lambda i, s: (0, i, 0)),
                 pl.BlockSpec(w.shape, lambda i, s: (0, 0, 0, 0)),
@@ -554,18 +642,87 @@
             ],
             out_specs=[pl.BlockSpec((count // 2, rows + EXTRA, part), lambda i, s: (0, i, 0))] * 2
             + [
-                pl.BlockSpec(w.shape, lambda i, s: (0, 0, 0, 0)),
+                pl.BlockSpec(low_shape, lambda i, s: (0, 0, 0)),
                 pl.BlockSpec((count, 1, part), lambda i, s: (0, 0, 0)),
             ],
+            scratch_shapes=[pltpu.VMEM(w.shape, f32)],
         ),
         out_shape=[jax.ShapeDtypeStruct((count // 2, n * (rows + EXTRA), part), bf16)] * 2
         + [
-            jax.ShapeDtypeStruct(w.shape, f32),
+            jax.ShapeDtypeStruct(low_shape, bf16),
             jax.ShapeDtypeStruct((count, 1, part), f32),
         ],
         compiler_params=params(),
-        cost_estimate=cost(14),
+        cost_estimate=cost(26),
     )(idx, *xs, *dms, qkv, w, gain, live)
+
+
+def fold_kernel(n, idx_ref, *refs):
+    total = refs[0][...].astype(f32)
+    for r in refs[1:n]:
+        total = total + r[...].astype(f32)
+    refs[n][...] = total.astype(bf16)
+
+
+def fold(idx, terms, bit):
+    n = len(terms)
+    _, rows, part = terms[0].shape
+    hop = bit // 2
+
+    def spec(i):
+        step = 1 if i < 2 else 1 << (i - 1)
+        return pl.BlockSpec((1, rows, part), lambda g, s: (hop * (2 * g + 1) // step, 0, 0))
+
+    return pl.pallas_call(
+        functools.partial(fold_kernel, n),
+        grid_spec=pltpu.PrefetchScalarGridSpec(
+            num_scalar_prefetch=1,
+            grid=(terms[0].shape[0] // bit,),
+            in_specs=[spec(i) for i in range(n)],
+            out_specs=pl.BlockSpec((1, rows, part), lambda g, s: (g, 0, 0)),
+        ),
+        out_shape=jax.ShapeDtypeStruct((terms[0].shape[0] // bit, rows, part), bf16),
+        compiler_params=params(),
+        cost_estimate=cost(2),
+    )(idx, *terms)
+
+
+def out_kernel(count, chunks, idx_ref, *refs):
+    low_ref, outs = refs[count * chunks], refs[count * chunks + 1 :]
+    local, size, _ = refs[0].shape
+    width = low_ref.shape[2]
+    lows = []
+    for c in range(chunks):
+        part_ = low_ref[:, c * size : (c + 1) * size]
+        lows.append(part_.reshape(local * size, width))
+    low = jnp.concatenate(lows, 0)
+    for j in range(count):
+        mine = [refs[c * count + j][...].reshape(local * size, -1) for c in range(chunks)]
+        out = dot(jnp.concatenate(mine, 0), low, 0, 0).astype(bf16)
+        if j & 1:
+            outs[-1][j // 2] = out
+        else:
+            outs[j // 2][...] = out
+
+
+def out_terms(idx, mixeds, low):
+    chunks, count = len(mixeds), len(mixeds[0])
+    part, width = mixeds[0][0].shape[2], low.shape[2]
+    return pl.pallas_call(
+        functools.partial(out_kernel, count, chunks),
+        grid_spec=pltpu.PrefetchScalarGridSpec(
+            num_scalar_prefetch=1,
+            grid=(1,),
+            in_specs=[pl.BlockSpec(m.shape, lambda i, s: (0, 0, 0)) for p in mixeds for m in p]
+            + [pl.BlockSpec(low.shape, lambda i, s: (0, 0, 0))],
+            out_specs=[pl.BlockSpec((part, width), lambda i, s: (0, 0))] * (count // 2)
+            + [pl.BlockSpec((count // 2, part, width), lambda i, s: (0, 0, 0))],
+        ),
+        out_shape=[jax.ShapeDtypeStruct((part, width), bf16)] * (count // 2)
+        + [jax.ShapeDtypeStruct((count // 2, part, width), bf16)],
+        compiler_params=params(),
+        cost_estimate=cost(6),
+    )(idx, *[m for p in mixeds for m in p], low)
 
 
 def input_kernel(count, terms_count, idx_ref, *refs):
@@ -625,10 +782,11 @@
 
 
 def block_kernel(count, idx_ref, *refs):
-    hidden_ref, live_ref, outs = refs[6], refs[7], refs[8:]
+    up, down, own, hidden_ref, live_ref = refs[:5]
+    outs = refs[5:]
     me = idx_ref[0]
     part = outs[0].shape[2]
-    branch = sum_halves(refs[:6])
+    branch = up[0].astype(f32) + down[0].astype(f32) + own[0].astype(f32)
     rows = ((hidden_ref[0] + branch) * row_to_column(live_ref[0])).astype(bf16)
     blocks = [rows[:, b * part : (b + 1) * part] for b in range(count)]
     for j in range(count):
@@ -644,14 +802,13 @@
         grid_spec=pltpu.PrefetchScalarGridSpec(
             num_scalar_prefetch=1,
             grid=(local,),
-            in_specs=half_specs(local, frames, width) * 3
-            + [each, pl.BlockSpec((1, 1, frames), lambda k, s: (k, 0, 0))],
+            in_specs=[each] * 4 + [pl.BlockSpec((1, 1, frames), lambda k, s: (k, 0, 0))],
             out_specs=[pl.BlockSpec((1, frames, part), lambda k, s: (k, 0, 0))] * count,
         ),
         out_shape=[jax.ShapeDtypeStruct((local, frames, part), bf16)] * count,
         compiler_params=params(),
         cost_estimate=cost(4),
-    )(idx, *recv, *own, hidden, live)
+    )(idx, *recv, own, hidden, live)
 
 
 def gather_kernel(count, idx_ref, *refs):
@@ -683,58 +840,39 @@
     )(idx, *pieces)
 
 
-def swap(value, count, bits, axis="pos"):
-    return lax.ppermute(value, axis, [(i, i ^ bits) for i in range(count)])
-
-
-def exchange(pieces):
-    count = len(pieces)
-    return [pieces[0]] + [swap(pieces[j], count, j) for j in range(1, count)]
-
-
-def gather_pos(value, count):
-    pieces = {0: value}
-    bit = count // 2
-    while bit:
-        for j in list(pieces):
-            pieces[j ^ bit] = swap(pieces[j], count, bit)
-        bit //= 2
-    return [pieces[j] for j in range(count)]
-
-
-def sum_axis(value, count, axis):
-    bit = 1
-    while bit < count:
-        value = value + swap(value, count, bit, axis)
-        bit *= 2
-    return value
-
-
-def after(value, *others):
-    return lax.optimization_barrier((value, *others))[0]
-
-
-def scatter_halves(blocks, bits, axis):
-    count = blocks.shape[0]
-    blocks = blocks.astype(f32)
-    left = list(range(count))
-    for bit in bits:
-        keep = [i for i, j in enumerate(left) if not j & bit]
-        send = [left.index(left[i] ^ bit) for i in keep]
-        moved = swap(jnp.stack([blocks[i] for i in send]).astype(bf16), count, bit, axis)
-        blocks = jnp.stack([blocks[i] for i in keep]) + moved.astype(f32)
-        left = [left[i] for i in keep]
-    return blocks[0]
-
-
-def gather_doubles(value, count, bits, axis):
-    blocks, have = value[None], [0]
-    for bit in bits:
-        blocks = jnp.concatenate([blocks, swap(blocks, count, bit, axis)], 0)
-        have = have + [j ^ bit for j in have]
-    inverse = jnp.array([have.index(j) for j in range(count)])
-    order = jnp.take(inverse, lax.axis_index(axis) ^ jnp.arange(count), mode="clip")
-    return jnp.take(blocks, order, axis=0, mode="clip")
+class Order:
+    def __init__(self):
+        self.last = []
+
+    def tie(self, *values, after=()):
+        flat, tree = jax.tree.flatten(values)
+        held = [*self.last, *jax.tree.leaves(after)]
+        if held:
+            flat = lax.optimization_barrier((*flat, *held))[: len(flat)]
+        values = jax.tree.unflatten(tree, flat)
+        return values[0] if len(values) == 1 else values
+
+    def run(self, kernel, first, *args, after=()):
+        out = kernel(self.tie(first, after=after), *args)
+        self.last = [min(jax.tree.leaves(out), key=lambda v: v.size)]
+        return out
+
+    def fuse(self, step, *args, after=()):
+        args = self.tie(*args, after=after)
+        out = step(*args) if isinstance(args, tuple) else step(args)
+        self.last = jax.tree.leaves(out)
+        return out
+
+    def send(self, value, axis, pairs):
+        return lax.ppermute(self.tie(value), axis, pairs)
+
+    def swap(self, value, bits, axis="pos"):
+        count = lax.axis_size(axis)
+        return self.send(value, axis, [(i, i ^ bits) for i in range(count)])
+
+    def exchange(self, pieces):
+        back = {j: self.swap(pieces[j], j) for j in range(len(pieces) - 1, 0, -1)}
+        return [pieces[0]] + [back[j] for j in range(1, len(pieces))]
 
 
 def ring_steps(count):
@@ -743,63 +881,91 @@
     return forward, [(b, a) for a, b in forward]
 
 
-def ring_gather(value, steps, count, beside=None):
-    forward, back = steps
-    far = count // 2
-    blocks = [[None, None] for _ in range(count)]
-    blocks[0] = list(value)
-    x_up, x_down = value
-    y_up, y_down = value[1], value[0]
-    tie = []
-    for s in range(1, far + 1):
-        if tie:
-            x_up, x_down = after(x_up, *tie), after(x_down, *tie)
-            y_up, y_down = after(y_up, *tie), after(y_down, *tie)
-        tie = beside(s - 1, blocks) if beside else []
-        x_up = blocks[s][0] = lax.ppermute(x_up, "frames", forward)
-        x_down = blocks[count - s][1] = lax.ppermute(x_down, "frames", back)
-        if s < far:
-            y_up = blocks[s][1] = lax.ppermute(y_up, "frames", forward)
-            y_down = blocks[count - s][0] = lax.ppermute(y_down, "frames", back)
-    if beside:
-        beside(far, blocks)
-    return blocks
-
-
-def ring_sum(blocks, steps, count, beside):
-    forward, back = steps
-    far = count // 2
-    y_up = lax.ppermute(blocks[count - far + 1][1], "frames", forward)
-    y_down = lax.ppermute(blocks[far - 1][0], "frames", back)
-    x_up = lax.ppermute(blocks[far][0], "frames", forward)
-    x_down = lax.ppermute(blocks[far][1], "frames", back)
-    tie = beside(0, blocks[far])
-    for h in range(far - 1, 0, -1):
-        ready = []
-        if h < far - 1:
-            x, y = merge(after(blocks[count - h][1], *tie), blocks[h][0], y_up, y_down)
-            y_up = lax.ppermute(x, "frames", forward)
-            y_down = lax.ppermute(y, "frames", back)
-            ready = [x, y]
-        x, y = merge(after(blocks[count - h][0], *tie), blocks[h][1], x_up, x_down)
-        x_up = lax.ppermute(x, "frames", forward)
-        x_down = lax.ppermute(y, "frames", back)
-        tie = beside(far - h, ready + [x, y])
-    return [x_up, y_up, y_down, x_down], tie
-
-
-CHUNKS = 2
+class RingGather:
+    def __init__(self, order, count, value):
+        self.order, self.count = order, count
+        self.forward, self.back = ring_steps(count)
+        self.blocks = [value] + [None] * (count - 1)
+
+    def step(self, s):
+        count, blocks = self.count, self.blocks
+        up, down = blocks[s - 1], blocks[(count - s + 1) % count]
+        if s == count // 2:
+            half = up.shape[0] // 2
+            up, down = up[:half], down[half:]
+        up = self.order.send(up, "frames", self.forward)
+        down = self.order.send(down, "frames", self.back)
+        if s < count // 2:
+            blocks[s], blocks[count - s] = up, down
+        else:
+            blocks[s] = (up, down)
+
+    def received(self, s):
+        return [self.blocks[s], self.blocks[self.count - s]]
+
+
+class RingSumWhole:
+    def __init__(self, order, count, blocks, idx):
+        self.order, self.count, self.blocks, self.idx = order, count, blocks, idx
+        self.forward, self.back = ring_steps(count)
+
+    def step(self, s, after=()):
+        count, far = self.count, self.count // 2
+        if s == 1:
+            block = self.blocks[far]
+            half = block.shape[0] // 2
+            f, b = block[:half], block[half:]
+        else:
+            h = far - s + 1
+            f, b = self.order.run(
+                merge_whole, self.idx, self.blocks[count - h], self.blocks[h], *self.parts, after=after
+            )
+        self.parts = [
+            self.order.send(f, "frames", self.forward),
+            self.order.send(b, "frames", self.back),
+        ]
+
+
+class RingSum:
+    def __init__(self, order, count, blocks, idx):
+        self.order, self.count, self.blocks, self.idx = order, count, blocks, idx
+        self.forward, self.back = ring_steps(count)
+        self.parts = {}
+
+    def step(self, chains, s, after=()):
+        count, far = self.count, self.count // 2
+        mine = []
+        for chain in chains:
+            h = far - s + 1 if chain == "x" else far - s
+            first, second = (0, 1) if chain == "x" else (1, 0)
+            mine += [self.blocks[(count - h) % count][first], self.blocks[h][second]]
+        if s > 1:
+            moved = [p for chain in chains for p in self.parts[chain]]
+            mine = self.order.run(merge, self.idx, mine, moved, after=after)
+        for i, chain in enumerate(chains):
+            self.parts[chain] = [
+                self.order.send(mine[2 * i], "frames", self.forward),
+                self.order.send(mine[2 * i + 1], "frames", self.back),
+            ]
+
+    def received(self):
+        return [self.parts["x"][0], self.parts["y"][0], self.parts["y"][1], self.parts["x"][1]]
+
+
+CHUNKS = 1
 
 
 def body(inputs, counts, gain_attn, weight_qkv, weight_out, gain_ffn, weight_ffn, cotangent):
     count = lax.axis_size("pos")
     ring = lax.axis_size("frames")
+    far = ring // 2
     me = lax.axis_index("pos")
     idx = me.astype(jnp.int32).reshape(1)
     frames, depth, part = inputs.shape
     width = part * count
     local = depth // count
-    steps = ring_steps(ring)
+    half = local // 2
+    order = Order()
 
     positions = jnp.arange(depth, dtype=jnp.int32)
     live = (positions[None, :] < counts[:, None]).astype(f32)
@@ -809,156 +975,186 @@
     w_out = weight_out.reshape(count, part, width)
     gain1 = gain_attn.reshape(count, 1, part)
     gain2 = gain_ffn.reshape(local, 1, width)
-
-    cot_pieces = split_cot(idx, cotangent, live_rows, count)
-    w_ffn = after(weight_ffn, cot_pieces[0]).transpose(1, 2, 0, 3)
-    cot_pieces = exchange(cot_pieces)
-
-    order = me ^ jnp.arange(count)
-    branch = jnp.take(jnp.stack(cot_pieces), order, axis=0, mode="clip").transpose(1, 2, 0, 3)
-    branch = branch.reshape(local, frames, width)
-    half = local // 2
-    xs = gather_pos(after(inputs, branch, w_ffn), count)
-
-    parts = []
-
-    def beside_grads(step, blocks):
-        if 1 <= step <= CHUNKS:
-            first = after(xs[0], *blocks[step], *blocks[ring - step])
-            parts.append(
-                attention(idx, [first] + xs[1:], w_qkv, gain1, live_rows, step - 1, CHUNKS)
-            )
-        return []
-
-    grads = ring_gather([branch[:half], branch[half:]], steps, ring, beside_grads)
-    qkvs = [p[0] for p in parts]
-    resids = [p[1] for p in parts]
-    mixeds = [exchange(p[2:]) for p in parts]
-    hidden, *norm = project(idx, mixeds, resids, w_out, gain2)
-
-    far = ring // 2
+    distance = me ^ jnp.arange(count)
+
+    def in_order(blocks):
+        return jnp.take(blocks, distance, axis=0, mode="clip")
+
+    cots = order.exchange(order.run(split_cot, idx, cotangent, live_rows, count))
+    w_ffn = order.fuse(lambda w: w.transpose(1, 2, 0, 3), weight_ffn)
+
+    def assemble(first, *rest):
+        rows = in_order(jnp.stack([first, *rest])).transpose(1, 2, 0, 3)
+        return rows.reshape(local, frames, width)
+
+    branch = order.fuse(assemble, *cots)
+    grads = RingGather(order, ring, branch)
+    grads.step(1)
+
+    xs = {0: inputs}
+    bit = count // 2
+    while bit:
+        for j in list(xs):
+            xs[j ^ bit] = order.swap(xs[j], bit)
+        bit //= 2
+    xs = [xs[j] for j in range(count)]
+    grads.step(2)
+    qkv, resid, *mixed = order.run(
+        attention, idx, xs, w_qkv, gain1, live_rows, 0, 1, after=grads.received(1)
+    )
+    mixed = order.exchange(mixed)
+    grads.step(3)
+    hidden, norm = order.run(
+        project, idx, [mixed], [resid], w_out, gain2, after=grads.received(2)
+    )
+    norms = RingGather(order, ring, norm)
+    norms.step(1)
+
     groups = [[0]] + [[s, ring - s] for s in range(1, far)] + [[far]]
     dnorms, branches, acts = [None] * ring, [None] * ring, []
 
-    def beside_norms(step, blocks):
-        group = groups[step]
-        norms = [list(blocks[d]) for d in group]
-        if step:
-            norms[0][0] = after(norms[0][0], acts[-1])
-        down, forth, act = ffn(norms, [grads[d] for d in group], w_ffn)
+    def feed(s, after=()):
+        group = groups[s]
+        down, forth, act = order.run(
+            ffn,
+            idx,
+            [norms.blocks[d] for d in group],
+            [grads.blocks[d] for d in group],
+            w_ffn,
+            after=after,
+        )
         for i, d in enumerate(group):
             dnorms[d], branches[d] = down[i], forth[i]
         acts.append(act)
-        return [act]
-
-    norms = ring_gather(norm, steps, ring, beside_norms)
-
-    totals, sets = [], [range(q, min(q + 6, far + 1)) for q in range(0, far + 1, 6)]
-
-    def weights(row, ready):
-        for i, chosen in enumerate(sets):
-            if row == 0:
-                totals.append(None)
-            others = [(grads if row == 2 else norms)[d] for q in chosen for d in groups[q]]
-            mine = [acts[q] for q in chosen]
-            mine[0] = after(mine[0], *ready)
-            totals[i] = weight_grad(mine, others, row, totals[i])
-        return totals
-
-    def beside_low(step, ready):
-        return weights(step - 1, ready) if 1 <= step <= 3 else []
-
-    recv, tie = ring_sum(dnorms, steps, ring, beside_low)
-    for d in (far, far - 1, far + 1):
-        branches[d] = [after(b, recv[1], recv[2]) for b in branches[d]]
-    recv[0] = after(recv[0], *tie)
-    low, gsum, *rest = resid_grad(idx, recv, dnorms[0], hidden, branch, gain2, w_out)
-    dms = exchange(rest[:count])
-    dhs = exchange([rest[count]] + [after(v, *dms) for v in rest[count + 1 :]])
-
-    backs = []
-
-    def beside_block(step, ready):
-        if 1 <= step <= CHUNKS:
-            c = step - 1
-            first = after(dms[0], *ready)
-            backs.append(
-                attention_back(
-                    idx, xs, [first] + dms[1:], qkvs[c], w_qkv, gain1, live_rows, c, CHUNKS
-                )
+
+    feed(0, after=grads.received(3))
+    for s in range(4, far + 1):
+        grads.step(s)
+    for s in range(2, far + 1):
+        norms.step(s)
+        feed(s - 1)
+
+    totals = {}
+
+    def weights(row):
+        for q in range(0, far + 1, 6):
+            chosen = range(q, min(q + 6, far + 1))
+            source = (grads if row == 2 else norms).blocks
+            totals[q] = order.run(
+                weight_grad,
+                idx,
+                [acts[i] for i in chosen],
+                [source[d] for i in chosen for d in groups[i]],
+                row,
+                totals.get(q),
             )
-            return backs[-1][:1]
-        return []
-
-    recv, _ = ring_sum(branches, steps, ring, beside_block)
-    rows = block_rows(idx, recv, branches[0], hidden, live_own, count)
-    block_out = gather_block(idx, exchange(rows))
-
-    grad_in, qkv_part, gain_part = [], 0.0, 0.0
-    for c in range(CHUNKS):
-        keep, send, qkv_c, gain_c = backs[c]
-        qkv_part = qkv_part + qkv_c
-        gain_part = gain_part + gain_c
-        terms = [keep, swap(send, count, 1)]
-        bit = 1
-        while bit < count // 2:
-            total = sum(t.astype(f32) for t in terms).astype(bf16)
-            index = [i for i in range(total.shape[0]) if i & 1]
-            going = jnp.stack([total[i] for i in index])
-            stay = [i for i in range(total.shape[0]) if not i & 1]
-            terms = [jnp.stack([t[i] for i in stay]) for t in terms]
-            terms.append(swap(going, count, 2 * bit))
-            bit *= 2
-        grad_in.append(input_grad(idx, xs, dhs, terms, gain1, c, CHUNKS))
-    grad_in = jnp.concatenate(grad_in, 0)
-
-    ffn_grad = totals[0]
-    for term in totals[1:]:
-        ffn_grad = ffn_grad + term
-    ffn_grad = ffn_grad.transpose(0, 2, 1, 3)
-
-    mixed_all = [jnp.concatenate([m[j] for m in mixeds], 1) for j in range(count)]
-    out_part = jnp.stack(
-        [
-            jnp.einsum("kfd,kfe->de", m, low, preferred_element_type=f32).astype(bf16)
-            for m in mixed_all
-        ]
+
+    dnorm = RingSum(order, ring, dnorms, idx)
+    forth = RingSumWhole(order, ring, branches, idx)
+    dnorm.step("y", 1)
+    feed(far)
+    dnorm.step("x", 1)
+    for s in range(2, far):
+        dnorm.step("y", s)
+        dnorm.step("x", s)
+    dnorm.step("x", far)
+    forth.step(1)
+
+    low, gsum, *rest = order.run(
+        resid_grad, idx, dnorm.received(), dnorms[0], hidden, branch, gain2, w_out
     )
-    out_part = after(out_part, *dms)
     bits = [1 << i for i in range((count - 1).bit_length())]
+
+    dms = order.exchange(rest[:count])
+    *stay, going = order.run(out_terms, idx, [mixed], low)
+    weights(0)
+
+    def out_sum(stay, moved):
+        shape = (2, part // 2, width)
+        mine = [v.reshape(shape) for v in stay]
+        moved = [moved[i].reshape(shape) for i in range(len(stay))]
+        return [v.reshape(part, width) for v in order.run(merge, idx, mine, moved)]
+
+    rows = width // ring
+
+    def pack(out, gsum):
+        columns = gsum.reshape(local, ring, rows).transpose(1, 0, 2).reshape(ring, 1, local * rows)
+        columns = jnp.pad(columns, ((0, 0), (0, 0), (0, -(local * rows) % width)))
+        pieces = [out.reshape(ring, part // ring, width), columns.reshape(ring, -1, width)]
+        return jnp.concatenate([p.astype(bf16) for p in pieces], 1)
+
+    forth.step(2, after=dms)
+    dhs = order.exchange(rest[count:])
+    keep, send, qkv_low, gain_sum = order.run(
+        attention_back, idx, xs, dms, qkv, w_qkv, gain1, live_rows, ring
+    )
+    forth.step(3, after=dhs)
+    out_moved = order.swap(going, 1)
+    sums = [keep, order.swap(send, 1)]
+    outs = out_sum(stay, out_moved)
+    for bit in bits[1:]:
+        out_moved = order.swap(jnp.stack(outs[1::2]), bit)
+        if bit == 2:
+            weights(1)
+        sums.append(order.swap(order.run(fold, idx, sums, bit), bit))
+        outs = out_sum(outs[0::2], out_moved)
+    packed = order.fuse(pack, outs[0], gsum)
+    packed = lax.all_to_all(packed, "frames", 0, 0, tiled=True)
+    for s in range(4, far + 1):
+        forth.step(s)
+    weights(2)
+    block = order.run(block_rows, idx, forth.parts, branches[0], hidden, live_own, count)
+    block = order.exchange(block)
+    packed = order.fuse(lambda m: jnp.sum(m.astype(f32), axis=0), packed)
+    out_low = packed[: part // ring].astype(bf16)
+    gain_ffn_grad = packed[part // ring :].reshape(-1)[: local * rows]
+
+    def both(a, b):
+        return jnp.concatenate([a, b], 0)
+
+    def unmix(blocks, axis, bits):
+        have = [0]
+        for bit in bits:
+            have = have + [j ^ bit for j in have]
+        inverse = jnp.array([have.index(j) for j in range(len(have))])
+        places = jnp.take(inverse, lax.axis_index(axis) ^ jnp.arange(len(have)), mode="clip")
+        return jnp.take(blocks, places, axis=0, mode="clip")
+
+    def join(a, b, c, d):
+        return both(a, c), b + d
+
+    def both_ways(out, gain, axis, bit):
+        nearby = order.swap(out, bit, axis), order.swap(gain, bit, axis)
+        return order.fuse(join, out, gain, *nearby)
+
     ring_bits = [1 << i for i in range((ring - 1).bit_length())]
-    out_low = scatter_halves(out_part, bits, "pos")
-    ring_order = lax.axis_index("frames") ^ jnp.arange(ring)
-    out_low = out_low.astype(bf16).reshape(ring, part // ring, width)
-    out_low = jnp.take(out_low, ring_order, axis=0, mode="clip")
-    out_low = scatter_halves(out_low, ring_bits, "frames")
-    out_grad = gather_doubles(out_low.astype(bf16), ring, ring_bits, "frames")
-    out_grad = gather_doubles(out_grad, count, bits[::-1], "pos")
-    out_grad = out_grad.reshape(width, width).astype(f32)
-    rows = width // ring
-    qkv_rows = qkv_part.reshape(3, ring, rows, part).transpose(1, 0, 2, 3)
-    packed = [
-        qkv_rows.reshape(ring, 3 * rows, part),
-        jnp.broadcast_to(gain_part.reshape(1, count, part), (ring, count, part)),
-    ]
-    columns = gsum.reshape(local, ring, rows).transpose(1, 0, 2).reshape(ring, local * rows)
-    lines = -(-local * rows // part)
-    columns = jnp.pad(columns, ((0, 0), (0, lines * part - local * rows)))
-    packed.append(columns.reshape(ring, lines, part))
-    packed = jnp.concatenate([p.astype(bf16) for p in packed], 1)
-    moved = lax.all_to_all(packed, "frames", 0, 0, tiled=True)
-    moved = jnp.sum(moved.astype(f32), axis=0)
-    qkv_grad = moved[: 3 * rows].reshape(3, rows, part)
-    gain_attn_grad = sum_axis(moved[3 * rows : 3 * rows + count], count, "pos").reshape(width)
-    gain_ffn_grad = moved[3 * rows + count :].reshape(-1)[: local * rows].reshape(local, rows)
+    out_low = out_low[None]
+    for i, bit in enumerate(ring_bits):
+        nearby = order.swap(out_low, bit, "frames"), order.swap(gain_sum, bit, "frames")
+        if i == 0:
+            grad_in = order.run(input_grad, idx, xs, dhs, sums, gain1, 0, 1)
+        if i == 1:
+            block_out = order.run(gather_block, idx, block)
+        out_low, gain_sum = order.fuse(join, out_low, gain_sum, *nearby)
+    moved = lax.all_to_all(order.tie(qkv_low), "frames", 0, 0, tiled=True)
+    out_low = unmix(out_low, "frames", ring_bits)[None]
+    for bit in bits[::-1]:
+        out_low, gain_sum = both_ways(out_low, gain_sum, "pos", bit)
+    qkv_grad = order.fuse(lambda m: jnp.sum(m.astype(f32), axis=0), moved).reshape(3, rows, part)
+    out_grad = unmix(out_low, "pos", bits[::-1]).reshape(width, width).astype(f32)
+    gain_attn_grad = gain_sum
+
+    ffn_grad = None
+    for term in totals.values():
+        ffn_grad = term if ffn_grad is None else ffn_grad + term
     return (
         block_out,
         grad_in,
-        gain_attn_grad,
+        gain_attn_grad.reshape(width),
         qkv_grad.transpose(1, 0, 2),
         out_grad,
-        gain_ffn_grad,
-        ffn_grad,
+        gain_ffn_grad.reshape(local, rows),
+        ffn_grad.transpose(0, 2, 1, 3),
     )
 
 

time: 603 us -> 509 us (0.84)
  the two profiles are of different devices: /device:TPU:10 before, /device:TPU:0 now
where the time goes in v3:
time: 509 us; the launch traced here: 500 us
  Pallas kernels  206 us (40%)
  waiting for transfers between devices  172 us (34%)
  starting transfers between devices  72.1 us (14%)
  local copies, waits for them, and re-layouts  39.5 us (8%)
  other arithmetic  9.11 us (2%)
    ppermute x70, waiting for transfers between devices, send(): return lax.ppermute(self.tie(value), axis, pairs)  153 us
    ppermute x70, starting transfers between devices, send(): return lax.ppermute(self.tie(value), axis, pairs)  63.7 us
    pallas_call x5, Pallas kernels, ffn(): pl.pallas_call(functools.partial(ffn_kernel, [len(v) for v in blocks]), g...  61.7 us
    pallas_call x3, Pallas kernels, weight_grad(): pl.pallas_call(kernel, grid_spec=pltpu.PrefetchScalarGridSpec(num_scalar_...  38.3 us
    pallas_call x1, Pallas kernels, attention_back(): pl.pallas_call(functools.partial(attn_back_kernel, count, ring), grid_spe...  23.4 us
    unnamed x143, local copies, waits for them, and re-layouts  17.8 us
    pallas_call x1, Pallas kernels, attention(): pl.pallas_call(functools.partial(attn_kernel, count), grid_spec=pltpu.Pre...  17.3 us
    pallas_call x7, Pallas kernels, merge(): pl.pallas_call(functools.partial(merge_kernel, n), grid_spec=pltpu.Prefet...  16.2 us
  transfers between devices with their start and end apart: 72, of which 33 were waited for; matrix products, arithmetic and copies ran while one was open for 5% of the time, Pallas kernels for 38%

profile of v3, /device:TPU:0, one launch (start us, length us, event | category | flops | bytes accessed | tf_op | source)
XLA Modules:
  0.0 500.1 jit_solution(18294435985401505716)
XLA Ops:
  2.3 2.8 shard_map.153
  8.1 13.2 %copy.29 = bf16[512,4,3,1024]{3,0,2,1:T(8,128)(2,1)} copy(bf16[512,4,3,1024]{3,1,2,0:T(4,128)(2,1)} %param.16) | data formatting | bytes 25165824 | tf_op jit(solution)/shard_map/optimization_barrier | solution.py:851
  26.5 21.8 %collective-permute-done.6.refs_2_ = bf16[128,16,256]{2,1,0:T(8,128)(2,1)S(1)} collective-permute-done((bf16[128,16,256]{2,1,0:T(8,128)(2,1)S(1)}, bf16[128,16,256]{2,1,0:T(8,128)(2,1)S(1)}, u32[]{:S(2)}, u32[]{:S(2)}) %collective-permute-start.6) | collective-permute-done | bytes 1048608 | tf_op jit(solution)/shard_map/ppermute | solution.py:867
  52.8 17.3 %shard_map.154 = (bf16[3,2048,256]{2,1,0:T(8,128)(2,1)}, bf16[4,4,128,256]{3,2,1,0:T(8,128)(2,1)}, bf16[4,128,256]{2,1,0:T(8,128)(2,1)}, bf16[4,128,256]{2,1,0:T...) custom-call(s32[1]{0:T(128)} %bitcast.idx_ref, bf16[128,16,256]{2,1,0:T(8,128)(2,1)} %refs_0_.5, ...), custom_call_target="tpu_custom_call" | custom-call | flops 920000 | bytes 800 | tf_op jit(solution)/shard_map/pallas_call | solution.py:211
  76.0 2.9 collective-permute-done.12.refs_3_
  78.9 4.7 collective-permute-done.11.refs_2_
  84.4 5.7 %shard_map.155 = (f32[4,128,1024]{2,1,0:T(8,128)}, bf16[4,128,1024]{2,1,0:T(8,128)(2,1)}) custom-call(s32[1]{0:T(128)} %bitcast.idx_ref, bf16[4,128,256]{2,1,0:T(8,128)(2,1)} %get-tuple-element.227.refs_0_, bf16[4,128,256]{2,1,0:T(8,128)(2,1)} %copy-done.29, bf16[4,128,256]{2,1,0:T(8,128)(2,1)} %copy-done.28, bf16[4,128,256]{2,1,0:T(8,128)(2,1)} %copy-done.27, ...), custom_call_target="tpu_custom_call" | custom-call | flops 690000 | bytes 600 | tf_op jit(solution)/shard_map/pallas_call | solution.py:281
  92.1 8.1 %collective-permute-done.14.refs_3_.refs_11_ = bf16[4,128,1024]{2,1,0:T(8,128)(2,1)S(1)} collective-permute-done((bf16[4,128,1024]{2,1,0:T(8,128)(2,1)}, bf16[4,128,1024]{2,1,0:T(8,128)(2,1)S(1)}, u32[]{:S(2)}, u32[]{:S(2)}) %collective-permute-start.14) | collective-permute-done | bytes 1048608 | tf_op jit(solution)/shard_map/ppermute | solution.py:867
  101.7 11.2 %shard_map.156 = (bf16[2,128,1024]{2,1,0:T(8,128)(2,1)}, bf16[2,128,1024]{2,1,0:T(8,128)(2,1)}, bf16[4,128,1024]{2,1,0:T(8,128)(2,1)}, bf16[4,3,128,512]{3,2,1,0:T(8,128)(2,1)}) custom-call(s32[1]{0:T(128)} %bitcast.idx_ref, bf16[4,128,1024]{2,1,0:T(8,128)(2,1)} %get-tuple-element.245.refs_0_.refs_5_, bf16[4,128,1024]{2,1,0:T(8,128)(2,1)} %bitcast.60, ...), custom_call_target="tpu_custom_call" | custom-call | flops 977500 | bytes 850 | tf_op jit(solution)/shard_map/pallas_call | solution.py:351
  113.0 7.4 %collective-permute-done.16.refs_1_.refs_7_ = bf16[4,128,1024]{2,1,0:T(8,128)(2,1)S(1)} collective-permute-done((bf16[4,128,1024]{2,1,0:T(8,128)(2,1)}, bf16[4,128,1024]{2,1,0:T(8,128)(2,1)S(1)}, u32[]{:S(2)}, u32[]{:S(2)}) %collective-permute-start.16) | collective-permute-done | bytes 1048608 | tf_op jit(solution)/shard_map/ppermute | solution.py:867
  122.8 13.1 %shard_map.157 = (bf16[2,128,1024]{2,1,0:T(8,128)(2,1)}, bf16[2,128,1024]{2,1,0:T(8,128)(2,1)}, bf16[2,128,1024]{2,1,0:T(8,128)(2,1)}, bf16[2,128,1024]{2,1,0:T(...) custom-call(s32[1]{0:T(128)} %bitcast.idx_ref, ...), custom_call_target="tpu_custom_call" | custom-call | flops 1552500 | bytes 1350 | tf_op jit(solution)/shard_map/pallas_call | solution.py:351
  135.9 7.7 %collective-permute-done.18.refs_1_.refs_9_ = bf16[4,128,1024]{2,1,0:T(8,128)(2,1)S(1)} collective-permute-done((bf16[4,128,1024]{2,1,0:T(8,128)(2,1)S(1)}, bf16[4,128,1024]{2,1,0:T(8,128)(2,1)S(1)}, u32[]{:S(2)}, u32[]{:S(2)}) %collective-permute-start.18) | collective-permute-done | bytes 1048608 | tf_op jit(solution)/shard_map/ppermute | solution.py:867
  148.1 13.1 %shard_map.158 = (bf16[2,128,1024]{2,1,0:T(8,128)(2,1)}, bf16[2,128,1024]{2,1,0:T(8,128)(2,1)}, bf16[2,128,1024]{2,1,0:T(8,128)(2,1)}, bf16[2,128,1024]{2,1,0:T(...) custom-call(s32[1]{0:T(128)} %bitcast.idx_ref, ...), custom_call_target="tpu_custom_call" | custom-call | flops 1552500 | bytes 1350 | tf_op jit(solution)/shard_map/pallas_call | solution.py:351
  161.2 8.5 %collective-permute-done.20.refs_1_.refs_11_ = bf16[4,128,1024]{2,1,0:T(8,128)(2,1)S(1)} collective-permute-done((bf16[4,128,1024]{2,1,0:T(8,128)(2,1)S(1)}, bf16[4,128,1024]{2,1,0:T(8,128)(2,1)S(1)}, u32[]{:S(2)}, u32[]{:S(2)}) %collective-permute-start.20) | collective-permute-done | bytes 1048608 | tf_op jit(solution)/shard_map/ppermute | solution.py:867
  172.3 13.2 %shard_map.159 = (bf16[2,128,1024]{2,1,0:T(8,128)(2,1)}, bf16[2,128,1024]{2,1,0:T(8,128)(2,1)}, bf16[2,128,1024]{2,1,0:T(8,128)(2,1)}, bf16[2,128,1024]{2,1,0:T(...) custom-call(s32[1]{0:T(128)} %bitcast.idx_ref, ...), custom_call_target="tpu_custom_call" | custom-call | flops 1552500 | bytes 1350 | tf_op jit(solution)/shard_map/pallas_call | solution.py:351
  187.6 4.7 collective-permute-done.22.refs_1_.refs_13_
  194.6 11.0 %shard_map.160 = (bf16[2,128,1024]{2,1,0:T(8,128)(2,1)}, bf16[2,128,1024]{2,1,0:T(8,128)(2,1)}, bf16[4,128,1024]{2,1,0:T(8,128)(2,1)}, bf16[4,3,128,512]{3,2,1,0:T(8,128)(2,1)}) custom-call(s32[1]{0:T(128)} %bitcast.idx_ref, bf16[2,128,1024]{2,1,0:T(8,128)(2,1)} %copy-done.16, bf16[2,128,1024]{2,1,0:T(8,128)(2,1)} %copy-done.15, ...), custom_call_target="tpu_custom_call" | custom-call | flops 977500 | bytes 850 | tf_op jit(solution)/shard_map/pallas_call | solution.py:351
  213.0 7.7 %collective-permute-done.28.refs_3_ = bf16[2,128,1024]{2,1,0:T(8,128)(2,1)S(1)} collective-permute-done((bf16[2,128,1024]{2,1,0:T(8,128)(2,1)}, bf16[2,128,1024]{2,1,0:T(8,128)(2,1)S(1)}, u32[]{:S(2)}, u32[]{:S(2)}) %collective-permute-start.28) | collective-permute-done | bytes 524320 | tf_op jit(solution)/shard_map/ppermute | solution.py:867
  232.2 5.5 %collective-permute-done.32.refs_3_ = bf16[2,128,1024]{2,1,0:T(8,128)(2,1)S(1)} collective-permute-done((bf16[2,128,1024]{2,1,0:T(8,128)(2,1)}, bf16[2,128,1024]{2,1,0:T(8,128)(2,1)S(1)}, u32[]{:S(2)}, u32[]{:S(2)}) %collective-permute-start.32) | collective-permute-done | bytes 524320 | tf_op jit(solution)/shard_map/ppermute | solution.py:867
  240.3 2.4 shard_map.164
  247.1 10.3 %collective-permute-done.34.refs_3_ = bf16[2,128,1024]{2,1,0:T(8,128)(2,1)S(1)} collective-permute-done((bf16[2,128,1024]{2,1,0:T(8,128)(2,1)}, bf16[2,128,1024]{2,1,0:T(8,128)(2,1)S(1)}, u32[]{:S(2)}, u32[]{:S(2)}) %collective-permute-start.34) | collective-permute-done | bytes 524320 | tf_op jit(solution)/shard_map/ppermute | solution.py:867
  257.4 2.6 collective-permute-done.33.refs_2_
  265.3 3.2 collective-permute-done.37.refs_2_
  271.2 3.4 collective-permute-done.38.refs_3_
  277.7 8.1 %shard_map.166 = (bf16[4,128,1024]{2,1,0:T(8,128)(2,1)}, f32[4,1,1024]{2,1,0:T(1,128)}, bf16[4,128,256]{2,1,0:T(8,128)(2,1)}, bf16[4,128,256]{2,1,0:T(8,128)(2,1...) custom-call(s32[1]{0:T(128)} %bitcast.idx_ref, ...), custom_call_target="tpu_custom_call" | custom-call | flops 920000 | bytes 800 | tf_op jit(solution)/shard_map/pallas_call | solution.py:520
  287.8 3.8 shard_map.167
  291.6 12.8 %shard_map.168.refs_14_ = f32[512,3,4,1024]{3,2,1,0:T(4,128)} custom-call(s32[1]{0:T(128)} %bitcast.idx_ref, bf16[4,3,128,512]{3,2,1,0:T(8,128)(2,1)} %get-tuple-element.307.refs_0_, bf16[4,3,256,512]{3,2,1,0:T(8,128)(2,1)} %get-tuple-element.308.refs_1_, bf16[4,3,256,512]{3,2,1,0:T(8,128)(2,1)} %get-tuple-element.309.refs_2_, ...), custom_call_target="tpu_custom_call" | custom-call | flops 1380000 | bytes 1200 | tf_op jit(solution)/shard_map/pallas_call | solution.py:416
  305.5 4.1 shard_map.169
  313.5 23.4 %shard_map.170 = (bf16[2,2112,256]{2,1,0:T(8,128)(2,1)}, bf16[2,2112,256]{2,1,0:T(8,128)(2,1)}, bf16[8,384,256]{2,1,0:T(8,128)(2,1)}, f32[4,1,256]{2,1,0:T(1,128)}) custom-call(s32[1]{0:T(128)} %bitcast.idx_ref, bf16[128,16,256]{2,1,0:T(8,128)(2,1)} %refs_0_.5, bf16[128,16,256]{2,1,0:T(8,128)(2,1)} %copy-done.10, bf16[128,16,256]{2,1,0:T(8,128)(2,1)} %copy-done.9, ...), custom_call_target="tpu_custom_call" | custom-call | flops 2990000 | bytes 2600 | tf_op jit(solution)/shard_map/pallas_call | solution.py:630
  338.4 4.4 shard_map.171
  345.6 2.8 collective-permute-done.49
  352.8 12.8 %shard_map.173.refs_14_ = f32[512,3,4,1024]{3,2,1,0:T(4,128)} custom-call(s32[1]{0:T(128)} %bitcast.idx_ref, bf16[4,3,128,512]{3,2,1,0:T(8,128)(2,1)} %get-tuple-element.307.refs_0_, bf16[4,3,256,512]{3,2,1,0:T(8,128)(2,1)} %get-tuple-element.308.refs_1_, bf16[4,3,256,512]{3,2,1,0:T(8,128)(2,1)} %get-tuple-element.309.refs_2_, ...), custom_call_target="tpu_custom_call", output_to_operand_aliasing={{}: (15, {})} | custom-call | flops 1380000 | bytes 1200 | tf_op jit(solution)/shard_map/pallas_call | solution.py:416
  366.9 2.8 shard_map.174
  375.8 4.3 shard_map.176
  382.1 4.2 all-to-all-start
  387.7 12.8 %shard_map.177 = f32[512,3,4,1024]{3,2,1,0:T(4,128)} custom-call(s32[1]{0:T(128)} %bitcast.idx_ref, bf16[4,3,128,512]{3,2,1,0:T(8,128)(2,1)} %get-tuple-element.307.refs_0_, bf16[4,3,256,512]{3,2,1,0:T(8,128)(2,1)} %get-tuple-element.308.refs_1_, bf16[4,3,256,512]{3,2,1,0:T(8,128)(2,1)} %get-tuple-element.309.refs_2_, ...), custom_call_target="tpu_custom_call", output_to_operand_aliasing={{}: (15, {})} | custom-call | flops 1380000 | bytes 1200 | tf_op jit(solution)/shard_map/pallas_call | solution.py:416
  400.4 7.3 %collective-permute-done.55.refs_1_ = bf16[4,128,1024]{2,1,0:T(8,128)(2,1)} collective-permute-done((bf16[4,128,1024]{2,1,0:T(8,128)(2,1)}, bf16[4,128,1024]{2,1,0:T(8,128)(2,1)}, u32[]{:S(2)}, u32[]{:S(2)}) %collective-permute-start.55) | collective-permute-done | bytes 1048608 | tf_op jit(solution)/shard_map/ppermute | solution.py:867
  408.0 4.4 shard_map.178
  412.4 7.0 %all-to-all-done = bf16[8,33,1024]{2,1,0:T(8,128)(2,1)S(1)} async-done(((bf16[8,33,1024]{2,1,0:T(8,128)(2,1)}), bf16[8,33,1024]{2,1,0:T(8,128)(2,1)S(1)}, u32[]{:S(2)}, u32[]{:S(2)}) %all-to-all-start) | async-done | bytes 540704 | tf_op jit(solution)/shard_map/all_to_all | solution.py:1102
  419.6 3.3 collective-permute-start.56
  424.8 5.9 %shard_map.179 = bf16[128,16,256]{2,1,0:T(8,128)(2,1)} custom-call(s32[1]{0:T(128)} %bitcast.idx_ref, bf16[128,16,256]{2,1,0:T(8,128)(2,1)} %refs_0_.5, bf16[128,16,256]{2,1,0:T(8,128)(2,1)} %copy-done.10, bf16[128,16,256]{2,1,0:T(8,128)(2,1)} %copy-done.9, bf16[128,16,256]{2,1,0:T(8,128)(2,1)} %copy-done.11, ...), custom_call_target="tpu_custom_call" | custom-call | flops 460000 | bytes 400 | tf_op jit(solution)/shard_map/pallas_call | solution.py:767
  432.9 2.6 collective-permute-done.60.refs_2_
  436.9 2.5 shard_map.180
  442.4 12.9 %collective-permute-done.65 = f32[4,1,256]{2,1,0:T(1,128)S(1)} collective-permute-done((f32[4,1,256]{2,1,0:T(1,128)S(1)}, f32[4,1,256]{2,1,0:T(1,128)S(1)}, u32[]{:S(2)}, u32[]{:S(2)}) %collective-permute-start.65) | collective-permute-done | bytes 4128 | tf_op jit(solution)/shard_map/ppermute | solution.py:867
  455.4 4.3 all-to-all-start.1
  463.7 12.0 %collective-permute-done.67 = f32[4,1,256]{2,1,0:T(1,128)S(1)} collective-permute-done((f32[4,1,256]{2,1,0:T(1,128)S(1)}, f32[4,1,256]{2,1,0:T(1,128)S(1)}, u32[]{:S(2)}, u32[]{:S(2)}) %collective-permute-start.67) | collective-permute-done | bytes 4128 | tf_op jit(solution)/shard_map/ppermute | solution.py:867
  482.9 2.6 bitcast_convert_fusion
  485.5 11.7 %all-to-all-done.1 = bf16[8,384,256]{2,1,0:T(8,128)(2,1)} async-done(((bf16[8,384,256]{2,1,0:T(8,128)(2,1)}), bf16[8,384,256]{2,1,0:T(8,128)(2,1)}, u32[]{:S(2)}, u32[]{:S(2)}) %all-to-all-start.1) | async-done | bytes 1572896 | tf_op jit(solution)/shard_map/all_to_all | solution.py:1139
  (312 shorter events, 123.9 us)
Async XLA Ops:
  5.0 16.3 %collective-permute-start.2 = (bf16[4,128,256]{2,1,0:T(8,128)(2,1)}, bf16[4,128,256]{2,1,0:T(8,128)(2,1)S(1)}, u32[]{:S(2)}, u32[]{:S(2)}) collective-permute-start(bf16[4,128,256]{2,1,0:T(8,128)(2,1)} %get-tuple-element.217), channel_id=1, source_target_pairs={{0,3},{1,2},{2,1},{3,0},{4,7},{5,6},{6,5},{7,4},{8,11},{9,10},{10,... | collective-permute-start | bytes 786440 | tf_op jit(solution)/shard_map/ppermute | solution.py:867
  22.8 25.5 %collective-permute-start.6 = (bf16[128,16,256]{2,1,0:T(8,128)(2,1)S(1)}, bf16[128,16,256]{2,1,0:T(8,128)(2,1)S(1)}, u32[]{:S(2)}, u32[]{:S(2)}) collective-permute-start(bf16[128,16,256]{2,1,0:T(8,128)(2,1)S(1)} %copy-done.8), channel_id=1, source_target_pairs={{0,2},{1,3},{2,0},{3,1},{4,6},{5,7},{6,4},{7,5},{8,10},{9,11},{10,... | collective-permute-start | bytes 3145736 | tf_op jit(solution)/shard_map/ppermute | solution.py:867
  24.5 24.9 %collective-permute-start.4 = (bf16[4,128,1024]{2,1,0:T(8,128)(2,1)S(1)}, bf16[4,128,1024]{2,1,0:T(8,128)(2,1)S(1)}, u32[]{:S(2)}, u32[]{:S(2)}) collective-permute-start(bf16[4,128,1024]{2,1,0:T(8,128)(2,1)S(1)} %bitcast.58), channel_id=1, source_target_pairs={{8,0},{16,8},{24,16},{28,24},{20,28},{12,20},{4,12},{0,4},{9,1},{1... | collective-permute-start | bytes 3145736 | tf_op jit(solution)/shard_map/ppermute | solution.py:867
  26.0 24.9 %collective-permute-start.3 = (bf16[4,128,1024]{2,1,0:T(8,128)(2,1)S(1)}, bf16[4,128,1024]{2,1,0:T(8,128)(2,1)}, u32[]{:S(2)}, u32[]{:S(2)}) collective-permute-start(bf16[4,128,1024]{2,1,0:T(8,128)(2,1)S(1)} %bitcast.59), channel_id=1, source_target_pairs={{0,8},{8,16},{16,24},{24,28},{28,20},{20,12},{12,4},{4,0},{1,9},{9... | collective-permute-start | bytes 3145736 | tf_op jit(solution)/shard_map/ppermute | solution.py:867
  26.5 24.9 %collective-permute-start.5 = (bf16[128,16,256]{2,1,0:T(8,128)(2,1)S(1)}, bf16[128,16,256]{2,1,0:T(8,128)(2,1)S(1)}, u32[]{:S(2)}, u32[]{:S(2)}) collective-permute-start(bf16[128,16,256]{2,1,0:T(8,128)(2,1)S(1)} %copy-done.8), channel_id=1, source_target_pairs={{0,1},{1,0},{2,3},{3,2},{4,5},{5,4},{6,7},{7,6},{8,9},{9,8},{10,11... | collective-permute-start | bytes 3145736 | tf_op jit(solution)/shard_map/ppermute | solution.py:867
  49.4 24.6 %collective-permute-start.9 = (bf16[4,128,1024]{2,1,0:T(8,128)(2,1)S(1)}, bf16[4,128,1024]{2,1,0:T(8,128)(2,1)}, u32[]{:S(2)}, u32[]{:S(2)}) collective-permute-start(bf16[4,128,1024]{2,1,0:T(8,128)(2,1)S(1)} %collective-permute-done.4.refs_3_.refs_7_), channel_id=1, source_target_pairs={{8,0},{16,8},{24,16},{28,24},{20,28},{12,20},{4,12},{0,4},{9,1},{1... | collective-permute-start | bytes 3145736 | tf_op jit(solution)/shard_map/ppermute | solution.py:867
  50.9 24.6 %collective-permute-start.8 = (bf16[4,128,1024]{2,1,0:T(8,128)(2,1)}, bf16[4,128,1024]{2,1,0:T(8,128)(2,1)}, u32[]{:S(2)}, u32[]{:S(2)}) collective-permute-start(bf16[4,128,1024]{2,1,0:T(8,128)(2,1)} %collective-permute-done.3.refs_2_.refs_6_), channel_id=1, source_target_pairs={{0,8},{8,16},{16,24},{24,28},{28,20},{20,12},{12,4},{4,0},{1,9},{9... | collective-permute-start | bytes 3145736 | tf_op jit(solution)/shard_map/ppermute | solution.py:867
  73.9 26.3 %collective-permute-start.14 = (bf16[4,128,1024]{2,1,0:T(8,128)(2,1)}, bf16[4,128,1024]{2,1,0:T(8,128)(2,1)S(1)}, u32[]{:S(2)}, u32[]{:S(2)}) collective-permute-start(bf16[4,128,1024]{2,1,0:T(8,128)(2,1)} %collective-permute-done.9.refs_3_.refs_9_), channel_id=1, source_target_pairs={{8,0},{16,8},{24,16},{28,24},{20,28},{12,20},{4,12},{0,4},{9,1},{1... | collective-permute-start | bytes 3145736 | tf_op jit(solution)/shard_map/ppermute | solution.py:867
  75.4 26.3 %collective-permute-start.13 = (bf16[4,128,1024]{2,1,0:T(8,128)(2,1)}, bf16[4,128,1024]{2,1,0:T(8,128)(2,1)S(1)}, u32[]{:S(2)}, u32[]{:S(2)}) collective-permute-start(bf16[4,128,1024]{2,1,0:T(8,128)(2,1)} %collective-permute-done.8.refs_2_.refs_8_), channel_id=1, source_target_pairs={{0,8},{8,16},{16,24},{24,28},{28,20},{20,12},{12,4},{4,0},{1,9},{9... | collective-permute-start | bytes 3145736 | tf_op jit(solution)/shard_map/ppermute | solution.py:867
  90.1 30.2 %collective-permute-start.16 = (bf16[4,128,1024]{2,1,0:T(8,128)(2,1)}, bf16[4,128,1024]{2,1,0:T(8,128)(2,1)S(1)}, u32[]{:S(2)}, u32[]{:S(2)}) collective-permute-start(bf16[4,128,1024]{2,1,0:T(8,128)(2,1)} %get-tuple-element.245.refs_0_.refs_5_), channel_id=1, source_target_pairs={{8,0},{16,8},{24,16},{28,24},{20,28},{12,20},{4,12},{0,4},{9,1},{1... | collective-permute-start | bytes 3145736 | tf_op jit(solution)/shard_map/ppermute | solution.py:867
  91.6 30.3 %collective-permute-start.15 = (bf16[4,128,1024]{2,1,0:T(8,128)(2,1)}, bf16[4,128,1024]{2,1,0:T(8,128)(2,1)S(1)}, u32[]{:S(2)}, u32[]{:S(2)}) collective-permute-start(bf16[4,128,1024]{2,1,0:T(8,128)(2,1)} %get-tuple-element.245.refs_0_.refs_5_), channel_id=1, source_target_pairs={{0,8},{8,16},{16,24},{24,28},{28,20},{20,12},{12,4},{4,0},{1,9},{9... | collective-permute-start | bytes 3145736 | tf_op jit(solution)/shard_map/ppermute | solution.py:867
  120.3 23.3 %collective-permute-start.18 = (bf16[4,128,1024]{2,1,0:T(8,128)(2,1)S(1)}, bf16[4,128,1024]{2,1,0:T(8,128)(2,1)S(1)}, u32[]{:S(2)}, u32[]{:S(2)}) collective-permute-start(bf16[4,128,1024]{2,1,0:T(8,128)(2,1)S(1)} %collective-permute-done.16.refs_1_.refs_7_), channel_id=1, source_target_pairs={{8,0},{16,8},{24,16},{28,24},{20,28},{12,20},{4,12},{0,4},{9,1},{1... | collective-permute-start | bytes 3145736 | tf_op jit(solution)/shard_map/ppermute | solution.py:867
  121.8 23.3 %collective-permute-start.17 = (bf16[4,128,1024]{2,1,0:T(8,128)(2,1)S(1)}, bf16[4,128,1024]{2,1,0:T(8,128)(2,1)S(1)}, u32[]{:S(2)}, u32[]{:S(2)}) collective-permute-start(bf16[4,128,1024]{2,1,0:T(8,128)(2,1)S(1)} %collective-permute-done.15.refs_0_.refs_6_), channel_id=1, source_target_pairs={{0,8},{8,16},{16,24},{24,28},{28,20},{20,12},{12,4},{4,0},{1,9},{9... | collective-permute-start | bytes 3145736 | tf_op jit(solution)/shard_map/ppermute | solution.py:867
  143.7 26.1 %collective-permute-start.20 = (bf16[4,128,1024]{2,1,0:T(8,128)(2,1)S(1)}, bf16[4,128,1024]{2,1,0:T(8,128)(2,1)S(1)}, u32[]{:S(2)}, u32[]{:S(2)}) collective-permute-start(bf16[4,128,1024]{2,1,0:T(8,128)(2,1)S(1)} %collective-permute-done.18.refs_1_.refs_9_), channel_id=1, source_target_pairs={{8,0},{16,8},{24,16},{28,24},{20,28},{12,20},{4,12},{0,4},{9,1},{1... | collective-permute-start | bytes 3145736 | tf_op jit(solution)/shard_map/ppermute | solution.py:867
  145.2 26.2 %collective-permute-start.19 = (bf16[4,128,1024]{2,1,0:T(8,128)(2,1)S(1)}, bf16[4,128,1024]{2,1,0:T(8,128)(2,1)S(1)}, u32[]{:S(2)}, u32[]{:S(2)}) collective-permute-start(bf16[4,128,1024]{2,1,0:T(8,128)(2,1)S(1)} %collective-permute-done.17.refs_0_.refs_8_), channel_id=1, source_target_pairs={{0,8},{8,16},{16,24},{24,28},{28,20},{20,12},{12,4},{4,0},{1,9},{9... | collective-permute-start | bytes 3145736 | tf_op jit(solution)/shard_map/ppermute | solution.py:867
  145.7 41.0 %collective-permute-start.24 = (bf16[2,128,1024]{2,1,0:T(8,128)(2,1)S(1)}, bf16[2,128,1024]{2,1,0:T(8,128)(2,1)S(1)}, u32[]{:S(2)}, u32[]{:S(2)}) collective-permute-start(bf16[2,128,1024]{2,1,0:T(8,128)(2,1)S(1)} %slice.57), channel_id=1, source_target_pairs={{8,0},{16,8},{24,16},{28,24},{20,28},{12,20},{4,12},{0,4},{9,1},{1... | collective-permute-start | bytes 1572872 | tf_op jit(solution)/shard_map/ppermute | solution.py:867
  147.3 40.2 %collective-permute-start.23 = (bf16[2,128,1024]{2,1,0:T(8,128)(2,1)S(1)}, bf16[2,128,1024]{2,1,0:T(8,128)(2,1)S(1)}, u32[]{:S(2)}, u32[]{:S(2)}) collective-permute-start(bf16[2,128,1024]{2,1,0:T(8,128)(2,1)S(1)} %slice.56), channel_id=1, source_target_pairs={{0,8},{8,16},{16,24},{24,28},{28,20},{20,12},{12,4},{4,0},{1,9},{9... | collective-permute-start | bytes 1572872 | tf_op jit(solution)/shard_map/ppermute | solution.py:867
  169.8 22.4 %collective-permute-start.22 = (bf16[2,128,1024]{2,1,0:T(8,128)(2,1)S(1)}, bf16[2,128,1024]{2,1,0:T(8,128)(2,1)S(1)}, u32[]{:S(2)}, u32[]{:S(2)}) collective-permute-start(bf16[2,128,1024]{2,1,0:T(8,128)(2,1)S(1)} %slice.55), channel_id=1, source_target_pairs={{8,0},{16,8},{24,16},{28,24},{20,28},{12,20},{4,12},{0,4},{9,1},{1... | collective-permute-start | bytes 1572872 | tf_op jit(solution)/shard_map/ppermute | solution.py:867
  171.4 22.3 %collective-permute-start.21 = (bf16[2,128,1024]{2,1,0:T(8,128)(2,1)S(1)}, bf16[2,128,1024]{2,1,0:T(8,128)(2,1)S(1)}, u32[]{:S(2)}, u32[]{:S(2)}) collective-permute-start(bf16[2,128,1024]{2,1,0:T(8,128)(2,1)S(1)} %slice.54), channel_id=1, source_target_pairs={{0,8},{8,16},{16,24},{24,28},{28,20},{20,12},{12,4},{4,0},{1,9},{9... | collective-permute-start | bytes 1572872 | tf_op jit(solution)/shard_map/ppermute | solution.py:867
  185.5 22.1 %collective-permute-start.25 = (bf16[2,128,1024]{2,1,0:T(8,128)(2,1)}, bf16[2,128,1024]{2,1,0:T(8,128)(2,1)S(1)}, u32[]{:S(2)}, u32[]{:S(2)}) collective-permute-start(bf16[2,128,1024]{2,1,0:T(8,128)(2,1)} %get-tuple-element.264), channel_id=1, source_target_pairs={{0,8},{8,16},{16,24},{24,28},{28,20},{20,12},{12,4},{4,0},{1,9},{9... | collective-permute-start | bytes 1572872 | tf_op jit(solution)/shard_map/ppermute | solution.py:867
  186.8 20.9 %collective-permute-start.26 = (bf16[2,128,1024]{2,1,0:T(8,128)(2,1)}, bf16[2,128,1024]{2,1,0:T(8,128)(2,1)S(1)}, u32[]{:S(2)}, u32[]{:S(2)}) collective-permute-start(bf16[2,128,1024]{2,1,0:T(8,128)(2,1)} %get-tuple-element.265), channel_id=1, source_target_pairs={{8,0},{16,8},{24,16},{28,24},{20,28},{12,20},{4,12},{0,4},{9,1},{1... | collective-permute-start | bytes 1572872 | tf_op jit(solution)/shard_map/ppermute | solution.py:867
  205.6 15.1 %collective-permute-start.28 = (bf16[2,128,1024]{2,1,0:T(8,128)(2,1)}, bf16[2,128,1024]{2,1,0:T(8,128)(2,1)S(1)}, u32[]{:S(2)}, u32[]{:S(2)}) collective-permute-start(bf16[2,128,1024]{2,1,0:T(8,128)(2,1)} %get-tuple-element.272), channel_id=1, source_target_pairs={{8,0},{16,8},{24,16},{28,24},{20,28},{12,20},{4,12},{0,4},{9,1},{1... | collective-permute-start | bytes 1572872 | tf_op jit(solution)/shard_map/ppermute | solution.py:867
  211.0 16.8 %collective-permute-start.30 = (bf16[2,128,1024]{2,1,0:T(8,128)(2,1)}, bf16[2,128,1024]{2,1,0:T(8,128)(2,1)S(1)}, u32[]{:S(2)}, u32[]{:S(2)}) collective-permute-start(bf16[2,128,1024]{2,1,0:T(8,128)(2,1)} %get-tuple-element.278), channel_id=1, source_target_pairs={{8,0},{16,8},{24,16},{28,24},{20,28},{12,20},{4,12},{0,4},{9,1},{1... | collective-permute-start | bytes 1572872 | tf_op jit(solution)/shard_map/ppermute | solution.py:867
  212.5 16.5 %collective-permute-start.29 = (bf16[2,128,1024]{2,1,0:T(8,128)(2,1)}, bf16[2,128,1024]{2,1,0:T(8,128)(2,1)S(1)}, u32[]{:S(2)}, u32[]{:S(2)}) collective-permute-start(bf16[2,128,1024]{2,1,0:T(8,128)(2,1)} %get-tuple-element.276), channel_id=1, source_target_pairs={{0,8},{8,16},{16,24},{24,28},{28,20},{20,12},{12,4},{4,0},{1,9},{9... | collective-permute-start | bytes 1572872 | tf_op jit(solution)/shard_map/ppermute | solution.py:867
  245.1 14.9 %collective-permute-start.33 = (bf16[2,128,1024]{2,1,0:T(8,128)(2,1)}, bf16[2,128,1024]{2,1,0:T(8,128)(2,1)S(1)}, u32[]{:S(2)}, u32[]{:S(2)}) collective-permute-start(bf16[2,128,1024]{2,1,0:T(8,128)(2,1)} %get-tuple-element.290), channel_id=1, source_target_pairs={{0,8},{8,16},{16,24},{24,28},{28,20},{20,12},{12,4},{4,0},{1,9},{9... | collective-permute-start | bytes 1572872 | tf_op jit(solution)/shard_map/ppermute | solution.py:867
  245.1 23.4 %collective-permute-start.37 = (bf16[2,128,1024]{2,1,0:T(8,128)(2,1)S(1)}, bf16[2,128,1024]{2,1,0:T(8,128)(2,1)S(1)}, u32[]{:S(2)}, u32[]{:S(2)}) collective-permute-start(bf16[2,128,1024]{2,1,0:T(8,128)(2,1)S(1)} %copy-done.64), channel_id=1, source_target_pairs={{8,0},{16,8},{24,16},{28,24},{20,28},{12,20},{4,12},{0,4},{9,1},{1... | collective-permute-start | bytes 1572872 | tf_op jit(solution)/shard_map/ppermute | solution.py:867
  247.1 24.1 %collective-permute-start.36 = (bf16[2,128,1024]{2,1,0:T(8,128)(2,1)S(1)}, bf16[2,128,1024]{2,1,0:T(8,128)(2,1)S(1)}, u32[]{:S(2)}, u32[]{:S(2)}) collective-permute-start(bf16[2,128,1024]{2,1,0:T(8,128)(2,1)S(1)} %copy-done.63), channel_id=1, source_target_pairs={{0,8},{8,16},{16,24},{24,28},{28,20},{20,12},{12,4},{4,0},{1,9},{9... | collective-permute-start | bytes 1572872 | tf_op jit(solution)/shard_map/ppermute | solution.py:867
  265.2 39.3 %collective-permute-start.43 = (bf16[2,128,1024]{2,1,0:T(8,128)(2,1)S(1)}, bf16[2,128,1024]{2,1,0:T(8,128)(2,1)S(1)}, u32[]{:S(2)}, u32[]{:S(2)}) collective-permute-start(bf16[2,128,1024]{2,1,0:T(8,128)(2,1)S(1)} %get-tuple-element.324), channel_id=1, source_target_pairs={{8,0},{16,8},{24,16},{28,24},{20,28},{12,20},{4,12},{0,4},{9,1},{1... | collective-permute-start | bytes 1572872 | tf_op jit(solution)/shard_map/ppermute | solution.py:867
  268.5 36.0 %collective-permute-start.42 = (bf16[2,128,1024]{2,1,0:T(8,128)(2,1)S(1)}, bf16[2,128,1024]{2,1,0:T(8,128)(2,1)S(1)}, u32[]{:S(2)}, u32[]{:S(2)}) collective-permute-start(bf16[2,128,1024]{2,1,0:T(8,128)(2,1)S(1)} %get-tuple-element.323), channel_id=1, source_target_pairs={{0,8},{8,16},{16,24},{24,28},{28,20},{20,12},{12,4},{4,0},{1,9},{9... | collective-permute-start | bytes 1572872 | tf_op jit(solution)/shard_map/ppermute | solution.py:867
  285.9 18.6 %collective-permute-start.41 = (bf16[4,128,256]{2,1,0:T(8,128)(2,1)}, bf16[4,128,256]{2,1,0:T(8,128)(2,1)S(1)}, u32[]{:S(2)}, u32[]{:S(2)}) collective-permute-start(bf16[4,128,256]{2,1,0:T(8,128)(2,1)} %get-tuple-element.318), channel_id=1, source_target_pairs={{0,3},{1,2},{2,1},{3,0},{4,7},{5,6},{6,5},{7,4},{8,11},{9,10},{10,... | collective-permute-start | bytes 786440 | tf_op jit(solution)/shard_map/ppermute | solution.py:867
  285.9 18.5 %collective-permute-start.40 = (bf16[4,128,256]{2,1,0:T(8,128)(2,1)}, bf16[4,128,256]{2,1,0:T(8,128)(2,1)S(1)}, u32[]{:S(2)}, u32[]{:S(2)}) collective-permute-start(bf16[4,128,256]{2,1,0:T(8,128)(2,1)} %get-tuple-element.316), channel_id=1, source_target_pairs={{0,2},{1,3},{2,0},{3,1},{4,6},{5,7},{6,4},{7,5},{8,10},{9,11},{10,... | collective-permute-start | bytes 786440 | tf_op jit(solution)/shard_map/ppermute | solution.py:867
  287.0 17.5 %collective-permute-start.39 = (bf16[4,128,256]{2,1,0:T(8,128)(2,1)}, bf16[4,128,256]{2,1,0:T(8,128)(2,1)S(1)}, u32[]{:S(2)}, u32[]{:S(2)}) collective-permute-start(bf16[4,128,256]{2,1,0:T(8,128)(2,1)} %get-tuple-element.314), channel_id=1, source_target_pairs={{0,1},{1,0},{2,3},{3,2},{4,5},{5,4},{6,7},{7,6},{8,9},{9,8},{10,11... | collective-permute-start | bytes 786440 | tf_op jit(solution)/shard_map/ppermute | solution.py:867
  309.6 27.4 %collective-permute-start.48 = (bf16[4,128,1024]{2,1,0:T(8,128)(2,1)}, bf16[4,128,1024]{2,1,0:T(8,128)(2,1)S(1)}, u32[]{:S(2)}, u32[]{:S(2)}) collective-permute-start(bf16[4,128,1024]{2,1,0:T(8,128)(2,1)} %get-tuple-element.341), channel_id=1, source_target_pairs={{8,0},{16,8},{24,16},{28,24},{20,28},{12,20},{4,12},{0,4},{9,1},{1... | collective-permute-start | bytes 3145736 | tf_op jit(solution)/shard_map/ppermute | solution.py:867
  310.4 26.6 %collective-permute-start.47 = (bf16[4,128,1024]{2,1,0:T(8,128)(2,1)}, bf16[4,128,1024]{2,1,0:T(8,128)(2,1)S(1)}, u32[]{:S(2)}, u32[]{:S(2)}) collective-permute-start(bf16[4,128,1024]{2,1,0:T(8,128)(2,1)} %get-tuple-element.339), channel_id=1, source_target_pairs={{0,8},{8,16},{16,24},{24,28},{28,20},{20,12},{12,4},{4,0},{1,9},{9... | collective-permute-start | bytes 3145736 | tf_op jit(solution)/shard_map/ppermute | solution.py:867
  311.6 25.3 %collective-permute-start.46 = (bf16[4,128,256]{2,1,0:T(8,128)(2,1)S(1)}, bf16[4,128,256]{2,1,0:T(8,128)(2,1)S(1)}, u32[]{:S(2)}, u32[]{:S(2)}) collective-permute-start(bf16[4,128,256]{2,1,0:T(8,128)(2,1)S(1)} %copy-done.67), channel_id=1, source_target_pairs={{0,3},{1,2},{2,1},{3,0},{4,7},{5,6},{6,5},{7,4},{8,11},{9,10},{10,... | collective-permute-start | bytes 786440 | tf_op jit(solution)/shard_map/ppermute | solution.py:867
  311.7 25.3 %collective-permute-start.45 = (bf16[4,128,256]{2,1,0:T(8,128)(2,1)S(1)}, bf16[4,128,256]{2,1,0:T(8,128)(2,1)S(1)}, u32[]{:S(2)}, u32[]{:S(2)}) collective-permute-start(bf16[4,128,256]{2,1,0:T(8,128)(2,1)S(1)} %copy-done.66), channel_id=1, source_target_pairs={{0,2},{1,3},{2,0},{3,1},{4,6},{5,7},{6,4},{7,5},{8,10},{9,11},{10,... | collective-permute-start | bytes 786440 | tf_op jit(solution)/shard_map/ppermute | solution.py:867
  312.7 24.3 %collective-permute-start.44 = (bf16[4,128,256]{2,1,0:T(8,128)(2,1)S(1)}, bf16[4,128,256]{2,1,0:T(8,128)(2,1)S(1)}, u32[]{:S(2)}, u32[]{:S(2)}) collective-permute-start(bf16[4,128,256]{2,1,0:T(8,128)(2,1)S(1)} %copy-done.65), channel_id=1, source_target_pairs={{0,1},{1,0},{2,3},{3,2},{4,5},{5,4},{6,7},{7,6},{8,9},{9,8},{10,11... | collective-permute-start | bytes 786440 | tf_op jit(solution)/shard_map/ppermute | solution.py:867
  342.7 22.8 %collective-permute-start.50 = (bf16[2,2112,256]{2,1,0:T(8,128)(2,1)S(1)}, bf16[2,2112,256]{2,1,0:T(8,128)(2,1)S(1)}, u32[]{:S(2)}, u32[]{:S(2)}) collective-permute-start(bf16[2,2112,256]{2,1,0:T(8,128)(2,1)S(1)} %copy-done.62), channel_id=1, source_target_pairs={{0,1},{1,0},{2,3},{3,2},{4,5},{5,4},{6,7},{7,6},{8,9},{9,8},{10,11... | collective-permute-start | bytes 6488072 | tf_op jit(solution)/shard_map/ppermute | solution.py:867
  343.3 31.2 %collective-permute-start.53 = (bf16[4,128,1024]{2,1,0:T(8,128)(2,1)}, bf16[4,128,1024]{2,1,0:T(8,128)(2,1)S(1)}, u32[]{:S(2)}, u32[]{:S(2)}) collective-permute-start(bf16[4,128,1024]{2,1,0:T(8,128)(2,1)} %get-tuple-element.363), channel_id=1, source_target_pairs={{8,0},{16,8},{24,16},{28,24},{20,28},{12,20},{4,12},{0,4},{9,1},{1... | collective-permute-start | bytes 3145736 | tf_op jit(solution)/shard_map/ppermute | solution.py:867
  344.2 30.3 %collective-permute-start.52 = (bf16[4,128,1024]{2,1,0:T(8,128)(2,1)}, bf16[4,128,1024]{2,1,0:T(8,128)(2,1)S(1)}, u32[]{:S(2)}, u32[]{:S(2)}) collective-permute-start(bf16[4,128,1024]{2,1,0:T(8,128)(2,1)} %get-tuple-element.361), channel_id=1, source_target_pairs={{0,8},{8,16},{16,24},{24,28},{28,20},{20,12},{12,4},{4,0},{1,9},{9... | collective-permute-start | bytes 3145736 | tf_op jit(solution)/shard_map/ppermute | solution.py:867
  351.8 17.9 %collective-permute-start.51 = (bf16[1,256,1024]{2,1,0:T(8,128)(2,1)}, bf16[1,256,1024]{2,1,0:T(8,128)(2,1)S(1)}, u32[]{:S(2)}, u32[]{:S(2)}) collective-permute-start(bf16[1,256,1024]{2,1,0:T(8,128)(2,1)} %bitcast.89), channel_id=1, source_target_pairs={{0,2},{1,3},{2,0},{3,1},{4,6},{5,7},{6,4},{7,5},{8,10},{9,11},{10,... | collective-permute-start | bytes 1572872 | tf_op jit(solution)/shard_map/ppermute | solution.py:867
  380.1 27.6 %collective-permute-start.55 = (bf16[4,128,1024]{2,1,0:T(8,128)(2,1)}, bf16[4,128,1024]{2,1,0:T(8,128)(2,1)}, u32[]{:S(2)}, u32[]{:S(2)}) collective-permute-start(bf16[4,128,1024]{2,1,0:T(8,128)(2,1)} %get-tuple-element.369), channel_id=1, source_target_pairs={{8,0},{16,8},{24,16},{28,24},{20,28},{12,20},{4,12},{0,4},{9,1},{1... | collective-permute-start | bytes 3145736 | tf_op jit(solution)/shard_map/ppermute | solution.py:867
  381.7 26.3 %collective-permute-start.54 = (bf16[4,128,1024]{2,1,0:T(8,128)(2,1)}, bf16[4,128,1024]{2,1,0:T(8,128)(2,1)}, u32[]{:S(2)}, u32[]{:S(2)}) collective-permute-start(bf16[4,128,1024]{2,1,0:T(8,128)(2,1)} %get-tuple-element.367), channel_id=1, source_target_pairs={{0,8},{8,16},{16,24},{24,28},{28,20},{20,12},{12,4},{4,0},{1,9},{9... | collective-permute-start | bytes 3145736 | tf_op jit(solution)/shard_map/ppermute | solution.py:867
  382.1 37.3 %all-to-all-start = ((bf16[8,33,1024]{2,1,0:T(8,128)(2,1)}), bf16[8,33,1024]{2,1,0:T(8,128)(2,1)S(1)}, u32[]{:S(2)}, u32[]{:S(2)}) async-start(bf16[8,33,1024]{2,1,0:T(8,128)(2,1)} %fusion.1), calls=%async_computation | async-start | bytes 1310720 | tf_op jit(solution)/shard_map/all_to_all | solution.py:1102
  386.3 37.1 %collective-permute-start.58 = (bf16[1,2112,256]{2,1,0:T(8,128)(2,1)S(1)}, bf16[1,2112,256]{2,1,0:T(8,128)(2,1)S(1)}, u32[]{:S(2)}, u32[]{:S(2)}) collective-permute-start(bf16[1,2112,256]{2,1,0:T(8,128)(2,1)S(1)} %copy-done.21), channel_id=1, source_target_pairs={{0,2},{1,3},{2,0},{3,1},{4,6},{5,7},{6,4},{7,5},{8,10},{9,11},{10,... | collective-permute-start | bytes 3244040 | tf_op jit(solution)/shard_map/ppermute | solution.py:867
  439.5 15.9 %collective-permute-start.64 = (bf16[4,32,1024]{2,1,0:T(8,128)(2,1)S(1)}, bf16[4,32,1024]{2,1,0:T(8,128)(2,1)S(1)}, u32[]{:S(2)}, u32[]{:S(2)}) collective-permute-start(bf16[4,32,1024]{2,1,0:T(8,128)(2,1)S(1)} %constant_dynamic-update-slice_fusion.2), channel_id=1, source_target_pairs={{0,16},{4,20},{8,24},{12,28},{16,0},{20,4},{24,8},{28,12},{1,17},{... | collective-permute-start | bytes 786440 | tf_op jit(solution)/shard_map/ppermute | solution.py:867
  440.3 15.0 %collective-permute-start.65 = (f32[4,1,256]{2,1,0:T(1,128)S(1)}, f32[4,1,256]{2,1,0:T(1,128)S(1)}, u32[]{:S(2)}, u32[]{:S(2)}) collective-permute-start(f32[4,1,256]{2,1,0:T(1,128)S(1)} %add.22), channel_id=1, source_target_pairs={{0,16},{4,20},{8,24},{12,28},{16,0},{20,4},{24,8},{28,12},{1,17},{... | collective-permute-start | bytes 12296 | tf_op jit(solution)/shard_map/ppermute | solution.py:867
  455.4 41.9 %all-to-all-start.1 = ((bf16[8,384,256]{2,1,0:T(8,128)(2,1)}), bf16[8,384,256]{2,1,0:T(8,128)(2,1)}, u32[]{:S(2)}, u32[]{:S(2)}) async-start(bf16[8,384,256]{2,1,0:T(8,128)(2,1)} %get-tuple-element.411), calls=%async_computation.1 | async-start | bytes 3145728 | tf_op jit(solution)/shard_map/all_to_all | solution.py:1139
  (92 other events, 803.1 us)

commit v4 on v3

--- a/solution.py
+++ b/solution.py
@@ -1094,17 +1094,14 @@
     outs = out_sum(stay, out_moved)
     for bit in bits[1:]:
         out_moved = order.swap(jnp.stack(outs[1::2]), bit)
-        if bit == 2:
-            weights(1)
         sums.append(order.swap(order.run(fold, idx, sums, bit), bit))
         outs = out_sum(outs[0::2], out_moved)
     packed = order.fuse(pack, outs[0], gsum)
     packed = lax.all_to_all(packed, "frames", 0, 0, tiled=True)
+    weights(1)
     for s in range(4, far + 1):
         forth.step(s)
     weights(2)
-    block = order.run(block_rows, idx, forth.parts, branches[0], hidden, live_own, count)
-    block = order.exchange(block)
     packed = order.fuse(lambda m: jnp.sum(m.astype(f32), axis=0), packed)
     out_low = packed[: part // ring].astype(bf16)
     gain_ffn_grad = packed[part // ring :].reshape(-1)[: local * rows]
@@ -1127,16 +1124,20 @@
         nearby = order.swap(out, bit, axis), order.swap(gain, bit, axis)
         return order.fuse(join, out, gain, *nearby)
 
-    ring_bits = [1 << i for i in range((ring - 1).bit_length())]
+    ring_bits = [1 << i for i in range((ring - 1).bit_length())][::-1]
     out_low = out_low[None]
     for i, bit in enumerate(ring_bits):
         nearby = order.swap(out_low, bit, "frames"), order.swap(gain_sum, bit, "frames")
         if i == 0:
+            block = order.run(
+                block_rows, idx, forth.parts, branches[0], hidden, live_own, count
+            )
+            block = order.exchange(block)
+        if i == 1:
             grad_in = order.run(input_grad, idx, xs, dhs, sums, gain1, 0, 1)
-        if i == 1:
-            block_out = order.run(gather_block, idx, block)
         out_low, gain_sum = order.fuse(join, out_low, gain_sum, *nearby)
     moved = lax.all_to_all(order.tie(qkv_low), "frames", 0, 0, tiled=True)
+    block_out = order.run(gather_block, idx, block)
     out_low = unmix(out_low, "frames", ring_bits)[None]
     for bit in bits[::-1]:
         out_low, gain_sum = both_ways(out_low, gain_sum, "pos", bit)

time: 509 us -> 492 us (0.967)
  waiting for transfers between devices: 172 us -> 152 us
    all_to_all x1, waiting for transfers between devices: 11.7 us -> 1.87 us  [body(): moved = lax.all_to_all(order.tie(qkv_low), 'frames', 0, 0, tiled=True)]
    all_to_all x1, waiting for transfers between devices: 7.02 us -> 0.01 us  [body(): packed = lax.all_to_all(packed, 'frames', 0, 0, tiled=True)]
    unnamed x143 -> x151, local copies, waits for them, and re-layouts: 17.8 us -> 18.9 us
  transfers between devices with their start and end apart: 72 -> 72, of which waited for: 33 -> 33; matrix products, arithmetic and copies ran while one was open for 5% -> 5% of each run, Pallas kernels for 38% -> 40%
where the time goes in v4:
time: 492 us; the launch traced here: 483 us
  Pallas kernels  205 us (42%)
  waiting for transfers between devices  152 us (31%)
  starting transfers between devices  73.8 us (15%)
  local copies, waits for them, and re-layouts  40.6 us (8%)
  other arithmetic  9.11 us (2%)
    ppermute x70, waiting for transfers between devices, send(): return lax.ppermute(self.tie(value), axis, pairs)  150 us
    ppermute x70, starting transfers between devices, send(): return lax.ppermute(self.tie(value), axis, pairs)  64.2 us
    pallas_call x5, Pallas kernels, ffn(): pl.pallas_call(functools.partial(ffn_kernel, [len(v) for v in blocks]), g...  61.6 us
    pallas_call x3, Pallas kernels, weight_grad(): pl.pallas_call(kernel, grid_spec=pltpu.PrefetchScalarGridSpec(num_scalar_...  38.4 us
    pallas_call x1, Pallas kernels, attention_back(): pl.pallas_call(functools.partial(attn_back_kernel, count, ring), grid_spe...  23 us
    unnamed x151, local copies, waits for them, and re-layouts  18.9 us
    pallas_call x1, Pallas kernels, attention(): pl.pallas_call(functools.partial(attn_kernel, count), grid_spec=pltpu.Pre...  17.1 us
    pallas_call x7, Pallas kernels, merge(): pl.pallas_call(functools.partial(merge_kernel, n), grid_spec=pltpu.Prefet...  16.2 us
  transfers between devices with their start and end apart: 72, of which 33 were waited for; matrix products, arithmetic and copies ran while one was open for 5% of the time, Pallas kernels for 40%

profile of v4, /device:TPU:0, one launch (start us, length us, event | category | flops | bytes accessed | tf_op | source)
XLA Modules:
  0.0 482.5 jit_solution(15344780758949283762)
XLA Ops:
  2.3 2.8 shard_map.153
  8.1 13.2 %copy.29 = bf16[512,4,3,1024]{3,0,2,1:T(8,128)(2,1)} copy(bf16[512,4,3,1024]{3,1,2,0:T(4,128)(2,1)} %param.16) | data formatting | bytes 25165824 | tf_op jit(solution)/shard_map/optimization_barrier | solution.py:851
  26.5 21.8 %collective-permute-done.6.refs_2_ = bf16[128,16,256]{2,1,0:T(8,128)(2,1)S(1)} collective-permute-done((bf16[128,16,256]{2,1,0:T(8,128)(2,1)S(1)}, bf16[128,16,256]{2,1,0:T(8,128)(2,1)S(1)}, u32[]{:S(2)}, u32[]{:S(2)}) %collective-permute-start.6) | collective-permute-done | bytes 1048608 | tf_op jit(solution)/shard_map/ppermute | solution.py:867
  52.8 17.1 %shard_map.154 = (bf16[3,2048,256]{2,1,0:T(8,128)(2,1)}, bf16[4,4,128,256]{3,2,1,0:T(8,128)(2,1)}, bf16[4,128,256]{2,1,0:T(8,128)(2,1)}, bf16[4,128,256]{2,1,0:T...) custom-call(s32[1]{0:T(128)} %bitcast.idx_ref, bf16[128,16,256]{2,1,0:T(8,128)(2,1)} %refs_0_.5, ...), custom_call_target="tpu_custom_call" | custom-call | flops 920000 | bytes 800 | tf_op jit(solution)/shard_map/pallas_call | solution.py:211
  76.0 2.7 collective-permute-done.12.refs_3_
  78.7 4.7 collective-permute-done.11.refs_2_
  84.3 5.7 %shard_map.155 = (f32[4,128,1024]{2,1,0:T(8,128)}, bf16[4,128,1024]{2,1,0:T(8,128)(2,1)}) custom-call(s32[1]{0:T(128)} %bitcast.idx_ref, bf16[4,128,256]{2,1,0:T(8,128)(2,1)} %get-tuple-element.227.refs_0_, bf16[4,128,256]{2,1,0:T(8,128)(2,1)} %copy-done.30, bf16[4,128,256]{2,1,0:T(8,128)(2,1)} %copy-done.29, bf16[4,128,256]{2,1,0:T(8,128)(2,1)} %copy-done.28, ...), custom_call_target="tpu_custom_call" | custom-call | flops 690000 | bytes 600 | tf_op jit(solution)/shard_map/pallas_call | solution.py:281
  92.0 8.3 %collective-permute-done.14.refs_3_.refs_11_ = bf16[4,128,1024]{2,1,0:T(8,128)(2,1)S(1)} collective-permute-done((bf16[4,128,1024]{2,1,0:T(8,128)(2,1)}, bf16[4,128,1024]{2,1,0:T(8,128)(2,1)S(1)}, u32[]{:S(2)}, u32[]{:S(2)}) %collective-permute-start.14) | collective-permute-done | bytes 1048608 | tf_op jit(solution)/shard_map/ppermute | solution.py:867
  101.7 11.3 %shard_map.156 = (bf16[2,128,1024]{2,1,0:T(8,128)(2,1)}, bf16[2,128,1024]{2,1,0:T(8,128)(2,1)}, bf16[4,128,1024]{2,1,0:T(8,128)(2,1)}, bf16[4,3,128,512]{3,2,1,0:T(8,128)(2,1)}) custom-call(s32[1]{0:T(128)} %bitcast.idx_ref, bf16[4,128,1024]{2,1,0:T(8,128)(2,1)} %get-tuple-element.245.refs_0_.refs_5_, bf16[4,128,1024]{2,1,0:T(8,128)(2,1)} %bitcast.60, ...), custom_call_target="tpu_custom_call" | custom-call | flops 977500 | bytes 850 | tf_op jit(solution)/shard_map/pallas_call | solution.py:351
  113.0 7.2 %collective-permute-done.16.refs_1_.refs_7_ = bf16[4,128,1024]{2,1,0:T(8,128)(2,1)S(1)} collective-permute-done((bf16[4,128,1024]{2,1,0:T(8,128)(2,1)}, bf16[4,128,1024]{2,1,0:T(8,128)(2,1)S(1)}, u32[]{:S(2)}, u32[]{:S(2)}) %collective-permute-start.16) | collective-permute-done | bytes 1048608 | tf_op jit(solution)/shard_map/ppermute | solution.py:867
  122.7 13.1 %shard_map.157 = (bf16[2,128,1024]{2,1,0:T(8,128)(2,1)}, bf16[2,128,1024]{2,1,0:T(8,128)(2,1)}, bf16[2,128,1024]{2,1,0:T(8,128)(2,1)}, bf16[2,128,1024]{2,1,0:T(...) custom-call(s32[1]{0:T(128)} %bitcast.idx_ref, ...), custom_call_target="tpu_custom_call" | custom-call | flops 1552500 | bytes 1350 | tf_op jit(solution)/shard_map/pallas_call | solution.py:351
  135.8 7.7 %collective-permute-done.18.refs_1_.refs_9_ = bf16[4,128,1024]{2,1,0:T(8,128)(2,1)S(1)} collective-permute-done((bf16[4,128,1024]{2,1,0:T(8,128)(2,1)S(1)}, bf16[4,128,1024]{2,1,0:T(8,128)(2,1)S(1)}, u32[]{:S(2)}, u32[]{:S(2)}) %collective-permute-start.18) | collective-permute-done | bytes 1048608 | tf_op jit(solution)/shard_map/ppermute | solution.py:867
  147.9 13.1 %shard_map.158 = (bf16[2,128,1024]{2,1,0:T(8,128)(2,1)}, bf16[2,128,1024]{2,1,0:T(8,128)(2,1)}, bf16[2,128,1024]{2,1,0:T(8,128)(2,1)}, bf16[2,128,1024]{2,1,0:T(...) custom-call(s32[1]{0:T(128)} %bitcast.idx_ref, ...), custom_call_target="tpu_custom_call" | custom-call | flops 1552500 | bytes 1350 | tf_op jit(solution)/shard_map/pallas_call | solution.py:351
  161.0 8.6 %collective-permute-done.20.refs_1_.refs_11_ = bf16[4,128,1024]{2,1,0:T(8,128)(2,1)S(1)} collective-permute-done((bf16[4,128,1024]{2,1,0:T(8,128)(2,1)S(1)}, bf16[4,128,1024]{2,1,0:T(8,128)(2,1)S(1)}, u32[]{:S(2)}, u32[]{:S(2)}) %collective-permute-start.20) | collective-permute-done | bytes 1048608 | tf_op jit(solution)/shard_map/ppermute | solution.py:867
  172.2 13.1 %shard_map.159 = (bf16[2,128,1024]{2,1,0:T(8,128)(2,1)}, bf16[2,128,1024]{2,1,0:T(8,128)(2,1)}, bf16[2,128,1024]{2,1,0:T(8,128)(2,1)}, bf16[2,128,1024]{2,1,0:T(...) custom-call(s32[1]{0:T(128)} %bitcast.idx_ref, ...), custom_call_target="tpu_custom_call" | custom-call | flops 1552500 | bytes 1350 | tf_op jit(solution)/shard_map/pallas_call | solution.py:351
  187.4 4.7 collective-permute-done.22.refs_1_.refs_13_
  194.4 11.0 %shard_map.160 = (bf16[2,128,1024]{2,1,0:T(8,128)(2,1)}, bf16[2,128,1024]{2,1,0:T(8,128)(2,1)}, bf16[4,128,1024]{2,1,0:T(8,128)(2,1)}, bf16[4,3,128,512]{3,2,1,0:T(8,128)(2,1)}) custom-call(s32[1]{0:T(128)} %bitcast.idx_ref, bf16[2,128,1024]{2,1,0:T(8,128)(2,1)} %copy-done.17, bf16[2,128,1024]{2,1,0:T(8,128)(2,1)} %copy-done.16, ...), custom_call_target="tpu_custom_call" | custom-call | flops 977500 | bytes 850 | tf_op jit(solution)/shard_map/pallas_call | solution.py:351
  212.8 7.4 %collective-permute-done.28.refs_3_ = bf16[2,128,1024]{2,1,0:T(8,128)(2,1)S(1)} collective-permute-done((bf16[2,128,1024]{2,1,0:T(8,128)(2,1)}, bf16[2,128,1024]{2,1,0:T(8,128)(2,1)S(1)}, u32[]{:S(2)}, u32[]{:S(2)}) %collective-permute-start.28) | collective-permute-done | bytes 524320 | tf_op jit(solution)/shard_map/ppermute | solution.py:867
  231.8 5.5 %collective-permute-done.32.refs_3_ = bf16[2,128,1024]{2,1,0:T(8,128)(2,1)S(1)} collective-permute-done((bf16[2,128,1024]{2,1,0:T(8,128)(2,1)}, bf16[2,128,1024]{2,1,0:T(8,128)(2,1)S(1)}, u32[]{:S(2)}, u32[]{:S(2)}) %collective-permute-start.32) | collective-permute-done | bytes 524320 | tf_op jit(solution)/shard_map/ppermute | solution.py:867
  239.9 2.4 shard_map.164
  246.7 10.3 %collective-permute-done.34.refs_3_ = bf16[2,128,1024]{2,1,0:T(8,128)(2,1)S(1)} collective-permute-done((bf16[2,128,1024]{2,1,0:T(8,128)(2,1)}, bf16[2,128,1024]{2,1,0:T(8,128)(2,1)S(1)}, u32[]{:S(2)}, u32[]{:S(2)}) %collective-permute-start.34) | collective-permute-done | bytes 524320 | tf_op jit(solution)/shard_map/ppermute | solution.py:867
  257.0 2.6 collective-permute-done.33.refs_2_
  265.4 2.8 collective-permute-done.37.refs_2_
  270.8 3.4 collective-permute-done.38.refs_3_
  277.3 8.1 %shard_map.166 = (bf16[4,128,1024]{2,1,0:T(8,128)(2,1)}, f32[4,1,1024]{2,1,0:T(1,128)}, bf16[4,128,256]{2,1,0:T(8,128)(2,1)}, bf16[4,128,256]{2,1,0:T(8,128)(2,1...) custom-call(s32[1]{0:T(128)} %bitcast.idx_ref, ...), custom_call_target="tpu_custom_call" | custom-call | flops 920000 | bytes 800 | tf_op jit(solution)/shard_map/pallas_call | solution.py:520
  287.4 3.8 shard_map.167
  291.2 12.8 %shard_map.168.refs_14_ = f32[512,3,4,1024]{3,2,1,0:T(4,128)} custom-call(s32[1]{0:T(128)} %bitcast.idx_ref, bf16[4,3,128,512]{3,2,1,0:T(8,128)(2,1)} %get-tuple-element.307.refs_0_, bf16[4,3,256,512]{3,2,1,0:T(8,128)(2,1)} %get-tuple-element.308.refs_1_, bf16[4,3,256,512]{3,2,1,0:T(8,128)(2,1)} %get-tuple-element.309.refs_2_, ...), custom_call_target="tpu_custom_call" | custom-call | flops 1380000 | bytes 1200 | tf_op jit(solution)/shard_map/pallas_call | solution.py:416
  305.0 4.1 shard_map.169
  313.0 23.0 %shard_map.170 = (bf16[2,2112,256]{2,1,0:T(8,128)(2,1)}, bf16[2,2112,256]{2,1,0:T(8,128)(2,1)}, bf16[8,384,256]{2,1,0:T(8,128)(2,1)}, f32[4,1,256]{2,1,0:T(1,128)}) custom-call(s32[1]{0:T(128)} %bitcast.idx_ref, bf16[128,16,256]{2,1,0:T(8,128)(2,1)} %refs_0_.5, bf16[128,16,256]{2,1,0:T(8,128)(2,1)} %copy-done.11, bf16[128,16,256]{2,1,0:T(8,128)(2,1)} %copy-done.10, ...), custom_call_target="tpu_custom_call" | custom-call | flops 2990000 | bytes 2600 | tf_op jit(solution)/shard_map/pallas_call | solution.py:630
  337.4 4.4 shard_map.171
  342.4 5.2 %collective-permute-done.49 = bf16[2,256,1024]{2,1,0:T(8,128)(2,1)S(1)} collective-permute-done((bf16[2,256,1024]{2,1,0:T(8,128)(2,1)S(1)}, bf16[2,256,1024]{2,1,0:T(8,128)(2,1)S(1)}, u32[]{:S(2)}, u32[]{:S(2)}) %collective-permute-start.49) | collective-permute-done | bytes 1048608 | tf_op jit(solution)/shard_map/ppermute | solution.py:867
  355.8 2.8 shard_map.173
  358.6 6.6 %collective-permute-done.51 = bf16[1,256,1024]{2,1,0:T(8,128)(2,1)S(1)} collective-permute-done((bf16[1,256,1024]{2,1,0:T(8,128)(2,1)}, bf16[1,256,1024]{2,1,0:T(8,128)(2,1)S(1)}, u32[]{:S(2)}, u32[]{:S(2)}) %collective-permute-start.51) | collective-permute-done | bytes 524320 | tf_op jit(solution)/shard_map/ppermute | solution.py:867
  370.0 4.4 all-to-all-start
  374.5 12.8 %shard_map.175.refs_14_ = f32[512,3,4,1024]{3,2,1,0:T(4,128)} custom-call(s32[1]{0:T(128)} %bitcast.idx_ref, bf16[4,3,128,512]{3,2,1,0:T(8,128)(2,1)} %get-tuple-element.307.refs_0_, bf16[4,3,256,512]{3,2,1,0:T(8,128)(2,1)} %get-tuple-element.308.refs_1_, bf16[4,3,256,512]{3,2,1,0:T(8,128)(2,1)} %get-tuple-element.309.refs_2_, ...), custom_call_target="tpu_custom_call", output_to_operand_aliasing={{}: (15, {})} | custom-call | flops 1380000 | bytes 1200 | tf_op jit(solution)/shard_map/pallas_call | solution.py:416
  388.6 4.3 shard_map.176
  396.4 12.8 %shard_map.177 = f32[512,3,4,1024]{3,2,1,0:T(4,128)} custom-call(s32[1]{0:T(128)} %bitcast.idx_ref, bf16[4,3,128,512]{3,2,1,0:T(8,128)(2,1)} %get-tuple-element.307.refs_0_, bf16[4,3,256,512]{3,2,1,0:T(8,128)(2,1)} %get-tuple-element.308.refs_1_, bf16[4,3,256,512]{3,2,1,0:T(8,128)(2,1)} %get-tuple-element.309.refs_2_, ...), custom_call_target="tpu_custom_call", output_to_operand_aliasing={{}: (15, {})} | custom-call | flops 1380000 | bytes 1200 | tf_op jit(solution)/shard_map/pallas_call | solution.py:416
  409.3 2.9 collective-permute-start.55
  413.0 5.2 %collective-permute-done.57.refs_1_ = bf16[4,128,1024]{2,1,0:T(8,128)(2,1)} collective-permute-done((bf16[4,128,1024]{2,1,0:T(8,128)(2,1)}, bf16[4,128,1024]{2,1,0:T(8,128)(2,1)}, u32[]{:S(2)}, u32[]{:S(2)}) %collective-permute-start.57) | collective-permute-done | bytes 1048608 | tf_op jit(solution)/shard_map/ppermute | solution.py:867
  419.0 4.4 shard_map.178
  426.6 5.9 %shard_map.179 = bf16[128,16,256]{2,1,0:T(8,128)(2,1)} custom-call(s32[1]{0:T(128)} %bitcast.idx_ref, bf16[128,16,256]{2,1,0:T(8,128)(2,1)} %refs_0_.5, bf16[128,16,256]{2,1,0:T(8,128)(2,1)} %copy-done.11, bf16[128,16,256]{2,1,0:T(8,128)(2,1)} %copy-done.10, bf16[128,16,256]{2,1,0:T(8,128)(2,1)} %copy-done.12, ...), custom_call_target="tpu_custom_call" | custom-call | flops 460000 | bytes 400 | tf_op jit(solution)/shard_map/pallas_call | solution.py:767
  432.5 2.5 collective-permute-start.61
  437.0 2.4 collective-permute-done.62
  439.5 5.2 %all-to-all-start.1 = ((bf16[8,384,256]{2,1,0:T(8,128)(2,1)}), bf16[8,384,256]{2,1,0:T(8,128)(2,1)}, u32[]{:S(2)}, u32[]{:S(2)}) async-start(bf16[8,384,256]{2,1,0:T(8,128)(2,1)} %get-tuple-element.411), calls=%async_computation.1 | async-start | bytes 3145728 | tf_op jit(solution)/shard_map/all_to_all | solution.py:1139
  446.0 3.0 collective-permute-done.64.refs_2_
  450.4 2.5 shard_map.180
  455.6 12.4 %collective-permute-done.67 = f32[4,1,256]{2,1,0:T(1,128)S(1)} collective-permute-done((f32[4,1,256]{2,1,0:T(1,128)S(1)}, f32[4,1,256]{2,1,0:T(1,128)S(1)}, u32[]{:S(2)}, u32[]{:S(2)}) %collective-permute-start.67) | collective-permute-done | bytes 4128 | tf_op jit(solution)/shard_map/ppermute | solution.py:867
  475.2 2.6 bitcast_convert_fusion
  (319 shorter events, 126.0 us)
Async XLA Ops:
  5.0 16.3 %collective-permute-start.2 = (bf16[4,128,256]{2,1,0:T(8,128)(2,1)}, bf16[4,128,256]{2,1,0:T(8,128)(2,1)S(1)}, u32[]{:S(2)}, u32[]{:S(2)}) collective-permute-start(bf16[4,128,256]{2,1,0:T(8,128)(2,1)} %get-tuple-element.217), channel_id=1, source_target_pairs={{0,3},{1,2},{2,1},{3,0},{4,7},{5,6},{6,5},{7,4},{8,11},{9,10},{10,... | collective-permute-start | bytes 786440 | tf_op jit(solution)/shard_map/ppermute | solution.py:867
  22.8 25.5 %collective-permute-start.6 = (bf16[128,16,256]{2,1,0:T(8,128)(2,1)S(1)}, bf16[128,16,256]{2,1,0:T(8,128)(2,1)S(1)}, u32[]{:S(2)}, u32[]{:S(2)}) collective-permute-start(bf16[128,16,256]{2,1,0:T(8,128)(2,1)S(1)} %copy-done.9), channel_id=1, source_target_pairs={{0,2},{1,3},{2,0},{3,1},{4,6},{5,7},{6,4},{7,5},{8,10},{9,11},{10,... | collective-permute-start | bytes 3145736 | tf_op jit(solution)/shard_map/ppermute | solution.py:867
  24.5 24.9 %collective-permute-start.4 = (bf16[4,128,1024]{2,1,0:T(8,128)(2,1)S(1)}, bf16[4,128,1024]{2,1,0:T(8,128)(2,1)S(1)}, u32[]{:S(2)}, u32[]{:S(2)}) collective-permute-start(bf16[4,128,1024]{2,1,0:T(8,128)(2,1)S(1)} %bitcast.58), channel_id=1, source_target_pairs={{8,0},{16,8},{24,16},{28,24},{20,28},{12,20},{4,12},{0,4},{9,1},{1... | collective-permute-start | bytes 3145736 | tf_op jit(solution)/shard_map/ppermute | solution.py:867
  26.0 24.9 %collective-permute-start.3 = (bf16[4,128,1024]{2,1,0:T(8,128)(2,1)S(1)}, bf16[4,128,1024]{2,1,0:T(8,128)(2,1)}, u32[]{:S(2)}, u32[]{:S(2)}) collective-permute-start(bf16[4,128,1024]{2,1,0:T(8,128)(2,1)S(1)} %bitcast.59), channel_id=1, source_target_pairs={{0,8},{8,16},{16,24},{24,28},{28,20},{20,12},{12,4},{4,0},{1,9},{9... | collective-permute-start | bytes 3145736 | tf_op jit(solution)/shard_map/ppermute | solution.py:867
  26.5 24.9 %collective-permute-start.5 = (bf16[128,16,256]{2,1,0:T(8,128)(2,1)S(1)}, bf16[128,16,256]{2,1,0:T(8,128)(2,1)S(1)}, u32[]{:S(2)}, u32[]{:S(2)}) collective-permute-start(bf16[128,16,256]{2,1,0:T(8,128)(2,1)S(1)} %copy-done.9), channel_id=1, source_target_pairs={{0,1},{1,0},{2,3},{3,2},{4,5},{5,4},{6,7},{7,6},{8,9},{9,8},{10,11... | collective-permute-start | bytes 3145736 | tf_op jit(solution)/shard_map/ppermute | solution.py:867
  49.4 24.6 %collective-permute-start.9 = (bf16[4,128,1024]{2,1,0:T(8,128)(2,1)S(1)}, bf16[4,128,1024]{2,1,0:T(8,128)(2,1)}, u32[]{:S(2)}, u32[]{:S(2)}) collective-permute-start(bf16[4,128,1024]{2,1,0:T(8,128)(2,1)S(1)} %collective-permute-done.4.refs_3_.refs_7_), channel_id=1, source_target_pairs={{8,0},{16,8},{24,16},{28,24},{20,28},{12,20},{4,12},{0,4},{9,1},{1... | collective-permute-start | bytes 3145736 | tf_op jit(solution)/shard_map/ppermute | solution.py:867
  50.9 24.6 %collective-permute-start.8 = (bf16[4,128,1024]{2,1,0:T(8,128)(2,1)}, bf16[4,128,1024]{2,1,0:T(8,128)(2,1)}, u32[]{:S(2)}, u32[]{:S(2)}) collective-permute-start(bf16[4,128,1024]{2,1,0:T(8,128)(2,1)} %collective-permute-done.3.refs_2_.refs_6_), channel_id=1, source_target_pairs={{0,8},{8,16},{16,24},{24,28},{28,20},{20,12},{12,4},{4,0},{1,9},{9... | collective-permute-start | bytes 3145736 | tf_op jit(solution)/shard_map/ppermute | solution.py:867
  73.9 26.3 %collective-permute-start.14 = (bf16[4,128,1024]{2,1,0:T(8,128)(2,1)}, bf16[4,128,1024]{2,1,0:T(8,128)(2,1)S(1)}, u32[]{:S(2)}, u32[]{:S(2)}) collective-permute-start(bf16[4,128,1024]{2,1,0:T(8,128)(2,1)} %collective-permute-done.9.refs_3_.refs_9_), channel_id=1, source_target_pairs={{8,0},{16,8},{24,16},{28,24},{20,28},{12,20},{4,12},{0,4},{9,1},{1... | collective-permute-start | bytes 3145736 | tf_op jit(solution)/shard_map/ppermute | solution.py:867
  75.4 26.3 %collective-permute-start.13 = (bf16[4,128,1024]{2,1,0:T(8,128)(2,1)}, bf16[4,128,1024]{2,1,0:T(8,128)(2,1)S(1)}, u32[]{:S(2)}, u32[]{:S(2)}) collective-permute-start(bf16[4,128,1024]{2,1,0:T(8,128)(2,1)} %collective-permute-done.8.refs_2_.refs_8_), channel_id=1, source_target_pairs={{0,8},{8,16},{16,24},{24,28},{28,20},{20,12},{12,4},{4,0},{1,9},{9... | collective-permute-start | bytes 3145736 | tf_op jit(solution)/shard_map/ppermute | solution.py:867
  90.0 30.2 %collective-permute-start.16 = (bf16[4,128,1024]{2,1,0:T(8,128)(2,1)}, bf16[4,128,1024]{2,1,0:T(8,128)(2,1)S(1)}, u32[]{:S(2)}, u32[]{:S(2)}) collective-permute-start(bf16[4,128,1024]{2,1,0:T(8,128)(2,1)} %get-tuple-element.245.refs_0_.refs_5_), channel_id=1, source_target_pairs={{8,0},{16,8},{24,16},{28,24},{20,28},{12,20},{4,12},{0,4},{9,1},{1... | collective-permute-start | bytes 3145736 | tf_op jit(solution)/shard_map/ppermute | solution.py:867
  91.4 30.3 %collective-permute-start.15 = (bf16[4,128,1024]{2,1,0:T(8,128)(2,1)}, bf16[4,128,1024]{2,1,0:T(8,128)(2,1)S(1)}, u32[]{:S(2)}, u32[]{:S(2)}) collective-permute-start(bf16[4,128,1024]{2,1,0:T(8,128)(2,1)} %get-tuple-element.245.refs_0_.refs_5_), channel_id=1, source_target_pairs={{0,8},{8,16},{16,24},{24,28},{28,20},{20,12},{12,4},{4,0},{1,9},{9... | collective-permute-start | bytes 3145736 | tf_op jit(solution)/shard_map/ppermute | solution.py:867
  120.2 23.3 %collective-permute-start.18 = (bf16[4,128,1024]{2,1,0:T(8,128)(2,1)S(1)}, bf16[4,128,1024]{2,1,0:T(8,128)(2,1)S(1)}, u32[]{:S(2)}, u32[]{:S(2)}) collective-permute-start(bf16[4,128,1024]{2,1,0:T(8,128)(2,1)S(1)} %collective-permute-done.16.refs_1_.refs_7_), channel_id=1, source_target_pairs={{8,0},{16,8},{24,16},{28,24},{20,28},{12,20},{4,12},{0,4},{9,1},{1... | collective-permute-start | bytes 3145736 | tf_op jit(solution)/shard_map/ppermute | solution.py:867
  121.7 23.3 %collective-permute-start.17 = (bf16[4,128,1024]{2,1,0:T(8,128)(2,1)S(1)}, bf16[4,128,1024]{2,1,0:T(8,128)(2,1)S(1)}, u32[]{:S(2)}, u32[]{:S(2)}) collective-permute-start(bf16[4,128,1024]{2,1,0:T(8,128)(2,1)S(1)} %collective-permute-done.15.refs_0_.refs_6_), channel_id=1, source_target_pairs={{0,8},{8,16},{16,24},{24,28},{28,20},{20,12},{12,4},{4,0},{1,9},{9... | collective-permute-start | bytes 3145736 | tf_op jit(solution)/shard_map/ppermute | solution.py:867
  143.5 26.1 %collective-permute-start.20 = (bf16[4,128,1024]{2,1,0:T(8,128)(2,1)S(1)}, bf16[4,128,1024]{2,1,0:T(8,128)(2,1)S(1)}, u32[]{:S(2)}, u32[]{:S(2)}) collective-permute-start(bf16[4,128,1024]{2,1,0:T(8,128)(2,1)S(1)} %collective-permute-done.18.refs_1_.refs_9_), channel_id=1, source_target_pairs={{8,0},{16,8},{24,16},{28,24},{20,28},{12,20},{4,12},{0,4},{9,1},{1... | collective-permute-start | bytes 3145736 | tf_op jit(solution)/shard_map/ppermute | solution.py:867
  145.0 26.2 %collective-permute-start.19 = (bf16[4,128,1024]{2,1,0:T(8,128)(2,1)S(1)}, bf16[4,128,1024]{2,1,0:T(8,128)(2,1)S(1)}, u32[]{:S(2)}, u32[]{:S(2)}) collective-permute-start(bf16[4,128,1024]{2,1,0:T(8,128)(2,1)S(1)} %collective-permute-done.17.refs_0_.refs_8_), channel_id=1, source_target_pairs={{0,8},{8,16},{16,24},{24,28},{28,20},{20,12},{12,4},{4,0},{1,9},{9... | collective-permute-start | bytes 3145736 | tf_op jit(solution)/shard_map/ppermute | solution.py:867
  145.6 41.0 %collective-permute-start.24 = (bf16[2,128,1024]{2,1,0:T(8,128)(2,1)S(1)}, bf16[2,128,1024]{2,1,0:T(8,128)(2,1)S(1)}, u32[]{:S(2)}, u32[]{:S(2)}) collective-permute-start(bf16[2,128,1024]{2,1,0:T(8,128)(2,1)S(1)} %slice.57), channel_id=1, source_target_pairs={{8,0},{16,8},{24,16},{28,24},{20,28},{12,20},{4,12},{0,4},{9,1},{1... | collective-permute-start | bytes 1572872 | tf_op jit(solution)/shard_map/ppermute | solution.py:867
  147.2 40.2 %collective-permute-start.23 = (bf16[2,128,1024]{2,1,0:T(8,128)(2,1)S(1)}, bf16[2,128,1024]{2,1,0:T(8,128)(2,1)S(1)}, u32[]{:S(2)}, u32[]{:S(2)}) collective-permute-start(bf16[2,128,1024]{2,1,0:T(8,128)(2,1)S(1)} %slice.56), channel_id=1, source_target_pairs={{0,8},{8,16},{16,24},{24,28},{28,20},{20,12},{12,4},{4,0},{1,9},{9... | collective-permute-start | bytes 1572872 | tf_op jit(solution)/shard_map/ppermute | solution.py:867
  169.7 22.4 %collective-permute-start.22 = (bf16[2,128,1024]{2,1,0:T(8,128)(2,1)S(1)}, bf16[2,128,1024]{2,1,0:T(8,128)(2,1)S(1)}, u32[]{:S(2)}, u32[]{:S(2)}) collective-permute-start(bf16[2,128,1024]{2,1,0:T(8,128)(2,1)S(1)} %slice.55), channel_id=1, source_target_pairs={{8,0},{16,8},{24,16},{28,24},{20,28},{12,20},{4,12},{0,4},{9,1},{1... | collective-permute-start | bytes 1572872 | tf_op jit(solution)/shard_map/ppermute | solution.py:867
  171.3 22.3 %collective-permute-start.21 = (bf16[2,128,1024]{2,1,0:T(8,128)(2,1)S(1)}, bf16[2,128,1024]{2,1,0:T(8,128)(2,1)S(1)}, u32[]{:S(2)}, u32[]{:S(2)}) collective-permute-start(bf16[2,128,1024]{2,1,0:T(8,128)(2,1)S(1)} %slice.54), channel_id=1, source_target_pairs={{0,8},{8,16},{16,24},{24,28},{28,20},{20,12},{12,4},{4,0},{1,9},{9... | collective-permute-start | bytes 1572872 | tf_op jit(solution)/shard_map/ppermute | solution.py:867
  185.3 22.1 %collective-permute-start.25 = (bf16[2,128,1024]{2,1,0:T(8,128)(2,1)}, bf16[2,128,1024]{2,1,0:T(8,128)(2,1)S(1)}, u32[]{:S(2)}, u32[]{:S(2)}) collective-permute-start(bf16[2,128,1024]{2,1,0:T(8,128)(2,1)} %get-tuple-element.264), channel_id=1, source_target_pairs={{0,8},{8,16},{16,24},{24,28},{28,20},{20,12},{12,4},{4,0},{1,9},{9... | collective-permute-start | bytes 1572872 | tf_op jit(solution)/shard_map/ppermute | solution.py:867
  186.6 20.9 %collective-permute-start.26 = (bf16[2,128,1024]{2,1,0:T(8,128)(2,1)}, bf16[2,128,1024]{2,1,0:T(8,128)(2,1)S(1)}, u32[]{:S(2)}, u32[]{:S(2)}) collective-permute-start(bf16[2,128,1024]{2,1,0:T(8,128)(2,1)} %get-tuple-element.265), channel_id=1, source_target_pairs={{8,0},{16,8},{24,16},{28,24},{20,28},{12,20},{4,12},{0,4},{9,1},{1... | collective-permute-start | bytes 1572872 | tf_op jit(solution)/shard_map/ppermute | solution.py:867
  205.4 14.8 %collective-permute-start.28 = (bf16[2,128,1024]{2,1,0:T(8,128)(2,1)}, bf16[2,128,1024]{2,1,0:T(8,128)(2,1)S(1)}, u32[]{:S(2)}, u32[]{:S(2)}) collective-permute-start(bf16[2,128,1024]{2,1,0:T(8,128)(2,1)} %get-tuple-element.272), channel_id=1, source_target_pairs={{8,0},{16,8},{24,16},{28,24},{20,28},{12,20},{4,12},{0,4},{9,1},{1... | collective-permute-start | bytes 1572872 | tf_op jit(solution)/shard_map/ppermute | solution.py:867
  207.0 14.4 %collective-permute-start.27 = (bf16[2,128,1024]{2,1,0:T(8,128)(2,1)}, bf16[2,128,1024]{2,1,0:T(8,128)(2,1)S(1)}, u32[]{:S(2)}, u32[]{:S(2)}) collective-permute-start(bf16[2,128,1024]{2,1,0:T(8,128)(2,1)} %get-tuple-element.270), channel_id=1, source_target_pairs={{0,8},{8,16},{16,24},{24,28},{28,20},{20,12},{12,4},{4,0},{1,9},{9... | collective-permute-start | bytes 1572872 | tf_op jit(solution)/shard_map/ppermute | solution.py:867
  210.8 16.5 %collective-permute-start.30 = (bf16[2,128,1024]{2,1,0:T(8,128)(2,1)}, bf16[2,128,1024]{2,1,0:T(8,128)(2,1)S(1)}, u32[]{:S(2)}, u32[]{:S(2)}) collective-permute-start(bf16[2,128,1024]{2,1,0:T(8,128)(2,1)} %get-tuple-element.278), channel_id=1, source_target_pairs={{8,0},{16,8},{24,16},{28,24},{20,28},{12,20},{4,12},{0,4},{9,1},{1... | collective-permute-start | bytes 1572872 | tf_op jit(solution)/shard_map/ppermute | solution.py:867
  212.4 16.2 %collective-permute-start.29 = (bf16[2,128,1024]{2,1,0:T(8,128)(2,1)}, bf16[2,128,1024]{2,1,0:T(8,128)(2,1)S(1)}, u32[]{:S(2)}, u32[]{:S(2)}) collective-permute-start(bf16[2,128,1024]{2,1,0:T(8,128)(2,1)} %get-tuple-element.276), channel_id=1, source_target_pairs={{0,8},{8,16},{16,24},{24,28},{28,20},{20,12},{12,4},{4,0},{1,9},{9... | collective-permute-start | bytes 1572872 | tf_op jit(solution)/shard_map/ppermute | solution.py:867
  242.4 14.6 %collective-permute-start.34 = (bf16[2,128,1024]{2,1,0:T(8,128)(2,1)}, bf16[2,128,1024]{2,1,0:T(8,128)(2,1)S(1)}, u32[]{:S(2)}, u32[]{:S(2)}) collective-permute-start(bf16[2,128,1024]{2,1,0:T(8,128)(2,1)} %get-tuple-element.292), channel_id=1, source_target_pairs={{8,0},{16,8},{24,16},{28,24},{20,28},{12,20},{4,12},{0,4},{9,1},{1... | collective-permute-start | bytes 1572872 | tf_op jit(solution)/shard_map/ppermute | solution.py:867
  244.7 14.9 %collective-permute-start.33 = (bf16[2,128,1024]{2,1,0:T(8,128)(2,1)}, bf16[2,128,1024]{2,1,0:T(8,128)(2,1)S(1)}, u32[]{:S(2)}, u32[]{:S(2)}) collective-permute-start(bf16[2,128,1024]{2,1,0:T(8,128)(2,1)} %get-tuple-element.290), channel_id=1, source_target_pairs={{0,8},{8,16},{16,24},{24,28},{28,20},{20,12},{12,4},{4,0},{1,9},{9... | collective-permute-start | bytes 1572872 | tf_op jit(solution)/shard_map/ppermute | solution.py:867
  244.7 23.5 %collective-permute-start.37 = (bf16[2,128,1024]{2,1,0:T(8,128)(2,1)S(1)}, bf16[2,128,1024]{2,1,0:T(8,128)(2,1)S(1)}, u32[]{:S(2)}, u32[]{:S(2)}) collective-permute-start(bf16[2,128,1024]{2,1,0:T(8,128)(2,1)S(1)} %copy-done.66), channel_id=1, source_target_pairs={{8,0},{16,8},{24,16},{28,24},{20,28},{12,20},{4,12},{0,4},{9,1},{1... | collective-permute-start | bytes 1572872 | tf_op jit(solution)/shard_map/ppermute | solution.py:867
  246.7 24.1 %collective-permute-start.36 = (bf16[2,128,1024]{2,1,0:T(8,128)(2,1)S(1)}, bf16[2,128,1024]{2,1,0:T(8,128)(2,1)S(1)}, u32[]{:S(2)}, u32[]{:S(2)}) collective-permute-start(bf16[2,128,1024]{2,1,0:T(8,128)(2,1)S(1)} %copy-done.65), channel_id=1, source_target_pairs={{0,8},{8,16},{16,24},{24,28},{28,20},{20,12},{12,4},{4,0},{1,9},{9... | collective-permute-start | bytes 1572872 | tf_op jit(solution)/shard_map/ppermute | solution.py:867
  264.8 39.2 %collective-permute-start.43 = (bf16[2,128,1024]{2,1,0:T(8,128)(2,1)S(1)}, bf16[2,128,1024]{2,1,0:T(8,128)(2,1)S(1)}, u32[]{:S(2)}, u32[]{:S(2)}) collective-permute-start(bf16[2,128,1024]{2,1,0:T(8,128)(2,1)S(1)} %get-tuple-element.324), channel_id=1, source_target_pairs={{8,0},{16,8},{24,16},{28,24},{20,28},{12,20},{4,12},{0,4},{9,1},{1... | collective-permute-start | bytes 1572872 | tf_op jit(solution)/shard_map/ppermute | solution.py:867
  268.1 35.9 %collective-permute-start.42 = (bf16[2,128,1024]{2,1,0:T(8,128)(2,1)S(1)}, bf16[2,128,1024]{2,1,0:T(8,128)(2,1)S(1)}, u32[]{:S(2)}, u32[]{:S(2)}) collective-permute-start(bf16[2,128,1024]{2,1,0:T(8,128)(2,1)S(1)} %get-tuple-element.323), channel_id=1, source_target_pairs={{0,8},{8,16},{16,24},{24,28},{28,20},{20,12},{12,4},{4,0},{1,9},{9... | collective-permute-start | bytes 1572872 | tf_op jit(solution)/shard_map/ppermute | solution.py:867
  285.4 18.6 %collective-permute-start.41 = (bf16[4,128,256]{2,1,0:T(8,128)(2,1)}, bf16[4,128,256]{2,1,0:T(8,128)(2,1)S(1)}, u32[]{:S(2)}, u32[]{:S(2)}) collective-permute-start(bf16[4,128,256]{2,1,0:T(8,128)(2,1)} %get-tuple-element.318), channel_id=1, source_target_pairs={{0,3},{1,2},{2,1},{3,0},{4,7},{5,6},{6,5},{7,4},{8,11},{9,10},{10,... | collective-permute-start | bytes 786440 | tf_op jit(solution)/shard_map/ppermute | solution.py:867
  285.5 18.5 %collective-permute-start.40 = (bf16[4,128,256]{2,1,0:T(8,128)(2,1)}, bf16[4,128,256]{2,1,0:T(8,128)(2,1)S(1)}, u32[]{:S(2)}, u32[]{:S(2)}) collective-permute-start(bf16[4,128,256]{2,1,0:T(8,128)(2,1)} %get-tuple-element.316), channel_id=1, source_target_pairs={{0,2},{1,3},{2,0},{3,1},{4,6},{5,7},{6,4},{7,5},{8,10},{9,11},{10,... | collective-permute-start | bytes 786440 | tf_op jit(solution)/shard_map/ppermute | solution.py:867
  287.0 17.0 %collective-permute-start.39 = (bf16[4,128,256]{2,1,0:T(8,128)(2,1)}, bf16[4,128,256]{2,1,0:T(8,128)(2,1)S(1)}, u32[]{:S(2)}, u32[]{:S(2)}) collective-permute-start(bf16[4,128,256]{2,1,0:T(8,128)(2,1)} %get-tuple-element.314), channel_id=1, source_target_pairs={{0,1},{1,0},{2,3},{3,2},{4,5},{5,4},{6,7},{7,6},{8,9},{9,8},{10,11... | collective-permute-start | bytes 786440 | tf_op jit(solution)/shard_map/ppermute | solution.py:867
  309.1 26.9 %collective-permute-start.48 = (bf16[4,128,1024]{2,1,0:T(8,128)(2,1)}, bf16[4,128,1024]{2,1,0:T(8,128)(2,1)S(1)}, u32[]{:S(2)}, u32[]{:S(2)}) collective-permute-start(bf16[4,128,1024]{2,1,0:T(8,128)(2,1)} %get-tuple-element.341), channel_id=1, source_target_pairs={{8,0},{16,8},{24,16},{28,24},{20,28},{12,20},{4,12},{0,4},{9,1},{1... | collective-permute-start | bytes 3145736 | tf_op jit(solution)/shard_map/ppermute | solution.py:867
  310.4 25.7 %collective-permute-start.47 = (bf16[4,128,1024]{2,1,0:T(8,128)(2,1)}, bf16[4,128,1024]{2,1,0:T(8,128)(2,1)S(1)}, u32[]{:S(2)}, u32[]{:S(2)}) collective-permute-start(bf16[4,128,1024]{2,1,0:T(8,128)(2,1)} %get-tuple-element.339), channel_id=1, source_target_pairs={{0,8},{8,16},{16,24},{24,28},{28,20},{20,12},{12,4},{4,0},{1,9},{9... | collective-permute-start | bytes 3145736 | tf_op jit(solution)/shard_map/ppermute | solution.py:867
  311.2 24.8 %collective-permute-start.46 = (bf16[4,128,256]{2,1,0:T(8,128)(2,1)S(1)}, bf16[4,128,256]{2,1,0:T(8,128)(2,1)S(1)}, u32[]{:S(2)}, u32[]{:S(2)}) collective-permute-start(bf16[4,128,256]{2,1,0:T(8,128)(2,1)S(1)} %copy-done.71), channel_id=1, source_target_pairs={{0,3},{1,2},{2,1},{3,0},{4,7},{5,6},{6,5},{7,4},{8,11},{9,10},{10,... | collective-permute-start | bytes 786440 | tf_op jit(solution)/shard_map/ppermute | solution.py:867
  311.6 24.4 %collective-permute-start.45 = (bf16[4,128,256]{2,1,0:T(8,128)(2,1)S(1)}, bf16[4,128,256]{2,1,0:T(8,128)(2,1)S(1)}, u32[]{:S(2)}, u32[]{:S(2)}) collective-permute-start(bf16[4,128,256]{2,1,0:T(8,128)(2,1)S(1)} %copy-done.70), channel_id=1, source_target_pairs={{0,2},{1,3},{2,0},{3,1},{4,6},{5,7},{6,4},{7,5},{8,10},{9,11},{10,... | collective-permute-start | bytes 786440 | tf_op jit(solution)/shard_map/ppermute | solution.py:867
  312.6 23.4 %collective-permute-start.44 = (bf16[4,128,256]{2,1,0:T(8,128)(2,1)S(1)}, bf16[4,128,256]{2,1,0:T(8,128)(2,1)S(1)}, u32[]{:S(2)}, u32[]{:S(2)}) collective-permute-start(bf16[4,128,256]{2,1,0:T(8,128)(2,1)S(1)} %copy-done.69), channel_id=1, source_target_pairs={{0,1},{1,0},{2,3},{3,2},{4,5},{5,4},{6,7},{7,6},{8,9},{9,8},{10,11... | collective-permute-start | bytes 786440 | tf_op jit(solution)/shard_map/ppermute | solution.py:867
  351.1 14.2 %collective-permute-start.51 = (bf16[1,256,1024]{2,1,0:T(8,128)(2,1)}, bf16[1,256,1024]{2,1,0:T(8,128)(2,1)S(1)}, u32[]{:S(2)}, u32[]{:S(2)}) collective-permute-start(bf16[1,256,1024]{2,1,0:T(8,128)(2,1)} %bitcast.89), channel_id=1, source_target_pairs={{0,2},{1,3},{2,0},{3,1},{4,6},{5,7},{6,4},{7,5},{8,10},{9,11},{10,... | collective-permute-start | bytes 1572872 | tf_op jit(solution)/shard_map/ppermute | solution.py:867
  352.4 34.9 %collective-permute-start.53 = (bf16[4,128,1024]{2,1,0:T(8,128)(2,1)}, bf16[4,128,1024]{2,1,0:T(8,128)(2,1)S(1)}, u32[]{:S(2)}, u32[]{:S(2)}) collective-permute-start(bf16[4,128,1024]{2,1,0:T(8,128)(2,1)} %get-tuple-element.363), channel_id=1, source_target_pairs={{8,0},{16,8},{24,16},{28,24},{20,28},{12,20},{4,12},{0,4},{9,1},{1... | collective-permute-start | bytes 3145736 | tf_op jit(solution)/shard_map/ppermute | solution.py:867
  354.0 33.3 %collective-permute-start.52 = (bf16[4,128,1024]{2,1,0:T(8,128)(2,1)}, bf16[4,128,1024]{2,1,0:T(8,128)(2,1)S(1)}, u32[]{:S(2)}, u32[]{:S(2)}) collective-permute-start(bf16[4,128,1024]{2,1,0:T(8,128)(2,1)} %get-tuple-element.361), channel_id=1, source_target_pairs={{0,8},{8,16},{16,24},{24,28},{28,20},{20,12},{12,4},{4,0},{1,9},{9... | collective-permute-start | bytes 3145736 | tf_op jit(solution)/shard_map/ppermute | solution.py:867
  370.0 39.2 %all-to-all-start = ((bf16[8,33,1024]{2,1,0:T(8,128)(2,1)}), bf16[8,33,1024]{2,1,0:T(8,128)(2,1)S(1)}, u32[]{:S(2)}, u32[]{:S(2)}) async-start(bf16[8,33,1024]{2,1,0:T(8,128)(2,1)} %fusion.1), calls=%async_computation | async-start | bytes 1310720 | tf_op jit(solution)/shard_map/all_to_all | solution.py:1100
  392.9 25.3 %collective-permute-start.57 = (bf16[4,128,1024]{2,1,0:T(8,128)(2,1)}, bf16[4,128,1024]{2,1,0:T(8,128)(2,1)}, u32[]{:S(2)}, u32[]{:S(2)}) collective-permute-start(bf16[4,128,1024]{2,1,0:T(8,128)(2,1)} %get-tuple-element.372), channel_id=1, source_target_pairs={{8,0},{16,8},{24,16},{28,24},{20,28},{12,20},{4,12},{0,4},{9,1},{1... | collective-permute-start | bytes 3145736 | tf_op jit(solution)/shard_map/ppermute | solution.py:867
  394.9 24.1 %collective-permute-start.56 = (bf16[4,128,1024]{2,1,0:T(8,128)(2,1)}, bf16[4,128,1024]{2,1,0:T(8,128)(2,1)}, u32[]{:S(2)}, u32[]{:S(2)}) collective-permute-start(bf16[4,128,1024]{2,1,0:T(8,128)(2,1)} %get-tuple-element.370), channel_id=1, source_target_pairs={{0,8},{8,16},{16,24},{24,28},{28,20},{20,12},{12,4},{4,0},{1,9},{9... | collective-permute-start | bytes 3145736 | tf_op jit(solution)/shard_map/ppermute | solution.py:867
  395.0 30.6 %collective-permute-start.60 = (bf16[1,2112,256]{2,1,0:T(8,128)(2,1)S(1)}, bf16[1,2112,256]{2,1,0:T(8,128)(2,1)S(1)}, u32[]{:S(2)}, u32[]{:S(2)}) collective-permute-start(bf16[1,2112,256]{2,1,0:T(8,128)(2,1)S(1)} %copy-done.22), channel_id=1, source_target_pairs={{0,2},{1,3},{2,0},{3,1},{4,6},{5,7},{6,4},{7,5},{8,10},{9,11},{10,... | collective-permute-start | bytes 3244040 | tf_op jit(solution)/shard_map/ppermute | solution.py:867
  439.5 40.2 %all-to-all-start.1 = ((bf16[8,384,256]{2,1,0:T(8,128)(2,1)}), bf16[8,384,256]{2,1,0:T(8,128)(2,1)}, u32[]{:S(2)}, u32[]{:S(2)}) async-start(bf16[8,384,256]{2,1,0:T(8,128)(2,1)} %get-tuple-element.411), calls=%async_computation.1 | async-start | bytes 3145728 | tf_op jit(solution)/shard_map/all_to_all | solution.py:1139
  453.5 14.5 %collective-permute-start.66 = (bf16[1,8,32,1024]{3,2,1,0:T(8,128)(2,1)S(1)}, bf16[1,8,32,1024]{3,2,1,0:T(8,128)(2,1)S(1)}, u32[]{:S(2)}, u32[]{:S(2)}) collective-permute-start(bf16[1,8,32,1024]{3,2,1,0:T(8,128)(2,1)S(1)} %bitcast.69), channel_id=1, source_target_pairs={{0,2},{1,3},{2,0},{3,1},{4,6},{5,7},{6,4},{7,5},{8,10},{9,11},{10,... | collective-permute-start | bytes 1572872 | tf_op jit(solution)/shard_map/ppermute | solution.py:867
  (96 other events, 813.1 us)

commit v5 on v4

--- a/solution.py
+++ b/solution.py
@@ -1067,7 +1067,6 @@
 
     dms = order.exchange(rest[:count])
     *stay, going = order.run(out_terms, idx, [mixed], low)
-    weights(0)
 
     def out_sum(stay, moved):
         shape = (2, part // 2, width)
@@ -1128,19 +1127,21 @@
     out_low = out_low[None]
     for i, bit in enumerate(ring_bits):
         nearby = order.swap(out_low, bit, "frames"), order.swap(gain_sum, bit, "frames")
-        if i == 0:
+        if i == 1:
             block = order.run(
                 block_rows, idx, forth.parts, branches[0], hidden, live_own, count
             )
-            block = order.exchange(block)
-        if i == 1:
-            grad_in = order.run(input_grad, idx, xs, dhs, sums, gain1, 0, 1)
         out_low, gain_sum = order.fuse(join, out_low, gain_sum, *nearby)
     moved = lax.all_to_all(order.tie(qkv_low), "frames", 0, 0, tiled=True)
+    block = order.exchange(block)
+    grad_in = order.run(input_grad, idx, xs, dhs, sums, gain1, 0, 1)
     block_out = order.run(gather_block, idx, block)
     out_low = unmix(out_low, "frames", ring_bits)[None]
-    for bit in bits[::-1]:
-        out_low, gain_sum = both_ways(out_low, gain_sum, "pos", bit)
+    for i, bit in enumerate(bits[::-1]):
+        nearby = order.swap(out_low, bit), order.swap(gain_sum, bit)
+        if i == 0:
+            weights(0)
+        out_low, gain_sum = order.fuse(join, out_low, gain_sum, *nearby)
     qkv_grad = order.fuse(lambda m: jnp.sum(m.astype(f32), axis=0), moved).reshape(3, rows, part)
     out_grad = unmix(out_low, "pos", bits[::-1]).reshape(width, width).astype(f32)
     gain_attn_grad = gain_sum

time: 492 us -> 487 us (0.990)
    unnamed x151 -> x139, local copies, waits for them, and re-layouts: 18.9 us -> 17.5 us
  transfers between devices with their start and end apart: 72 -> 72, of which waited for: 33 -> 32; matrix products, arithmetic and copies ran while one was open for 5% -> 5% of each run, Pallas kernels for 40% -> 40%
where the time goes in v5:
time: 487 us; the launch traced here: 478 us
  Pallas kernels  205 us (42%)
  waiting for transfers between devices  152 us (31%)
  starting transfers between devices  70.9 us (15%)
  local copies, waits for them, and re-layouts  39.2 us (8%)
  other arithmetic  9.11 us (2%)
    ppermute x70, waiting for transfers between devices, send(): return lax.ppermute(self.tie(value), axis, pairs)  150 us
    ppermute x70, starting transfers between devices, send(): return lax.ppermute(self.tie(value), axis, pairs)  62.8 us
    pallas_call x5, Pallas kernels, ffn(): pl.pallas_call(functools.partial(ffn_kernel, [len(v) for v in blocks]), g...  61.6 us
    pallas_call x3, Pallas kernels, weight_grad(): pl.pallas_call(kernel, grid_spec=pltpu.PrefetchScalarGridSpec(num_scalar_...  38.4 us
    pallas_call x1, Pallas kernels, attention_back(): pl.pallas_call(functools.partial(attn_back_kernel, count, ring), grid_spe...  23.4 us
    unnamed x139, local copies, waits for them, and re-layouts  17.5 us
    pallas_call x1, Pallas kernels, attention(): pl.pallas_call(functools.partial(attn_kernel, count), grid_spec=pltpu.Pre...  17.3 us
    pallas_call x7, Pallas kernels, merge(): pl.pallas_call(functools.partial(merge_kernel, n), grid_spec=pltpu.Prefet...  16.2 us
  transfers between devices with their start and end apart: 72, of which 32 were waited for; matrix products, arithmetic and copies ran while one was open for 5% of the time, Pallas kernels for 40%

profile of v5, /device:TPU:0, one launch (start us, length us, event | category | flops | bytes accessed | tf_op | source)
XLA Modules:
  0.0 478.0 jit_solution(1329060358476809448)
XLA Ops:
  2.2 2.8 shard_map.153
  8.1 13.2 %copy.29 = bf16[512,4,3,1024]{3,0,2,1:T(8,128)(2,1)} copy(bf16[512,4,3,1024]{3,1,2,0:T(4,128)(2,1)} %param.16) | data formatting | bytes 25165824 | tf_op jit(solution)/shard_map/optimization_barrier | solution.py:851
  26.5 21.8 %collective-permute-done.6.refs_2_ = bf16[128,16,256]{2,1,0:T(8,128)(2,1)S(1)} collective-permute-done((bf16[128,16,256]{2,1,0:T(8,128)(2,1)S(1)}, bf16[128,16,256]{2,1,0:T(8,128)(2,1)S(1)}, u32[]{:S(2)}, u32[]{:S(2)}) %collective-permute-start.6) | collective-permute-done | bytes 1048608 | tf_op jit(solution)/shard_map/ppermute | solution.py:867
  52.7 17.3 %shard_map.154 = (bf16[3,2048,256]{2,1,0:T(8,128)(2,1)}, bf16[4,4,128,256]{3,2,1,0:T(8,128)(2,1)}, bf16[4,128,256]{2,1,0:T(8,128)(2,1)}, bf16[4,128,256]{2,1,0:T...) custom-call(s32[1]{0:T(128)} %bitcast.idx_ref, bf16[128,16,256]{2,1,0:T(8,128)(2,1)} %refs_0_.5, ...), custom_call_target="tpu_custom_call" | custom-call | flops 920000 | bytes 800 | tf_op jit(solution)/shard_map/pallas_call | solution.py:211
  76.0 2.9 collective-permute-done.12.refs_3_
  78.8 4.7 collective-permute-done.11.refs_2_
  84.4 5.7 %shard_map.155 = (f32[4,128,1024]{2,1,0:T(8,128)}, bf16[4,128,1024]{2,1,0:T(8,128)(2,1)}) custom-call(s32[1]{0:T(128)} %bitcast.idx_ref, bf16[4,128,256]{2,1,0:T(8,128)(2,1)} %get-tuple-element.227.refs_0_, bf16[4,128,256]{2,1,0:T(8,128)(2,1)} %copy-done.30, bf16[4,128,256]{2,1,0:T(8,128)(2,1)} %copy-done.29, bf16[4,128,256]{2,1,0:T(8,128)(2,1)} %copy-done.28, ...), custom_call_target="tpu_custom_call" | custom-call | flops 690000 | bytes 600 | tf_op jit(solution)/shard_map/pallas_call | solution.py:281
  92.1 8.1 %collective-permute-done.14.refs_3_.refs_11_ = bf16[4,128,1024]{2,1,0:T(8,128)(2,1)S(1)} collective-permute-done((bf16[4,128,1024]{2,1,0:T(8,128)(2,1)}, bf16[4,128,1024]{2,1,0:T(8,128)(2,1)S(1)}, u32[]{:S(2)}, u32[]{:S(2)}) %collective-permute-start.14) | collective-permute-done | bytes 1048608 | tf_op jit(solution)/shard_map/ppermute | solution.py:867
  101.7 11.3 %shard_map.156 = (bf16[2,128,1024]{2,1,0:T(8,128)(2,1)}, bf16[2,128,1024]{2,1,0:T(8,128)(2,1)}, bf16[4,128,1024]{2,1,0:T(8,128)(2,1)}, bf16[4,3,128,512]{3,2,1,0:T(8,128)(2,1)}) custom-call(s32[1]{0:T(128)} %bitcast.idx_ref, bf16[4,128,1024]{2,1,0:T(8,128)(2,1)} %get-tuple-element.245.refs_0_.refs_5_, bf16[4,128,1024]{2,1,0:T(8,128)(2,1)} %bitcast.60, ...), custom_call_target="tpu_custom_call" | custom-call | flops 977500 | bytes 850 | tf_op jit(solution)/shard_map/pallas_call | solution.py:351
  113.0 7.3 %collective-permute-done.16.refs_1_.refs_7_ = bf16[4,128,1024]{2,1,0:T(8,128)(2,1)S(1)} collective-permute-done((bf16[4,128,1024]{2,1,0:T(8,128)(2,1)}, bf16[4,128,1024]{2,1,0:T(8,128)(2,1)S(1)}, u32[]{:S(2)}, u32[]{:S(2)}) %collective-permute-start.16) | collective-permute-done | bytes 1048608 | tf_op jit(solution)/shard_map/ppermute | solution.py:867
  122.9 13.1 %shard_map.157 = (bf16[2,128,1024]{2,1,0:T(8,128)(2,1)}, bf16[2,128,1024]{2,1,0:T(8,128)(2,1)}, bf16[2,128,1024]{2,1,0:T(8,128)(2,1)}, bf16[2,128,1024]{2,1,0:T(...) custom-call(s32[1]{0:T(128)} %bitcast.idx_ref, ...), custom_call_target="tpu_custom_call" | custom-call | flops 1552500 | bytes 1350 | tf_op jit(solution)/shard_map/pallas_call | solution.py:351
  135.9 7.7 %collective-permute-done.18.refs_1_.refs_9_ = bf16[4,128,1024]{2,1,0:T(8,128)(2,1)S(1)} collective-permute-done((bf16[4,128,1024]{2,1,0:T(8,128)(2,1)S(1)}, bf16[4,128,1024]{2,1,0:T(8,128)(2,1)S(1)}, u32[]{:S(2)}, u32[]{:S(2)}) %collective-permute-start.18) | collective-permute-done | bytes 1048608 | tf_op jit(solution)/shard_map/ppermute | solution.py:867
  148.1 13.2 %shard_map.158 = (bf16[2,128,1024]{2,1,0:T(8,128)(2,1)}, bf16[2,128,1024]{2,1,0:T(8,128)(2,1)}, bf16[2,128,1024]{2,1,0:T(8,128)(2,1)}, bf16[2,128,1024]{2,1,0:T(...) custom-call(s32[1]{0:T(128)} %bitcast.idx_ref, ...), custom_call_target="tpu_custom_call" | custom-call | flops 1552500 | bytes 1350 | tf_op jit(solution)/shard_map/pallas_call | solution.py:351
  161.2 8.5 %collective-permute-done.20.refs_1_.refs_11_ = bf16[4,128,1024]{2,1,0:T(8,128)(2,1)S(1)} collective-permute-done((bf16[4,128,1024]{2,1,0:T(8,128)(2,1)S(1)}, bf16[4,128,1024]{2,1,0:T(8,128)(2,1)S(1)}, u32[]{:S(2)}, u32[]{:S(2)}) %collective-permute-start.20) | collective-permute-done | bytes 1048608 | tf_op jit(solution)/shard_map/ppermute | solution.py:867
  172.4 13.1 %shard_map.159 = (bf16[2,128,1024]{2,1,0:T(8,128)(2,1)}, bf16[2,128,1024]{2,1,0:T(8,128)(2,1)}, bf16[2,128,1024]{2,1,0:T(8,128)(2,1)}, bf16[2,128,1024]{2,1,0:T(...) custom-call(s32[1]{0:T(128)} %bitcast.idx_ref, ...), custom_call_target="tpu_custom_call" | custom-call | flops 1552500 | bytes 1350 | tf_op jit(solution)/shard_map/pallas_call | solution.py:351
  187.5 4.7 collective-permute-done.22.refs_1_.refs_13_
  194.5 11.0 %shard_map.160 = (bf16[2,128,1024]{2,1,0:T(8,128)(2,1)}, bf16[2,128,1024]{2,1,0:T(8,128)(2,1)}, bf16[4,128,1024]{2,1,0:T(8,128)(2,1)}, bf16[4,3,128,512]{3,2,1,0:T(8,128)(2,1)}) custom-call(s32[1]{0:T(128)} %bitcast.idx_ref, bf16[2,128,1024]{2,1,0:T(8,128)(2,1)} %copy-done.17, bf16[2,128,1024]{2,1,0:T(8,128)(2,1)} %copy-done.16, ...), custom_call_target="tpu_custom_call" | custom-call | flops 977500 | bytes 850 | tf_op jit(solution)/shard_map/pallas_call | solution.py:351
  212.9 7.6 %collective-permute-done.28.refs_3_ = bf16[2,128,1024]{2,1,0:T(8,128)(2,1)S(1)} collective-permute-done((bf16[2,128,1024]{2,1,0:T(8,128)(2,1)}, bf16[2,128,1024]{2,1,0:T(8,128)(2,1)S(1)}, u32[]{:S(2)}, u32[]{:S(2)}) %collective-permute-start.28) | collective-permute-done | bytes 524320 | tf_op jit(solution)/shard_map/ppermute | solution.py:867
  232.1 5.5 %collective-permute-done.32.refs_3_ = bf16[2,128,1024]{2,1,0:T(8,128)(2,1)S(1)} collective-permute-done((bf16[2,128,1024]{2,1,0:T(8,128)(2,1)}, bf16[2,128,1024]{2,1,0:T(8,128)(2,1)S(1)}, u32[]{:S(2)}, u32[]{:S(2)}) %collective-permute-start.32) | collective-permute-done | bytes 524320 | tf_op jit(solution)/shard_map/ppermute | solution.py:867
  247.0 10.3 %collective-permute-done.34.refs_3_ = bf16[2,128,1024]{2,1,0:T(8,128)(2,1)S(1)} collective-permute-done((bf16[2,128,1024]{2,1,0:T(8,128)(2,1)}, bf16[2,128,1024]{2,1,0:T(8,128)(2,1)S(1)}, u32[]{:S(2)}, u32[]{:S(2)}) %collective-permute-start.34) | collective-permute-done | bytes 524320 | tf_op jit(solution)/shard_map/ppermute | solution.py:867
  257.3 2.6 collective-permute-done.33.refs_2_
  265.2 3.2 collective-permute-done.37.refs_2_
  268.6 2.5 collective-permute-done.36.refs_1_
  271.1 3.4 collective-permute-done.38.refs_3_
  277.6 8.1 %shard_map.166 = (bf16[4,128,1024]{2,1,0:T(8,128)(2,1)}, f32[4,1,1024]{2,1,0:T(1,128)}, bf16[4,128,256]{2,1,0:T(8,128)(2,1)}, bf16[4,128,256]{2,1,0:T(8,128)(2,1...) custom-call(s32[1]{0:T(128)} %bitcast.idx_ref, ...), custom_call_target="tpu_custom_call" | custom-call | flops 920000 | bytes 800 | tf_op jit(solution)/shard_map/pallas_call | solution.py:520
  287.6 3.8 shard_map.167
  291.4 3.2 collective-permute-done.41.refs_7_
  294.6 4.9 %collective-permute-done.40.refs_6_ = bf16[4,128,256]{2,1,0:T(8,128)(2,1)S(1)} collective-permute-done((bf16[4,128,256]{2,1,0:T(8,128)(2,1)}, bf16[4,128,256]{2,1,0:T(8,128)(2,1)S(1)}, u32[]{:S(2)}, u32[]{:S(2)}) %collective-permute-start.40) | collective-permute-done | bytes 262176 | tf_op jit(solution)/shard_map/ppermute | solution.py:867
  300.5 4.1 shard_map.168
  308.8 23.4 %shard_map.169 = (bf16[2,2112,256]{2,1,0:T(8,128)(2,1)}, bf16[2,2112,256]{2,1,0:T(8,128)(2,1)}, bf16[8,384,256]{2,1,0:T(8,128)(2,1)}, f32[4,1,256]{2,1,0:T(1,128)}) custom-call(s32[1]{0:T(128)} %bitcast.idx_ref, bf16[128,16,256]{2,1,0:T(8,128)(2,1)} %refs_0_.5, bf16[128,16,256]{2,1,0:T(8,128)(2,1)} %copy-done.11, bf16[128,16,256]{2,1,0:T(8,128)(2,1)} %copy-done.10, ...), custom_call_target="tpu_custom_call" | custom-call | flops 2990000 | bytes 2600 | tf_op jit(solution)/shard_map/pallas_call | solution.py:630
  333.6 4.3 shard_map.170
  338.4 4.9 %collective-permute-done.49 = bf16[2,256,1024]{2,1,0:T(8,128)(2,1)S(1)} collective-permute-done((bf16[2,256,1024]{2,1,0:T(8,128)(2,1)S(1)}, bf16[2,256,1024]{2,1,0:T(8,128)(2,1)S(1)}, u32[]{:S(2)}, u32[]{:S(2)}) %collective-permute-start.49) | collective-permute-done | bytes 1048608 | tf_op jit(solution)/shard_map/ppermute | solution.py:867
  351.0 2.8 shard_map.172
  353.8 7.4 %collective-permute-done.51 = bf16[1,256,1024]{2,1,0:T(8,128)(2,1)S(1)} collective-permute-done((bf16[1,256,1024]{2,1,0:T(8,128)(2,1)}, bf16[1,256,1024]{2,1,0:T(8,128)(2,1)S(1)}, u32[]{:S(2)}, u32[]{:S(2)}) %collective-permute-start.51) | collective-permute-done | bytes 524320 | tf_op jit(solution)/shard_map/ppermute | solution.py:867
  366.0 3.5 all-to-all-start
  369.5 12.8 %shard_map.174.refs_14_ = f32[512,3,4,1024]{3,2,1,0:T(4,128)} custom-call(s32[1]{0:T(128)} %bitcast.idx_ref, bf16[4,3,128,512]{3,2,1,0:T(8,128)(2,1)} %get-tuple-element.352.refs_0_, bf16[4,3,256,512]{3,2,1,0:T(8,128)(2,1)} %get-tuple-element.353.refs_1_, bf16[4,3,256,512]{3,2,1,0:T(8,128)(2,1)} %get-tuple-element.354.refs_2_, ...), custom_call_target="tpu_custom_call" | custom-call | flops 1380000 | bytes 1200 | tf_op jit(solution)/shard_map/pallas_call | solution.py:416
  383.7 4.2 shard_map.175
  390.0 12.8 %shard_map.176.refs_14_ = f32[512,3,4,1024]{3,2,1,0:T(4,128)} custom-call(s32[1]{0:T(128)} %bitcast.idx_ref, bf16[4,3,128,512]{3,2,1,0:T(8,128)(2,1)} %get-tuple-element.352.refs_0_, bf16[4,3,256,512]{3,2,1,0:T(8,128)(2,1)} %get-tuple-element.353.refs_1_, bf16[4,3,256,512]{3,2,1,0:T(8,128)(2,1)} %get-tuple-element.354.refs_2_, ...), custom_call_target="tpu_custom_call", output_to_operand_aliasing={{}: (15, {})} | custom-call | flops 1380000 | bytes 1200 | tf_op jit(solution)/shard_map/pallas_call | solution.py:416
  402.9 2.9 collective-permute-start.54
  406.7 10.2 %collective-permute-done.55 = f32[4,1,256]{2,1,0:T(1,128)S(1)} collective-permute-done((f32[4,1,256]{2,1,0:T(1,128)S(1)}, f32[4,1,256]{2,1,0:T(1,128)S(1)}, u32[]{:S(2)}, u32[]{:S(2)}) %collective-permute-start.55) | collective-permute-done | bytes 4128 | tf_op jit(solution)/shard_map/ppermute | solution.py:867
  419.6 4.4 shard_map.177
  424.0 2.8 collective-permute-start.60
  426.8 4.3 collective-permute-done.61
  433.2 4.5 all-to-all-start.1
  440.0 5.9 %shard_map.178 = bf16[128,16,256]{2,1,0:T(8,128)(2,1)} custom-call(s32[1]{0:T(128)} %bitcast.idx_ref, bf16[128,16,256]{2,1,0:T(8,128)(2,1)} %refs_0_.5, bf16[128,16,256]{2,1,0:T(8,128)(2,1)} %copy-done.11, bf16[128,16,256]{2,1,0:T(8,128)(2,1)} %copy-done.10, bf16[128,16,256]{2,1,0:T(8,128)(2,1)} %copy-done.12, ...), custom_call_target="tpu_custom_call" | custom-call | flops 460000 | bytes 400 | tf_op jit(solution)/shard_map/pallas_call | solution.py:767
  446.5 2.5 shard_map.179
  451.1 12.8 %shard_map.180 = f32[512,3,4,1024]{3,2,1,0:T(4,128)} custom-call(s32[1]{0:T(128)} %bitcast.idx_ref, bf16[4,3,128,512]{3,2,1,0:T(8,128)(2,1)} %get-tuple-element.352.refs_0_, bf16[4,3,256,512]{3,2,1,0:T(8,128)(2,1)} %get-tuple-element.353.refs_1_, bf16[4,3,256,512]{3,2,1,0:T(8,128)(2,1)} %get-tuple-element.354.refs_2_, ...), custom_call_target="tpu_custom_call", output_to_operand_aliasing={{}: (15, {})} | custom-call | flops 1380000 | bytes 1200 | tf_op jit(solution)/shard_map/pallas_call | solution.py:416
  471.1 2.6 bitcast_convert_fusion
  (307 shorter events, 121.8 us)
Async XLA Ops:
  5.0 16.3 %collective-permute-start.2 = (bf16[4,128,256]{2,1,0:T(8,128)(2,1)}, bf16[4,128,256]{2,1,0:T(8,128)(2,1)S(1)}, u32[]{:S(2)}, u32[]{:S(2)}) collective-permute-start(bf16[4,128,256]{2,1,0:T(8,128)(2,1)} %get-tuple-element.217), channel_id=1, source_target_pairs={{0,3},{1,2},{2,1},{3,0},{4,7},{5,6},{6,5},{7,4},{8,11},{9,10},{10,... | collective-permute-start | bytes 786440 | tf_op jit(solution)/shard_map/ppermute | solution.py:867
  22.8 25.5 %collective-permute-start.6 = (bf16[128,16,256]{2,1,0:T(8,128)(2,1)S(1)}, bf16[128,16,256]{2,1,0:T(8,128)(2,1)S(1)}, u32[]{:S(2)}, u32[]{:S(2)}) collective-permute-start(bf16[128,16,256]{2,1,0:T(8,128)(2,1)S(1)} %copy-done.9), channel_id=1, source_target_pairs={{0,2},{1,3},{2,0},{3,1},{4,6},{5,7},{6,4},{7,5},{8,10},{9,11},{10,... | collective-permute-start | bytes 3145736 | tf_op jit(solution)/shard_map/ppermute | solution.py:867
  24.5 24.9 %collective-permute-start.4 = (bf16[4,128,1024]{2,1,0:T(8,128)(2,1)S(1)}, bf16[4,128,1024]{2,1,0:T(8,128)(2,1)S(1)}, u32[]{:S(2)}, u32[]{:S(2)}) collective-permute-start(bf16[4,128,1024]{2,1,0:T(8,128)(2,1)S(1)} %bitcast.58), channel_id=1, source_target_pairs={{8,0},{16,8},{24,16},{28,24},{20,28},{12,20},{4,12},{0,4},{9,1},{1... | collective-permute-start | bytes 3145736 | tf_op jit(solution)/shard_map/ppermute | solution.py:867
  26.0 24.9 %collective-permute-start.3 = (bf16[4,128,1024]{2,1,0:T(8,128)(2,1)S(1)}, bf16[4,128,1024]{2,1,0:T(8,128)(2,1)}, u32[]{:S(2)}, u32[]{:S(2)}) collective-permute-start(bf16[4,128,1024]{2,1,0:T(8,128)(2,1)S(1)} %bitcast.59), channel_id=1, source_target_pairs={{0,8},{8,16},{16,24},{24,28},{28,20},{20,12},{12,4},{4,0},{1,9},{9... | collective-permute-start | bytes 3145736 | tf_op jit(solution)/shard_map/ppermute | solution.py:867
  26.5 24.9 %collective-permute-start.5 = (bf16[128,16,256]{2,1,0:T(8,128)(2,1)S(1)}, bf16[128,16,256]{2,1,0:T(8,128)(2,1)S(1)}, u32[]{:S(2)}, u32[]{:S(2)}) collective-permute-start(bf16[128,16,256]{2,1,0:T(8,128)(2,1)S(1)} %copy-done.9), channel_id=1, source_target_pairs={{0,1},{1,0},{2,3},{3,2},{4,5},{5,4},{6,7},{7,6},{8,9},{9,8},{10,11... | collective-permute-start | bytes 3145736 | tf_op jit(solution)/shard_map/ppermute | solution.py:867
  49.4 24.6 %collective-permute-start.9 = (bf16[4,128,1024]{2,1,0:T(8,128)(2,1)S(1)}, bf16[4,128,1024]{2,1,0:T(8,128)(2,1)}, u32[]{:S(2)}, u32[]{:S(2)}) collective-permute-start(bf16[4,128,1024]{2,1,0:T(8,128)(2,1)S(1)} %collective-permute-done.4.refs_3_.refs_7_), channel_id=1, source_target_pairs={{8,0},{16,8},{24,16},{28,24},{20,28},{12,20},{4,12},{0,4},{9,1},{1... | collective-permute-start | bytes 3145736 | tf_op jit(solution)/shard_map/ppermute | solution.py:867
  50.9 24.6 %collective-permute-start.8 = (bf16[4,128,1024]{2,1,0:T(8,128)(2,1)}, bf16[4,128,1024]{2,1,0:T(8,128)(2,1)}, u32[]{:S(2)}, u32[]{:S(2)}) collective-permute-start(bf16[4,128,1024]{2,1,0:T(8,128)(2,1)} %collective-permute-done.3.refs_2_.refs_6_), channel_id=1, source_target_pairs={{0,8},{8,16},{16,24},{24,28},{28,20},{20,12},{12,4},{4,0},{1,9},{9... | collective-permute-start | bytes 3145736 | tf_op jit(solution)/shard_map/ppermute | solution.py:867
  73.9 26.3 %collective-permute-start.14 = (bf16[4,128,1024]{2,1,0:T(8,128)(2,1)}, bf16[4,128,1024]{2,1,0:T(8,128)(2,1)S(1)}, u32[]{:S(2)}, u32[]{:S(2)}) collective-permute-start(bf16[4,128,1024]{2,1,0:T(8,128)(2,1)} %collective-permute-done.9.refs_3_.refs_9_), channel_id=1, source_target_pairs={{8,0},{16,8},{24,16},{28,24},{20,28},{12,20},{4,12},{0,4},{9,1},{1... | collective-permute-start | bytes 3145736 | tf_op jit(solution)/shard_map/ppermute | solution.py:867
  75.4 26.3 %collective-permute-start.13 = (bf16[4,128,1024]{2,1,0:T(8,128)(2,1)}, bf16[4,128,1024]{2,1,0:T(8,128)(2,1)S(1)}, u32[]{:S(2)}, u32[]{:S(2)}) collective-permute-start(bf16[4,128,1024]{2,1,0:T(8,128)(2,1)} %collective-permute-done.8.refs_2_.refs_8_), channel_id=1, source_target_pairs={{0,8},{8,16},{16,24},{24,28},{28,20},{20,12},{12,4},{4,0},{1,9},{9... | collective-permute-start | bytes 3145736 | tf_op jit(solution)/shard_map/ppermute | solution.py:867
  90.1 30.2 %collective-permute-start.16 = (bf16[4,128,1024]{2,1,0:T(8,128)(2,1)}, bf16[4,128,1024]{2,1,0:T(8,128)(2,1)S(1)}, u32[]{:S(2)}, u32[]{:S(2)}) collective-permute-start(bf16[4,128,1024]{2,1,0:T(8,128)(2,1)} %get-tuple-element.245.refs_0_.refs_5_), channel_id=1, source_target_pairs={{8,0},{16,8},{24,16},{28,24},{20,28},{12,20},{4,12},{0,4},{9,1},{1... | collective-permute-start | bytes 3145736 | tf_op jit(solution)/shard_map/ppermute | solution.py:867
  91.6 30.3 %collective-permute-start.15 = (bf16[4,128,1024]{2,1,0:T(8,128)(2,1)}, bf16[4,128,1024]{2,1,0:T(8,128)(2,1)S(1)}, u32[]{:S(2)}, u32[]{:S(2)}) collective-permute-start(bf16[4,128,1024]{2,1,0:T(8,128)(2,1)} %get-tuple-element.245.refs_0_.refs_5_), channel_id=1, source_target_pairs={{0,8},{8,16},{16,24},{24,28},{28,20},{20,12},{12,4},{4,0},{1,9},{9... | collective-permute-start | bytes 3145736 | tf_op jit(solution)/shard_map/ppermute | solution.py:867
  120.3 23.3 %collective-permute-start.18 = (bf16[4,128,1024]{2,1,0:T(8,128)(2,1)S(1)}, bf16[4,128,1024]{2,1,0:T(8,128)(2,1)S(1)}, u32[]{:S(2)}, u32[]{:S(2)}) collective-permute-start(bf16[4,128,1024]{2,1,0:T(8,128)(2,1)S(1)} %collective-permute-done.16.refs_1_.refs_7_), channel_id=1, source_target_pairs={{8,0},{16,8},{24,16},{28,24},{20,28},{12,20},{4,12},{0,4},{9,1},{1... | collective-permute-start | bytes 3145736 | tf_op jit(solution)/shard_map/ppermute | solution.py:867
  121.8 23.3 %collective-permute-start.17 = (bf16[4,128,1024]{2,1,0:T(8,128)(2,1)S(1)}, bf16[4,128,1024]{2,1,0:T(8,128)(2,1)S(1)}, u32[]{:S(2)}, u32[]{:S(2)}) collective-permute-start(bf16[4,128,1024]{2,1,0:T(8,128)(2,1)S(1)} %collective-permute-done.15.refs_0_.refs_6_), channel_id=1, source_target_pairs={{0,8},{8,16},{16,24},{24,28},{28,20},{20,12},{12,4},{4,0},{1,9},{9... | collective-permute-start | bytes 3145736 | tf_op jit(solution)/shard_map/ppermute | solution.py:867
  143.6 26.1 %collective-permute-start.20 = (bf16[4,128,1024]{2,1,0:T(8,128)(2,1)S(1)}, bf16[4,128,1024]{2,1,0:T(8,128)(2,1)S(1)}, u32[]{:S(2)}, u32[]{:S(2)}) collective-permute-start(bf16[4,128,1024]{2,1,0:T(8,128)(2,1)S(1)} %collective-permute-done.18.refs_1_.refs_9_), channel_id=1, source_target_pairs={{8,0},{16,8},{24,16},{28,24},{20,28},{12,20},{4,12},{0,4},{9,1},{1... | collective-permute-start | bytes 3145736 | tf_op jit(solution)/shard_map/ppermute | solution.py:867
  145.1 26.2 %collective-permute-start.19 = (bf16[4,128,1024]{2,1,0:T(8,128)(2,1)S(1)}, bf16[4,128,1024]{2,1,0:T(8,128)(2,1)S(1)}, u32[]{:S(2)}, u32[]{:S(2)}) collective-permute-start(bf16[4,128,1024]{2,1,0:T(8,128)(2,1)S(1)} %collective-permute-done.17.refs_0_.refs_8_), channel_id=1, source_target_pairs={{0,8},{8,16},{16,24},{24,28},{28,20},{20,12},{12,4},{4,0},{1,9},{9... | collective-permute-start | bytes 3145736 | tf_op jit(solution)/shard_map/ppermute | solution.py:867
  145.7 40.9 %collective-permute-start.24 = (bf16[2,128,1024]{2,1,0:T(8,128)(2,1)S(1)}, bf16[2,128,1024]{2,1,0:T(8,128)(2,1)S(1)}, u32[]{:S(2)}, u32[]{:S(2)}) collective-permute-start(bf16[2,128,1024]{2,1,0:T(8,128)(2,1)S(1)} %slice.57), channel_id=1, source_target_pairs={{8,0},{16,8},{24,16},{28,24},{20,28},{12,20},{4,12},{0,4},{9,1},{1... | collective-permute-start | bytes 1572872 | tf_op jit(solution)/shard_map/ppermute | solution.py:867
  147.3 40.2 %collective-permute-start.23 = (bf16[2,128,1024]{2,1,0:T(8,128)(2,1)S(1)}, bf16[2,128,1024]{2,1,0:T(8,128)(2,1)S(1)}, u32[]{:S(2)}, u32[]{:S(2)}) collective-permute-start(bf16[2,128,1024]{2,1,0:T(8,128)(2,1)S(1)} %slice.56), channel_id=1, source_target_pairs={{0,8},{8,16},{16,24},{24,28},{28,20},{20,12},{12,4},{4,0},{1,9},{9... | collective-permute-start | bytes 1572872 | tf_op jit(solution)/shard_map/ppermute | solution.py:867
  169.8 22.4 %collective-permute-start.22 = (bf16[2,128,1024]{2,1,0:T(8,128)(2,1)S(1)}, bf16[2,128,1024]{2,1,0:T(8,128)(2,1)S(1)}, u32[]{:S(2)}, u32[]{:S(2)}) collective-permute-start(bf16[2,128,1024]{2,1,0:T(8,128)(2,1)S(1)} %slice.55), channel_id=1, source_target_pairs={{8,0},{16,8},{24,16},{28,24},{20,28},{12,20},{4,12},{0,4},{9,1},{1... | collective-permute-start | bytes 1572872 | tf_op jit(solution)/shard_map/ppermute | solution.py:867
  171.4 22.3 %collective-permute-start.21 = (bf16[2,128,1024]{2,1,0:T(8,128)(2,1)S(1)}, bf16[2,128,1024]{2,1,0:T(8,128)(2,1)S(1)}, u32[]{:S(2)}, u32[]{:S(2)}) collective-permute-start(bf16[2,128,1024]{2,1,0:T(8,128)(2,1)S(1)} %slice.54), channel_id=1, source_target_pairs={{0,8},{8,16},{16,24},{24,28},{28,20},{20,12},{12,4},{4,0},{1,9},{9... | collective-permute-start | bytes 1572872 | tf_op jit(solution)/shard_map/ppermute | solution.py:867
  185.4 22.1 %collective-permute-start.25 = (bf16[2,128,1024]{2,1,0:T(8,128)(2,1)}, bf16[2,128,1024]{2,1,0:T(8,128)(2,1)S(1)}, u32[]{:S(2)}, u32[]{:S(2)}) collective-permute-start(bf16[2,128,1024]{2,1,0:T(8,128)(2,1)} %get-tuple-element.264), channel_id=1, source_target_pairs={{0,8},{8,16},{16,24},{24,28},{28,20},{20,12},{12,4},{4,0},{1,9},{9... | collective-permute-start | bytes 1572872 | tf_op jit(solution)/shard_map/ppermute | solution.py:867
  186.6 20.9 %collective-permute-start.26 = (bf16[2,128,1024]{2,1,0:T(8,128)(2,1)}, bf16[2,128,1024]{2,1,0:T(8,128)(2,1)S(1)}, u32[]{:S(2)}, u32[]{:S(2)}) collective-permute-start(bf16[2,128,1024]{2,1,0:T(8,128)(2,1)} %get-tuple-element.265), channel_id=1, source_target_pairs={{8,0},{16,8},{24,16},{28,24},{20,28},{12,20},{4,12},{0,4},{9,1},{1... | collective-permute-start | bytes 1572872 | tf_op jit(solution)/shard_map/ppermute | solution.py:867
  205.5 15.0 %collective-permute-start.28 = (bf16[2,128,1024]{2,1,0:T(8,128)(2,1)}, bf16[2,128,1024]{2,1,0:T(8,128)(2,1)S(1)}, u32[]{:S(2)}, u32[]{:S(2)}) collective-permute-start(bf16[2,128,1024]{2,1,0:T(8,128)(2,1)} %get-tuple-element.272), channel_id=1, source_target_pairs={{8,0},{16,8},{24,16},{28,24},{20,28},{12,20},{4,12},{0,4},{9,1},{1... | collective-permute-start | bytes 1572872 | tf_op jit(solution)/shard_map/ppermute | solution.py:867
  207.1 14.7 %collective-permute-start.27 = (bf16[2,128,1024]{2,1,0:T(8,128)(2,1)}, bf16[2,128,1024]{2,1,0:T(8,128)(2,1)S(1)}, u32[]{:S(2)}, u32[]{:S(2)}) collective-permute-start(bf16[2,128,1024]{2,1,0:T(8,128)(2,1)} %get-tuple-element.270), channel_id=1, source_target_pairs={{0,8},{8,16},{16,24},{24,28},{28,20},{20,12},{12,4},{4,0},{1,9},{9... | collective-permute-start | bytes 1572872 | tf_op jit(solution)/shard_map/ppermute | solution.py:867
  210.9 16.7 %collective-permute-start.30 = (bf16[2,128,1024]{2,1,0:T(8,128)(2,1)}, bf16[2,128,1024]{2,1,0:T(8,128)(2,1)S(1)}, u32[]{:S(2)}, u32[]{:S(2)}) collective-permute-start(bf16[2,128,1024]{2,1,0:T(8,128)(2,1)} %get-tuple-element.278), channel_id=1, source_target_pairs={{8,0},{16,8},{24,16},{28,24},{20,28},{12,20},{4,12},{0,4},{9,1},{1... | collective-permute-start | bytes 1572872 | tf_op jit(solution)/shard_map/ppermute | solution.py:867
  212.5 16.4 %collective-permute-start.29 = (bf16[2,128,1024]{2,1,0:T(8,128)(2,1)}, bf16[2,128,1024]{2,1,0:T(8,128)(2,1)S(1)}, u32[]{:S(2)}, u32[]{:S(2)}) collective-permute-start(bf16[2,128,1024]{2,1,0:T(8,128)(2,1)} %get-tuple-element.276), channel_id=1, source_target_pairs={{0,8},{8,16},{16,24},{24,28},{28,20},{20,12},{12,4},{4,0},{1,9},{9... | collective-permute-start | bytes 1572872 | tf_op jit(solution)/shard_map/ppermute | solution.py:867
  242.6 14.6 %collective-permute-start.34 = (bf16[2,128,1024]{2,1,0:T(8,128)(2,1)}, bf16[2,128,1024]{2,1,0:T(8,128)(2,1)S(1)}, u32[]{:S(2)}, u32[]{:S(2)}) collective-permute-start(bf16[2,128,1024]{2,1,0:T(8,128)(2,1)} %get-tuple-element.292), channel_id=1, source_target_pairs={{8,0},{16,8},{24,16},{28,24},{20,28},{12,20},{4,12},{0,4},{9,1},{1... | collective-permute-start | bytes 1572872 | tf_op jit(solution)/shard_map/ppermute | solution.py:867
  244.9 14.9 %collective-permute-start.33 = (bf16[2,128,1024]{2,1,0:T(8,128)(2,1)}, bf16[2,128,1024]{2,1,0:T(8,128)(2,1)S(1)}, u32[]{:S(2)}, u32[]{:S(2)}) collective-permute-start(bf16[2,128,1024]{2,1,0:T(8,128)(2,1)} %get-tuple-element.290), channel_id=1, source_target_pairs={{0,8},{8,16},{16,24},{24,28},{28,20},{20,12},{12,4},{4,0},{1,9},{9... | collective-permute-start | bytes 1572872 | tf_op jit(solution)/shard_map/ppermute | solution.py:867
  244.9 23.5 %collective-permute-start.37 = (bf16[2,128,1024]{2,1,0:T(8,128)(2,1)S(1)}, bf16[2,128,1024]{2,1,0:T(8,128)(2,1)S(1)}, u32[]{:S(2)}, u32[]{:S(2)}) collective-permute-start(bf16[2,128,1024]{2,1,0:T(8,128)(2,1)S(1)} %copy-done.62), channel_id=1, source_target_pairs={{8,0},{16,8},{24,16},{28,24},{20,28},{12,20},{4,12},{0,4},{9,1},{1... | collective-permute-start | bytes 1572872 | tf_op jit(solution)/shard_map/ppermute | solution.py:867
  247.0 24.1 %collective-permute-start.36 = (bf16[2,128,1024]{2,1,0:T(8,128)(2,1)S(1)}, bf16[2,128,1024]{2,1,0:T(8,128)(2,1)S(1)}, u32[]{:S(2)}, u32[]{:S(2)}) collective-permute-start(bf16[2,128,1024]{2,1,0:T(8,128)(2,1)S(1)} %copy-done.61), channel_id=1, source_target_pairs={{0,8},{8,16},{16,24},{24,28},{28,20},{20,12},{12,4},{4,0},{1,9},{9... | collective-permute-start | bytes 1572872 | tf_op jit(solution)/shard_map/ppermute | solution.py:867
  265.1 34.4 %collective-permute-start.43 = (bf16[2,128,1024]{2,1,0:T(8,128)(2,1)S(1)}, bf16[2,128,1024]{2,1,0:T(8,128)(2,1)S(1)}, u32[]{:S(2)}, u32[]{:S(2)}) collective-permute-start(bf16[2,128,1024]{2,1,0:T(8,128)(2,1)S(1)} %get-tuple-element.318), channel_id=1, source_target_pairs={{8,0},{16,8},{24,16},{28,24},{20,28},{12,20},{4,12},{0,4},{9,1},{1... | collective-permute-start | bytes 1572872 | tf_op jit(solution)/shard_map/ppermute | solution.py:867
  268.4 31.1 %collective-permute-start.42 = (bf16[2,128,1024]{2,1,0:T(8,128)(2,1)S(1)}, bf16[2,128,1024]{2,1,0:T(8,128)(2,1)S(1)}, u32[]{:S(2)}, u32[]{:S(2)}) collective-permute-start(bf16[2,128,1024]{2,1,0:T(8,128)(2,1)S(1)} %get-tuple-element.317), channel_id=1, source_target_pairs={{0,8},{8,16},{16,24},{24,28},{28,20},{20,12},{12,4},{4,0},{1,9},{9... | collective-permute-start | bytes 1572872 | tf_op jit(solution)/shard_map/ppermute | solution.py:867
  304.7 27.5 %collective-permute-start.48 = (bf16[4,128,1024]{2,1,0:T(8,128)(2,1)}, bf16[4,128,1024]{2,1,0:T(8,128)(2,1)S(1)}, u32[]{:S(2)}, u32[]{:S(2)}) collective-permute-start(bf16[4,128,1024]{2,1,0:T(8,128)(2,1)} %get-tuple-element.335), channel_id=1, source_target_pairs={{8,0},{16,8},{24,16},{28,24},{20,28},{12,20},{4,12},{0,4},{9,1},{1... | collective-permute-start | bytes 3145736 | tf_op jit(solution)/shard_map/ppermute | solution.py:867
  305.6 26.6 %collective-permute-start.47 = (bf16[4,128,1024]{2,1,0:T(8,128)(2,1)}, bf16[4,128,1024]{2,1,0:T(8,128)(2,1)S(1)}, u32[]{:S(2)}, u32[]{:S(2)}) collective-permute-start(bf16[4,128,1024]{2,1,0:T(8,128)(2,1)} %get-tuple-element.333), channel_id=1, source_target_pairs={{0,8},{8,16},{16,24},{24,28},{28,20},{20,12},{12,4},{4,0},{1,9},{9... | collective-permute-start | bytes 3145736 | tf_op jit(solution)/shard_map/ppermute | solution.py:867
  306.9 25.3 %collective-permute-start.46 = (bf16[4,128,256]{2,1,0:T(8,128)(2,1)S(1)}, bf16[4,128,256]{2,1,0:T(8,128)(2,1)S(1)}, u32[]{:S(2)}, u32[]{:S(2)}) collective-permute-start(bf16[4,128,256]{2,1,0:T(8,128)(2,1)S(1)} %copy-done.65), channel_id=1, source_target_pairs={{0,3},{1,2},{2,1},{3,0},{4,7},{5,6},{6,5},{7,4},{8,11},{9,10},{10,... | collective-permute-start | bytes 786440 | tf_op jit(solution)/shard_map/ppermute | solution.py:867
  307.0 25.1 %collective-permute-start.45 = (bf16[4,128,256]{2,1,0:T(8,128)(2,1)S(1)}, bf16[4,128,256]{2,1,0:T(8,128)(2,1)S(1)}, u32[]{:S(2)}, u32[]{:S(2)}) collective-permute-start(bf16[4,128,256]{2,1,0:T(8,128)(2,1)S(1)} %copy-done.64), channel_id=1, source_target_pairs={{0,2},{1,3},{2,0},{3,1},{4,6},{5,7},{6,4},{7,5},{8,10},{9,11},{10,... | collective-permute-start | bytes 786440 | tf_op jit(solution)/shard_map/ppermute | solution.py:867
  308.1 24.1 %collective-permute-start.44 = (bf16[4,128,256]{2,1,0:T(8,128)(2,1)S(1)}, bf16[4,128,256]{2,1,0:T(8,128)(2,1)S(1)}, u32[]{:S(2)}, u32[]{:S(2)}) collective-permute-start(bf16[4,128,256]{2,1,0:T(8,128)(2,1)S(1)} %copy-done.63), channel_id=1, source_target_pairs={{0,1},{1,0},{2,3},{3,2},{4,5},{5,4},{6,7},{7,6},{8,9},{9,8},{10,11... | collective-permute-start | bytes 786440 | tf_op jit(solution)/shard_map/ppermute | solution.py:867
  346.7 14.5 %collective-permute-start.51 = (bf16[1,256,1024]{2,1,0:T(8,128)(2,1)}, bf16[1,256,1024]{2,1,0:T(8,128)(2,1)S(1)}, u32[]{:S(2)}, u32[]{:S(2)}) collective-permute-start(bf16[1,256,1024]{2,1,0:T(8,128)(2,1)} %bitcast.89), channel_id=1, source_target_pairs={{0,2},{1,3},{2,0},{3,1},{4,6},{5,7},{6,4},{7,5},{8,10},{9,11},{10,... | collective-permute-start | bytes 1572872 | tf_op jit(solution)/shard_map/ppermute | solution.py:867
  347.6 34.8 %collective-permute-start.53 = (bf16[4,128,1024]{2,1,0:T(8,128)(2,1)}, bf16[4,128,1024]{2,1,0:T(8,128)(2,1)S(1)}, u32[]{:S(2)}, u32[]{:S(2)}) collective-permute-start(bf16[4,128,1024]{2,1,0:T(8,128)(2,1)} %get-tuple-element.362), channel_id=1, source_target_pairs={{8,0},{16,8},{24,16},{28,24},{20,28},{12,20},{4,12},{0,4},{9,1},{1... | collective-permute-start | bytes 3145736 | tf_op jit(solution)/shard_map/ppermute | solution.py:867
  348.4 34.0 %collective-permute-start.52 = (bf16[4,128,1024]{2,1,0:T(8,128)(2,1)}, bf16[4,128,1024]{2,1,0:T(8,128)(2,1)S(1)}, u32[]{:S(2)}, u32[]{:S(2)}) collective-permute-start(bf16[4,128,1024]{2,1,0:T(8,128)(2,1)} %get-tuple-element.360), channel_id=1, source_target_pairs={{0,8},{8,16},{16,24},{24,28},{28,20},{20,12},{12,4},{4,0},{1,9},{9... | collective-permute-start | bytes 3145736 | tf_op jit(solution)/shard_map/ppermute | solution.py:867
  366.0 36.8 %all-to-all-start = ((bf16[8,33,1024]{2,1,0:T(8,128)(2,1)}), bf16[8,33,1024]{2,1,0:T(8,128)(2,1)S(1)}, u32[]{:S(2)}, u32[]{:S(2)}) async-start(bf16[8,33,1024]{2,1,0:T(8,128)(2,1)} %fusion.1), calls=%async_computation | async-start | bytes 1310720 | tf_op jit(solution)/shard_map/all_to_all | solution.py:1099
  387.9 31.7 %collective-permute-start.59 = (bf16[4,128,1024]{2,1,0:T(8,128)(2,1)}, bf16[4,128,1024]{2,1,0:T(8,128)(2,1)}, u32[]{:S(2)}, u32[]{:S(2)}) collective-permute-start(bf16[4,128,1024]{2,1,0:T(8,128)(2,1)} %get-tuple-element.377), channel_id=1, source_target_pairs={{8,0},{16,8},{24,16},{28,24},{20,28},{12,20},{4,12},{0,4},{9,1},{1... | collective-permute-start | bytes 3145736 | tf_op jit(solution)/shard_map/ppermute | solution.py:867
  389.9 29.7 %collective-permute-start.58 = (bf16[4,128,1024]{2,1,0:T(8,128)(2,1)}, bf16[4,128,1024]{2,1,0:T(8,128)(2,1)}, u32[]{:S(2)}, u32[]{:S(2)}) collective-permute-start(bf16[4,128,1024]{2,1,0:T(8,128)(2,1)} %get-tuple-element.375), channel_id=1, source_target_pairs={{0,8},{8,16},{16,24},{24,28},{28,20},{20,12},{12,4},{4,0},{1,9},{9... | collective-permute-start | bytes 3145736 | tf_op jit(solution)/shard_map/ppermute | solution.py:867
  405.9 33.2 %collective-permute-start.62 = (bf16[1,2112,256]{2,1,0:T(8,128)(2,1)S(1)}, bf16[1,2112,256]{2,1,0:T(8,128)(2,1)S(1)}, u32[]{:S(2)}, u32[]{:S(2)}) collective-permute-start(bf16[1,2112,256]{2,1,0:T(8,128)(2,1)S(1)} %copy-done.22), channel_id=1, source_target_pairs={{0,2},{1,3},{2,0},{3,1},{4,6},{5,7},{6,4},{7,5},{8,10},{9,11},{10,... | collective-permute-start | bytes 3244040 | tf_op jit(solution)/shard_map/ppermute | solution.py:867
  431.2 15.3 %collective-permute-start.65 = (bf16[4,128,256]{2,1,0:T(8,128)(2,1)}, bf16[4,128,256]{2,1,0:T(8,128)(2,1)}, u32[]{:S(2)}, u32[]{:S(2)}) collective-permute-start(bf16[4,128,256]{2,1,0:T(8,128)(2,1)} %get-tuple-element.398), channel_id=1, source_target_pairs={{0,3},{1,2},{2,1},{3,0},{4,7},{5,6},{6,5},{7,4},{8,11},{9,10},{10,... | collective-permute-start | bytes 786440 | tf_op jit(solution)/shard_map/ppermute | solution.py:867
  431.3 15.2 %collective-permute-start.64 = (bf16[4,128,256]{2,1,0:T(8,128)(2,1)}, bf16[4,128,256]{2,1,0:T(8,128)(2,1)}, u32[]{:S(2)}, u32[]{:S(2)}) collective-permute-start(bf16[4,128,256]{2,1,0:T(8,128)(2,1)} %get-tuple-element.396), channel_id=1, source_target_pairs={{0,2},{1,3},{2,0},{3,1},{4,6},{5,7},{6,4},{7,5},{8,10},{9,11},{10,... | collective-permute-start | bytes 786440 | tf_op jit(solution)/shard_map/ppermute | solution.py:867
  432.2 14.3 %collective-permute-start.63 = (bf16[4,128,256]{2,1,0:T(8,128)(2,1)}, bf16[4,128,256]{2,1,0:T(8,128)(2,1)}, u32[]{:S(2)}, u32[]{:S(2)}) collective-permute-start(bf16[4,128,256]{2,1,0:T(8,128)(2,1)} %get-tuple-element.394), channel_id=1, source_target_pairs={{0,1},{1,0},{2,3},{3,2},{4,5},{5,4},{6,7},{7,6},{8,9},{9,8},{10,11... | collective-permute-start | bytes 786440 | tf_op jit(solution)/shard_map/ppermute | solution.py:867
  433.2 42.0 %all-to-all-start.1 = ((bf16[8,384,256]{2,1,0:T(8,128)(2,1)}), bf16[8,384,256]{2,1,0:T(8,128)(2,1)}, u32[]{:S(2)}, u32[]{:S(2)}) async-start(bf16[8,384,256]{2,1,0:T(8,128)(2,1)} %get-tuple-element.411), calls=%async_computation.1 | async-start | bytes 3145728 | tf_op jit(solution)/shard_map/all_to_all | solution.py:1135
  449.1 14.8 %collective-permute-start.66 = (bf16[1,8,32,1024]{3,2,1,0:T(8,128)(2,1)S(1)}, bf16[1,8,32,1024]{3,2,1,0:T(8,128)(2,1)S(1)}, u32[]{:S(2)}, u32[]{:S(2)}) collective-permute-start(bf16[1,8,32,1024]{3,2,1,0:T(8,128)(2,1)S(1)} %bitcast.69), channel_id=1, source_target_pairs={{0,2},{1,3},{2,0},{3,1},{4,6},{5,7},{6,4},{7,5},{8,10},{9,11},{10,... | collective-permute-start | bytes 1572872 | tf_op jit(solution)/shard_map/ppermute | solution.py:867
  (90 other events, 821.0 us)

commit v6 on v5

--- a/solution.py
+++ b/solution.py
@@ -11,7 +11,7 @@
 EPS = 1e-05
 MASKED = -1e30
 GROUP = 16
-STEP = 32
+STEP = 64
 EXTRA = 16
 COST = 0.0001
 VMEM_LIMIT = 56 * 1024 * 1024

time: 487 us -> 492 us (1.010)
  waiting for transfers between devices: 152 us -> 157 us
    ppermute x70, waiting for transfers between devices: 150 us -> 157 us  [send(): return lax.ppermute(self.tie(value), axis, pairs)]
where the time goes in v6:
time: 492 us; the launch traced here: 483 us
  Pallas kernels  204 us (41%)
  waiting for transfers between devices  157 us (32%)
  starting transfers between devices  71.2 us (14%)
  local copies, waits for them, and re-layouts  39 us (8%)
  other arithmetic  9.1 us (2%)
    ppermute x70, waiting for transfers between devices, send(): return lax.ppermute(self.tie(value), axis, pairs)  157 us
    ppermute x70, starting transfers between devices, send(): return lax.ppermute(self.tie(value), axis, pairs)  63.1 us
    pallas_call x5, Pallas kernels, ffn(): pl.pallas_call(functools.partial(ffn_kernel, [len(v) for v in blocks]), g...  61.5 us
    pallas_call x3, Pallas kernels, weight_grad(): pl.pallas_call(kernel, grid_spec=pltpu.PrefetchScalarGridSpec(num_scalar_...  38.3 us
    pallas_call x1, Pallas kernels, attention_back(): pl.pallas_call(functools.partial(attn_back_kernel, count, ring), grid_spe...  22.9 us
    pallas_call x1, Pallas kernels, attention(): pl.pallas_call(functools.partial(attn_kernel, count), grid_spec=pltpu.Pre...  17.4 us
    unnamed x139, local copies, waits for them, and re-layouts  17.4 us
    pallas_call x7, Pallas kernels, merge(): pl.pallas_call(functools.partial(merge_kernel, n), grid_spec=pltpu.Prefet...  16.3 us
  transfers between devices with their start and end apart: 72, of which 32 were waited for; matrix products, arithmetic and copies ran while one was open for 5% of the time, Pallas kernels for 40%

profile of v6, /device:TPU:0, one launch (start us, length us, event | category | flops | bytes accessed | tf_op | source)
XLA Modules:
  0.0 482.8 jit_solution(5350078342836918869)
XLA Ops:
  2.3 2.8 shard_map.153
  8.1 13.2 %copy.29 = bf16[512,4,3,1024]{3,0,2,1:T(8,128)(2,1)} copy(bf16[512,4,3,1024]{3,1,2,0:T(4,128)(2,1)} %param.16) | data formatting | bytes 25165824 | tf_op jit(solution)/shard_map/optimization_barrier | solution.py:851
  26.5 21.8 %collective-permute-done.6.refs_2_ = bf16[128,16,256]{2,1,0:T(8,128)(2,1)S(1)} collective-permute-done((bf16[128,16,256]{2,1,0:T(8,128)(2,1)S(1)}, bf16[128,16,256]{2,1,0:T(8,128)(2,1)S(1)}, u32[]{:S(2)}, u32[]{:S(2)}) %collective-permute-start.6) | collective-permute-done | bytes 1048608 | tf_op jit(solution)/shard_map/ppermute | solution.py:867
  52.7 17.4 %shard_map.154 = (bf16[3,2048,256]{2,1,0:T(8,128)(2,1)}, bf16[4,4,128,256]{3,2,1,0:T(8,128)(2,1)}, bf16[4,128,256]{2,1,0:T(8,128)(2,1)}, bf16[4,128,256]{2,1,0:T...) custom-call(s32[1]{0:T(128)} %bitcast.idx_ref, bf16[128,16,256]{2,1,0:T(8,128)(2,1)} %refs_0_.5, ...), custom_call_target="tpu_custom_call" | custom-call | flops 920000 | bytes 800 | tf_op jit(solution)/shard_map/pallas_call | solution.py:211
  76.0 3.0 collective-permute-done.12.refs_3_
  79.0 4.7 collective-permute-done.11.refs_2_
  84.5 5.7 %shard_map.155 = (f32[4,128,1024]{2,1,0:T(8,128)}, bf16[4,128,1024]{2,1,0:T(8,128)(2,1)}) custom-call(s32[1]{0:T(128)} %bitcast.idx_ref, bf16[4,128,256]{2,1,0:T(8,128)(2,1)} %get-tuple-element.227.refs_0_, bf16[4,128,256]{2,1,0:T(8,128)(2,1)} %copy-done.30, bf16[4,128,256]{2,1,0:T(8,128)(2,1)} %copy-done.29, bf16[4,128,256]{2,1,0:T(8,128)(2,1)} %copy-done.28, ...), custom_call_target="tpu_custom_call" | custom-call | flops 690000 | bytes 600 | tf_op jit(solution)/shard_map/pallas_call | solution.py:281
  92.2 8.0 %collective-permute-done.14.refs_3_.refs_11_ = bf16[4,128,1024]{2,1,0:T(8,128)(2,1)S(1)} collective-permute-done((bf16[4,128,1024]{2,1,0:T(8,128)(2,1)}, bf16[4,128,1024]{2,1,0:T(8,128)(2,1)S(1)}, u32[]{:S(2)}, u32[]{:S(2)}) %collective-permute-start.14) | collective-permute-done | bytes 1048608 | tf_op jit(solution)/shard_map/ppermute | solution.py:867
  101.7 11.3 %shard_map.156 = (bf16[2,128,1024]{2,1,0:T(8,128)(2,1)}, bf16[2,128,1024]{2,1,0:T(8,128)(2,1)}, bf16[4,128,1024]{2,1,0:T(8,128)(2,1)}, bf16[4,3,128,512]{3,2,1,0:T(8,128)(2,1)}) custom-call(s32[1]{0:T(128)} %bitcast.idx_ref, bf16[4,128,1024]{2,1,0:T(8,128)(2,1)} %get-tuple-element.245.refs_0_.refs_5_, bf16[4,128,1024]{2,1,0:T(8,128)(2,1)} %bitcast.60, ...), custom_call_target="tpu_custom_call" | custom-call | flops 977500 | bytes 850 | tf_op jit(solution)/shard_map/pallas_call | solution.py:351
  113.0 7.5 %collective-permute-done.16.refs_1_.refs_7_ = bf16[4,128,1024]{2,1,0:T(8,128)(2,1)S(1)} collective-permute-done((bf16[4,128,1024]{2,1,0:T(8,128)(2,1)}, bf16[4,128,1024]{2,1,0:T(8,128)(2,1)S(1)}, u32[]{:S(2)}, u32[]{:S(2)}) %collective-permute-start.16) | collective-permute-done | bytes 1048608 | tf_op jit(solution)/shard_map/ppermute | solution.py:867
  123.0 13.1 %shard_map.157 = (bf16[2,128,1024]{2,1,0:T(8,128)(2,1)}, bf16[2,128,1024]{2,1,0:T(8,128)(2,1)}, bf16[2,128,1024]{2,1,0:T(8,128)(2,1)}, bf16[2,128,1024]{2,1,0:T(...) custom-call(s32[1]{0:T(128)} %bitcast.idx_ref, ...), custom_call_target="tpu_custom_call" | custom-call | flops 1552500 | bytes 1350 | tf_op jit(solution)/shard_map/pallas_call | solution.py:351
  136.1 7.7 %collective-permute-done.18.refs_1_.refs_9_ = bf16[4,128,1024]{2,1,0:T(8,128)(2,1)S(1)} collective-permute-done((bf16[4,128,1024]{2,1,0:T(8,128)(2,1)S(1)}, bf16[4,128,1024]{2,1,0:T(8,128)(2,1)S(1)}, u32[]{:S(2)}, u32[]{:S(2)}) %collective-permute-start.18) | collective-permute-done | bytes 1048608 | tf_op jit(solution)/shard_map/ppermute | solution.py:867
  148.0 13.2 %shard_map.158 = (bf16[2,128,1024]{2,1,0:T(8,128)(2,1)}, bf16[2,128,1024]{2,1,0:T(8,128)(2,1)}, bf16[2,128,1024]{2,1,0:T(8,128)(2,1)}, bf16[2,128,1024]{2,1,0:T(...) custom-call(s32[1]{0:T(128)} %bitcast.idx_ref, ...), custom_call_target="tpu_custom_call" | custom-call | flops 1552500 | bytes 1350 | tf_op jit(solution)/shard_map/pallas_call | solution.py:351
  161.2 8.7 %collective-permute-done.20.refs_1_.refs_11_ = bf16[4,128,1024]{2,1,0:T(8,128)(2,1)S(1)} collective-permute-done((bf16[4,128,1024]{2,1,0:T(8,128)(2,1)S(1)}, bf16[4,128,1024]{2,1,0:T(8,128)(2,1)S(1)}, u32[]{:S(2)}, u32[]{:S(2)}) %collective-permute-start.20) | collective-permute-done | bytes 1048608 | tf_op jit(solution)/shard_map/ppermute | solution.py:867
  172.5 13.1 %shard_map.159 = (bf16[2,128,1024]{2,1,0:T(8,128)(2,1)}, bf16[2,128,1024]{2,1,0:T(8,128)(2,1)}, bf16[2,128,1024]{2,1,0:T(8,128)(2,1)}, bf16[2,128,1024]{2,1,0:T(...) custom-call(s32[1]{0:T(128)} %bitcast.idx_ref, ...), custom_call_target="tpu_custom_call" | custom-call | flops 1552500 | bytes 1350 | tf_op jit(solution)/shard_map/pallas_call | solution.py:351
  187.6 4.8 collective-permute-done.22.refs_1_.refs_13_
  194.6 11.0 %shard_map.160 = (bf16[2,128,1024]{2,1,0:T(8,128)(2,1)}, bf16[2,128,1024]{2,1,0:T(8,128)(2,1)}, bf16[4,128,1024]{2,1,0:T(8,128)(2,1)}, bf16[4,3,128,512]{3,2,1,0:T(8,128)(2,1)}) custom-call(s32[1]{0:T(128)} %bitcast.idx_ref, bf16[2,128,1024]{2,1,0:T(8,128)(2,1)} %copy-done.17, bf16[2,128,1024]{2,1,0:T(8,128)(2,1)} %copy-done.16, ...), custom_call_target="tpu_custom_call" | custom-call | flops 977500 | bytes 850 | tf_op jit(solution)/shard_map/pallas_call | solution.py:351
  213.0 7.7 %collective-permute-done.28.refs_3_ = bf16[2,128,1024]{2,1,0:T(8,128)(2,1)S(1)} collective-permute-done((bf16[2,128,1024]{2,1,0:T(8,128)(2,1)}, bf16[2,128,1024]{2,1,0:T(8,128)(2,1)S(1)}, u32[]{:S(2)}, u32[]{:S(2)}) %collective-permute-start.28) | collective-permute-done | bytes 524320 | tf_op jit(solution)/shard_map/ppermute | solution.py:867
  232.7 5.2 %collective-permute-done.32.refs_3_ = bf16[2,128,1024]{2,1,0:T(8,128)(2,1)S(1)} collective-permute-done((bf16[2,128,1024]{2,1,0:T(8,128)(2,1)}, bf16[2,128,1024]{2,1,0:T(8,128)(2,1)S(1)}, u32[]{:S(2)}, u32[]{:S(2)}) %collective-permute-start.32) | collective-permute-done | bytes 524320 | tf_op jit(solution)/shard_map/ppermute | solution.py:867
  240.6 2.5 shard_map.164
  247.1 9.9 %collective-permute-done.34.refs_3_ = bf16[2,128,1024]{2,1,0:T(8,128)(2,1)S(1)} collective-permute-done((bf16[2,128,1024]{2,1,0:T(8,128)(2,1)}, bf16[2,128,1024]{2,1,0:T(8,128)(2,1)S(1)}, u32[]{:S(2)}, u32[]{:S(2)}) %collective-permute-start.34) | collective-permute-done | bytes 524320 | tf_op jit(solution)/shard_map/ppermute | solution.py:867
  265.1 3.1 collective-permute-done.37.refs_2_
  270.1 4.8 collective-permute-done.38.refs_3_
  277.2 8.1 %shard_map.166 = (bf16[4,128,1024]{2,1,0:T(8,128)(2,1)}, f32[4,1,1024]{2,1,0:T(1,128)}, bf16[4,128,256]{2,1,0:T(8,128)(2,1)}, bf16[4,128,256]{2,1,0:T(8,128)(2,1...) custom-call(s32[1]{0:T(128)} %bitcast.idx_ref, ...), custom_call_target="tpu_custom_call" | custom-call | flops 920000 | bytes 800 | tf_op jit(solution)/shard_map/pallas_call | solution.py:520
  287.3 3.8 shard_map.167
  291.1 3.1 collective-permute-done.41.refs_7_
  294.2 5.6 %collective-permute-done.40.refs_6_ = bf16[4,128,256]{2,1,0:T(8,128)(2,1)S(1)} collective-permute-done((bf16[4,128,256]{2,1,0:T(8,128)(2,1)}, bf16[4,128,256]{2,1,0:T(8,128)(2,1)S(1)}, u32[]{:S(2)}, u32[]{:S(2)}) %collective-permute-start.40) | collective-permute-done | bytes 262176 | tf_op jit(solution)/shard_map/ppermute | solution.py:867
  300.9 4.1 shard_map.168
  308.9 22.9 %shard_map.169 = (bf16[2,2080,256]{2,1,0:T(8,128)(2,1)}, bf16[2,2080,256]{2,1,0:T(8,128)(2,1)}, bf16[8,384,256]{2,1,0:T(8,128)(2,1)}, f32[4,1,256]{2,1,0:T(1,128)}) custom-call(s32[1]{0:T(128)} %bitcast.idx_ref, bf16[128,16,256]{2,1,0:T(8,128)(2,1)} %refs_0_.5, bf16[128,16,256]{2,1,0:T(8,128)(2,1)} %copy-done.11, bf16[128,16,256]{2,1,0:T(8,128)(2,1)} %copy-done.10, ...), custom_call_target="tpu_custom_call" | custom-call | flops 2990000 | bytes 2600 | tf_op jit(solution)/shard_map/pallas_call | solution.py:630
  333.2 4.3 shard_map.170
  338.0 4.8 %collective-permute-done.49 = bf16[2,256,1024]{2,1,0:T(8,128)(2,1)S(1)} collective-permute-done((bf16[2,256,1024]{2,1,0:T(8,128)(2,1)S(1)}, bf16[2,256,1024]{2,1,0:T(8,128)(2,1)S(1)}, u32[]{:S(2)}, u32[]{:S(2)}) %collective-permute-start.49) | collective-permute-done | bytes 1048608 | tf_op jit(solution)/shard_map/ppermute | solution.py:867
  350.4 2.8 shard_map.172
  353.2 7.6 %collective-permute-done.51 = bf16[1,256,1024]{2,1,0:T(8,128)(2,1)S(1)} collective-permute-done((bf16[1,256,1024]{2,1,0:T(8,128)(2,1)}, bf16[1,256,1024]{2,1,0:T(8,128)(2,1)S(1)}, u32[]{:S(2)}, u32[]{:S(2)}) %collective-permute-start.51) | collective-permute-done | bytes 524320 | tf_op jit(solution)/shard_map/ppermute | solution.py:867
  365.6 3.8 all-to-all-start
  369.4 12.8 %shard_map.174.refs_14_ = f32[512,3,4,1024]{3,2,1,0:T(4,128)} custom-call(s32[1]{0:T(128)} %bitcast.idx_ref, bf16[4,3,128,512]{3,2,1,0:T(8,128)(2,1)} %get-tuple-element.352.refs_0_, bf16[4,3,256,512]{3,2,1,0:T(8,128)(2,1)} %get-tuple-element.353.refs_1_, bf16[4,3,256,512]{3,2,1,0:T(8,128)(2,1)} %get-tuple-element.354.refs_2_, ...), custom_call_target="tpu_custom_call" | custom-call | flops 1380000 | bytes 1200 | tf_op jit(solution)/shard_map/pallas_call | solution.py:416
  383.5 4.2 shard_map.175
  389.8 12.8 %shard_map.176.refs_14_ = f32[512,3,4,1024]{3,2,1,0:T(4,128)} custom-call(s32[1]{0:T(128)} %bitcast.idx_ref, bf16[4,3,128,512]{3,2,1,0:T(8,128)(2,1)} %get-tuple-element.352.refs_0_, bf16[4,3,256,512]{3,2,1,0:T(8,128)(2,1)} %get-tuple-element.353.refs_1_, bf16[4,3,256,512]{3,2,1,0:T(8,128)(2,1)} %get-tuple-element.354.refs_2_, ...), custom_call_target="tpu_custom_call", output_to_operand_aliasing={{}: (15, {})} | custom-call | flops 1380000 | bytes 1200 | tf_op jit(solution)/shard_map/pallas_call | solution.py:416
  402.7 2.9 collective-permute-start.54
  405.7 11.0 %collective-permute-done.55 = f32[4,1,256]{2,1,0:T(1,128)S(1)} collective-permute-done((f32[4,1,256]{2,1,0:T(1,128)S(1)}, f32[4,1,256]{2,1,0:T(1,128)S(1)}, u32[]{:S(2)}, u32[]{:S(2)}) %collective-permute-start.55) | collective-permute-done | bytes 4128 | tf_op jit(solution)/shard_map/ppermute | solution.py:867
  419.7 4.4 shard_map.177
  424.1 2.7 collective-permute-start.60
  426.9 4.3 collective-permute-done.61
  433.3 4.3 all-to-all-start.1
  439.0 6.9 %collective-permute-done.62.refs_10_ = bf16[1,2080,256]{2,1,0:T(8,128)(2,1)S(1)} collective-permute-done((bf16[1,2080,256]{2,1,0:T(8,128)(2,1)S(1)}, bf16[1,2080,256]{2,1,0:T(8,128)(2,1)S(1)}, u32[]{:S(2)}, u32[]{:S(2)}) %collective-permute-start.62) | collective-permute-done | bytes 1064992 | tf_op jit(solution)/shard_map/ppermute | solution.py:867
  446.9 5.3 %shard_map.178 = bf16[128,16,256]{2,1,0:T(8,128)(2,1)} custom-call(s32[1]{0:T(128)} %bitcast.idx_ref, bf16[128,16,256]{2,1,0:T(8,128)(2,1)} %refs_0_.5, bf16[128,16,256]{2,1,0:T(8,128)(2,1)} %copy-done.11, bf16[128,16,256]{2,1,0:T(8,128)(2,1)} %copy-done.10, bf16[128,16,256]{2,1,0:T(8,128)(2,1)} %copy-done.12, ...), custom_call_target="tpu_custom_call" | custom-call | flops 460000 | bytes 400 | tf_op jit(solution)/shard_map/pallas_call | solution.py:767
  452.8 2.5 shard_map.179
  457.3 12.8 %shard_map.180 = f32[512,3,4,1024]{3,2,1,0:T(4,128)} custom-call(s32[1]{0:T(128)} %bitcast.idx_ref, bf16[4,3,128,512]{3,2,1,0:T(8,128)(2,1)} %get-tuple-element.352.refs_0_, bf16[4,3,256,512]{3,2,1,0:T(8,128)(2,1)} %get-tuple-element.353.refs_1_, bf16[4,3,256,512]{3,2,1,0:T(8,128)(2,1)} %get-tuple-element.354.refs_2_, ...), custom_call_target="tpu_custom_call", output_to_operand_aliasing={{}: (15, {})} | custom-call | flops 1380000 | bytes 1200 | tf_op jit(solution)/shard_map/pallas_call | solution.py:416
  477.3 2.6 bitcast_convert_fusion
  (307 shorter events, 120.8 us)
Async XLA Ops:
  5.0 16.3 %collective-permute-start.2 = (bf16[4,128,256]{2,1,0:T(8,128)(2,1)}, bf16[4,128,256]{2,1,0:T(8,128)(2,1)S(1)}, u32[]{:S(2)}, u32[]{:S(2)}) collective-permute-start(bf16[4,128,256]{2,1,0:T(8,128)(2,1)} %get-tuple-element.217), channel_id=1, source_target_pairs={{0,3},{1,2},{2,1},{3,0},{4,7},{5,6},{6,5},{7,4},{8,11},{9,10},{10,... | collective-permute-start | bytes 786440 | tf_op jit(solution)/shard_map/ppermute | solution.py:867
  22.8 25.5 %collective-permute-start.6 = (bf16[128,16,256]{2,1,0:T(8,128)(2,1)S(1)}, bf16[128,16,256]{2,1,0:T(8,128)(2,1)S(1)}, u32[]{:S(2)}, u32[]{:S(2)}) collective-permute-start(bf16[128,16,256]{2,1,0:T(8,128)(2,1)S(1)} %copy-done.9), channel_id=1, source_target_pairs={{0,2},{1,3},{2,0},{3,1},{4,6},{5,7},{6,4},{7,5},{8,10},{9,11},{10,... | collective-permute-start | bytes 3145736 | tf_op jit(solution)/shard_map/ppermute | solution.py:867
  24.5 24.9 %collective-permute-start.4 = (bf16[4,128,1024]{2,1,0:T(8,128)(2,1)S(1)}, bf16[4,128,1024]{2,1,0:T(8,128)(2,1)S(1)}, u32[]{:S(2)}, u32[]{:S(2)}) collective-permute-start(bf16[4,128,1024]{2,1,0:T(8,128)(2,1)S(1)} %bitcast.58), channel_id=1, source_target_pairs={{8,0},{16,8},{24,16},{28,24},{20,28},{12,20},{4,12},{0,4},{9,1},{1... | collective-permute-start | bytes 3145736 | tf_op jit(solution)/shard_map/ppermute | solution.py:867
  26.0 24.9 %collective-permute-start.3 = (bf16[4,128,1024]{2,1,0:T(8,128)(2,1)S(1)}, bf16[4,128,1024]{2,1,0:T(8,128)(2,1)}, u32[]{:S(2)}, u32[]{:S(2)}) collective-permute-start(bf16[4,128,1024]{2,1,0:T(8,128)(2,1)S(1)} %bitcast.59), channel_id=1, source_target_pairs={{0,8},{8,16},{16,24},{24,28},{28,20},{20,12},{12,4},{4,0},{1,9},{9... | collective-permute-start | bytes 3145736 | tf_op jit(solution)/shard_map/ppermute | solution.py:867
  26.5 24.9 %collective-permute-start.5 = (bf16[128,16,256]{2,1,0:T(8,128)(2,1)S(1)}, bf16[128,16,256]{2,1,0:T(8,128)(2,1)S(1)}, u32[]{:S(2)}, u32[]{:S(2)}) collective-permute-start(bf16[128,16,256]{2,1,0:T(8,128)(2,1)S(1)} %copy-done.9), channel_id=1, source_target_pairs={{0,1},{1,0},{2,3},{3,2},{4,5},{5,4},{6,7},{7,6},{8,9},{9,8},{10,11... | collective-permute-start | bytes 3145736 | tf_op jit(solution)/shard_map/ppermute | solution.py:867
  49.4 24.6 %collective-permute-start.9 = (bf16[4,128,1024]{2,1,0:T(8,128)(2,1)S(1)}, bf16[4,128,1024]{2,1,0:T(8,128)(2,1)}, u32[]{:S(2)}, u32[]{:S(2)}) collective-permute-start(bf16[4,128,1024]{2,1,0:T(8,128)(2,1)S(1)} %collective-permute-done.4.refs_3_.refs_7_), channel_id=1, source_target_pairs={{8,0},{16,8},{24,16},{28,24},{20,28},{12,20},{4,12},{0,4},{9,1},{1... | collective-permute-start | bytes 3145736 | tf_op jit(solution)/shard_map/ppermute | solution.py:867
  50.9 24.6 %collective-permute-start.8 = (bf16[4,128,1024]{2,1,0:T(8,128)(2,1)}, bf16[4,128,1024]{2,1,0:T(8,128)(2,1)}, u32[]{:S(2)}, u32[]{:S(2)}) collective-permute-start(bf16[4,128,1024]{2,1,0:T(8,128)(2,1)} %collective-permute-done.3.refs_2_.refs_6_), channel_id=1, source_target_pairs={{0,8},{8,16},{16,24},{24,28},{28,20},{20,12},{12,4},{4,0},{1,9},{9... | collective-permute-start | bytes 3145736 | tf_op jit(solution)/shard_map/ppermute | solution.py:867
  73.9 26.3 %collective-permute-start.14 = (bf16[4,128,1024]{2,1,0:T(8,128)(2,1)}, bf16[4,128,1024]{2,1,0:T(8,128)(2,1)S(1)}, u32[]{:S(2)}, u32[]{:S(2)}) collective-permute-start(bf16[4,128,1024]{2,1,0:T(8,128)(2,1)} %collective-permute-done.9.refs_3_.refs_9_), channel_id=1, source_target_pairs={{8,0},{16,8},{24,16},{28,24},{20,28},{12,20},{4,12},{0,4},{9,1},{1... | collective-permute-start | bytes 3145736 | tf_op jit(solution)/shard_map/ppermute | solution.py:867
  75.4 26.3 %collective-permute-start.13 = (bf16[4,128,1024]{2,1,0:T(8,128)(2,1)}, bf16[4,128,1024]{2,1,0:T(8,128)(2,1)S(1)}, u32[]{:S(2)}, u32[]{:S(2)}) collective-permute-start(bf16[4,128,1024]{2,1,0:T(8,128)(2,1)} %collective-permute-done.8.refs_2_.refs_8_), channel_id=1, source_target_pairs={{0,8},{8,16},{16,24},{24,28},{28,20},{20,12},{12,4},{4,0},{1,9},{9... | collective-permute-start | bytes 3145736 | tf_op jit(solution)/shard_map/ppermute | solution.py:867
  90.2 30.2 %collective-permute-start.16 = (bf16[4,128,1024]{2,1,0:T(8,128)(2,1)}, bf16[4,128,1024]{2,1,0:T(8,128)(2,1)S(1)}, u32[]{:S(2)}, u32[]{:S(2)}) collective-permute-start(bf16[4,128,1024]{2,1,0:T(8,128)(2,1)} %get-tuple-element.245.refs_0_.refs_5_), channel_id=1, source_target_pairs={{8,0},{16,8},{24,16},{28,24},{20,28},{12,20},{4,12},{0,4},{9,1},{1... | collective-permute-start | bytes 3145736 | tf_op jit(solution)/shard_map/ppermute | solution.py:867
  91.7 30.2 %collective-permute-start.15 = (bf16[4,128,1024]{2,1,0:T(8,128)(2,1)}, bf16[4,128,1024]{2,1,0:T(8,128)(2,1)S(1)}, u32[]{:S(2)}, u32[]{:S(2)}) collective-permute-start(bf16[4,128,1024]{2,1,0:T(8,128)(2,1)} %get-tuple-element.245.refs_0_.refs_5_), channel_id=1, source_target_pairs={{0,8},{8,16},{16,24},{24,28},{28,20},{20,12},{12,4},{4,0},{1,9},{9... | collective-permute-start | bytes 3145736 | tf_op jit(solution)/shard_map/ppermute | solution.py:867
  120.4 23.3 %collective-permute-start.18 = (bf16[4,128,1024]{2,1,0:T(8,128)(2,1)S(1)}, bf16[4,128,1024]{2,1,0:T(8,128)(2,1)S(1)}, u32[]{:S(2)}, u32[]{:S(2)}) collective-permute-start(bf16[4,128,1024]{2,1,0:T(8,128)(2,1)S(1)} %collective-permute-done.16.refs_1_.refs_7_), channel_id=1, source_target_pairs={{8,0},{16,8},{24,16},{28,24},{20,28},{12,20},{4,12},{0,4},{9,1},{1... | collective-permute-start | bytes 3145736 | tf_op jit(solution)/shard_map/ppermute | solution.py:867
  121.9 23.3 %collective-permute-start.17 = (bf16[4,128,1024]{2,1,0:T(8,128)(2,1)S(1)}, bf16[4,128,1024]{2,1,0:T(8,128)(2,1)S(1)}, u32[]{:S(2)}, u32[]{:S(2)}) collective-permute-start(bf16[4,128,1024]{2,1,0:T(8,128)(2,1)S(1)} %collective-permute-done.15.refs_0_.refs_6_), channel_id=1, source_target_pairs={{0,8},{8,16},{16,24},{24,28},{28,20},{20,12},{12,4},{4,0},{1,9},{9... | collective-permute-start | bytes 3145736 | tf_op jit(solution)/shard_map/ppermute | solution.py:867
  143.8 26.1 %collective-permute-start.20 = (bf16[4,128,1024]{2,1,0:T(8,128)(2,1)S(1)}, bf16[4,128,1024]{2,1,0:T(8,128)(2,1)S(1)}, u32[]{:S(2)}, u32[]{:S(2)}) collective-permute-start(bf16[4,128,1024]{2,1,0:T(8,128)(2,1)S(1)} %collective-permute-done.18.refs_1_.refs_9_), channel_id=1, source_target_pairs={{8,0},{16,8},{24,16},{28,24},{20,28},{12,20},{4,12},{0,4},{9,1},{1... | collective-permute-start | bytes 3145736 | tf_op jit(solution)/shard_map/ppermute | solution.py:867
  145.3 26.2 %collective-permute-start.19 = (bf16[4,128,1024]{2,1,0:T(8,128)(2,1)S(1)}, bf16[4,128,1024]{2,1,0:T(8,128)(2,1)S(1)}, u32[]{:S(2)}, u32[]{:S(2)}) collective-permute-start(bf16[4,128,1024]{2,1,0:T(8,128)(2,1)S(1)} %collective-permute-done.17.refs_0_.refs_8_), channel_id=1, source_target_pairs={{0,8},{8,16},{16,24},{24,28},{28,20},{20,12},{12,4},{4,0},{1,9},{9... | collective-permute-start | bytes 3145736 | tf_op jit(solution)/shard_map/ppermute | solution.py:867
  145.9 40.9 %collective-permute-start.24 = (bf16[2,128,1024]{2,1,0:T(8,128)(2,1)S(1)}, bf16[2,128,1024]{2,1,0:T(8,128)(2,1)S(1)}, u32[]{:S(2)}, u32[]{:S(2)}) collective-permute-start(bf16[2,128,1024]{2,1,0:T(8,128)(2,1)S(1)} %slice.57), channel_id=1, source_target_pairs={{8,0},{16,8},{24,16},{28,24},{20,28},{12,20},{4,12},{0,4},{9,1},{1... | collective-permute-start | bytes 1572872 | tf_op jit(solution)/shard_map/ppermute | solution.py:867
  147.4 40.1 %collective-permute-start.23 = (bf16[2,128,1024]{2,1,0:T(8,128)(2,1)S(1)}, bf16[2,128,1024]{2,1,0:T(8,128)(2,1)S(1)}, u32[]{:S(2)}, u32[]{:S(2)}) collective-permute-start(bf16[2,128,1024]{2,1,0:T(8,128)(2,1)S(1)} %slice.56), channel_id=1, source_target_pairs={{0,8},{8,16},{16,24},{24,28},{28,20},{20,12},{12,4},{4,0},{1,9},{9... | collective-permute-start | bytes 1572872 | tf_op jit(solution)/shard_map/ppermute | solution.py:867
  169.9 22.4 %collective-permute-start.22 = (bf16[2,128,1024]{2,1,0:T(8,128)(2,1)S(1)}, bf16[2,128,1024]{2,1,0:T(8,128)(2,1)S(1)}, u32[]{:S(2)}, u32[]{:S(2)}) collective-permute-start(bf16[2,128,1024]{2,1,0:T(8,128)(2,1)S(1)} %slice.55), channel_id=1, source_target_pairs={{8,0},{16,8},{24,16},{28,24},{20,28},{12,20},{4,12},{0,4},{9,1},{1... | collective-permute-start | bytes 1572872 | tf_op jit(solution)/shard_map/ppermute | solution.py:867
  171.5 22.4 %collective-permute-start.21 = (bf16[2,128,1024]{2,1,0:T(8,128)(2,1)S(1)}, bf16[2,128,1024]{2,1,0:T(8,128)(2,1)S(1)}, u32[]{:S(2)}, u32[]{:S(2)}) collective-permute-start(bf16[2,128,1024]{2,1,0:T(8,128)(2,1)S(1)} %slice.54), channel_id=1, source_target_pairs={{0,8},{8,16},{16,24},{24,28},{28,20},{20,12},{12,4},{4,0},{1,9},{9... | collective-permute-start | bytes 1572872 | tf_op jit(solution)/shard_map/ppermute | solution.py:867
  185.5 22.1 %collective-permute-start.25 = (bf16[2,128,1024]{2,1,0:T(8,128)(2,1)}, bf16[2,128,1024]{2,1,0:T(8,128)(2,1)S(1)}, u32[]{:S(2)}, u32[]{:S(2)}) collective-permute-start(bf16[2,128,1024]{2,1,0:T(8,128)(2,1)} %get-tuple-element.264), channel_id=1, source_target_pairs={{0,8},{8,16},{16,24},{24,28},{28,20},{20,12},{12,4},{4,0},{1,9},{9... | collective-permute-start | bytes 1572872 | tf_op jit(solution)/shard_map/ppermute | solution.py:867
  186.7 20.9 %collective-permute-start.26 = (bf16[2,128,1024]{2,1,0:T(8,128)(2,1)}, bf16[2,128,1024]{2,1,0:T(8,128)(2,1)S(1)}, u32[]{:S(2)}, u32[]{:S(2)}) collective-permute-start(bf16[2,128,1024]{2,1,0:T(8,128)(2,1)} %get-tuple-element.265), channel_id=1, source_target_pairs={{8,0},{16,8},{24,16},{28,24},{20,28},{12,20},{4,12},{0,4},{9,1},{1... | collective-permute-start | bytes 1572872 | tf_op jit(solution)/shard_map/ppermute | solution.py:867
  205.6 15.1 %collective-permute-start.28 = (bf16[2,128,1024]{2,1,0:T(8,128)(2,1)}, bf16[2,128,1024]{2,1,0:T(8,128)(2,1)S(1)}, u32[]{:S(2)}, u32[]{:S(2)}) collective-permute-start(bf16[2,128,1024]{2,1,0:T(8,128)(2,1)} %get-tuple-element.272), channel_id=1, source_target_pairs={{8,0},{16,8},{24,16},{28,24},{20,28},{12,20},{4,12},{0,4},{9,1},{1... | collective-permute-start | bytes 1572872 | tf_op jit(solution)/shard_map/ppermute | solution.py:867
  207.2 15.1 %collective-permute-start.27 = (bf16[2,128,1024]{2,1,0:T(8,128)(2,1)}, bf16[2,128,1024]{2,1,0:T(8,128)(2,1)S(1)}, u32[]{:S(2)}, u32[]{:S(2)}) collective-permute-start(bf16[2,128,1024]{2,1,0:T(8,128)(2,1)} %get-tuple-element.270), channel_id=1, source_target_pairs={{0,8},{8,16},{16,24},{24,28},{28,20},{20,12},{12,4},{4,0},{1,9},{9... | collective-permute-start | bytes 1572872 | tf_op jit(solution)/shard_map/ppermute | solution.py:867
  211.0 17.2 %collective-permute-start.30 = (bf16[2,128,1024]{2,1,0:T(8,128)(2,1)}, bf16[2,128,1024]{2,1,0:T(8,128)(2,1)S(1)}, u32[]{:S(2)}, u32[]{:S(2)}) collective-permute-start(bf16[2,128,1024]{2,1,0:T(8,128)(2,1)} %get-tuple-element.278), channel_id=1, source_target_pairs={{8,0},{16,8},{24,16},{28,24},{20,28},{12,20},{4,12},{0,4},{9,1},{1... | collective-permute-start | bytes 1572872 | tf_op jit(solution)/shard_map/ppermute | solution.py:867
  212.6 16.9 %collective-permute-start.29 = (bf16[2,128,1024]{2,1,0:T(8,128)(2,1)}, bf16[2,128,1024]{2,1,0:T(8,128)(2,1)S(1)}, u32[]{:S(2)}, u32[]{:S(2)}) collective-permute-start(bf16[2,128,1024]{2,1,0:T(8,128)(2,1)} %get-tuple-element.276), channel_id=1, source_target_pairs={{0,8},{8,16},{16,24},{24,28},{28,20},{20,12},{12,4},{4,0},{1,9},{9... | collective-permute-start | bytes 1572872 | tf_op jit(solution)/shard_map/ppermute | solution.py:867
  245.0 23.1 %collective-permute-start.37 = (bf16[2,128,1024]{2,1,0:T(8,128)(2,1)S(1)}, bf16[2,128,1024]{2,1,0:T(8,128)(2,1)S(1)}, u32[]{:S(2)}, u32[]{:S(2)}) collective-permute-start(bf16[2,128,1024]{2,1,0:T(8,128)(2,1)S(1)} %copy-done.62), channel_id=1, source_target_pairs={{8,0},{16,8},{24,16},{28,24},{20,28},{12,20},{4,12},{0,4},{9,1},{1... | collective-permute-start | bytes 1572872 | tf_op jit(solution)/shard_map/ppermute | solution.py:867
  246.6 23.5 %collective-permute-start.36 = (bf16[2,128,1024]{2,1,0:T(8,128)(2,1)S(1)}, bf16[2,128,1024]{2,1,0:T(8,128)(2,1)S(1)}, u32[]{:S(2)}, u32[]{:S(2)}) collective-permute-start(bf16[2,128,1024]{2,1,0:T(8,128)(2,1)S(1)} %copy-done.61), channel_id=1, source_target_pairs={{0,8},{8,16},{16,24},{24,28},{28,20},{20,12},{12,4},{4,0},{1,9},{9... | collective-permute-start | bytes 1572872 | tf_op jit(solution)/shard_map/ppermute | solution.py:867
  264.1 35.7 %collective-permute-start.43 = (bf16[2,128,1024]{2,1,0:T(8,128)(2,1)S(1)}, bf16[2,128,1024]{2,1,0:T(8,128)(2,1)S(1)}, u32[]{:S(2)}, u32[]{:S(2)}) collective-permute-start(bf16[2,128,1024]{2,1,0:T(8,128)(2,1)S(1)} %get-tuple-element.318), channel_id=1, source_target_pairs={{8,0},{16,8},{24,16},{28,24},{20,28},{12,20},{4,12},{0,4},{9,1},{1... | collective-permute-start | bytes 1572872 | tf_op jit(solution)/shard_map/ppermute | solution.py:867
  268.2 31.7 %collective-permute-start.42 = (bf16[2,128,1024]{2,1,0:T(8,128)(2,1)S(1)}, bf16[2,128,1024]{2,1,0:T(8,128)(2,1)S(1)}, u32[]{:S(2)}, u32[]{:S(2)}) collective-permute-start(bf16[2,128,1024]{2,1,0:T(8,128)(2,1)S(1)} %get-tuple-element.317), channel_id=1, source_target_pairs={{0,8},{8,16},{16,24},{24,28},{28,20},{20,12},{12,4},{4,0},{1,9},{9... | collective-permute-start | bytes 1572872 | tf_op jit(solution)/shard_map/ppermute | solution.py:867
  285.4 14.4 %collective-permute-start.40 = (bf16[4,128,256]{2,1,0:T(8,128)(2,1)}, bf16[4,128,256]{2,1,0:T(8,128)(2,1)S(1)}, u32[]{:S(2)}, u32[]{:S(2)}) collective-permute-start(bf16[4,128,256]{2,1,0:T(8,128)(2,1)} %get-tuple-element.310), channel_id=1, source_target_pairs={{0,2},{1,3},{2,0},{3,1},{4,6},{5,7},{6,4},{7,5},{8,10},{9,11},{10,... | collective-permute-start | bytes 786440 | tf_op jit(solution)/shard_map/ppermute | solution.py:867
  305.0 26.8 %collective-permute-start.48 = (bf16[4,128,1024]{2,1,0:T(8,128)(2,1)}, bf16[4,128,1024]{2,1,0:T(8,128)(2,1)S(1)}, u32[]{:S(2)}, u32[]{:S(2)}) collective-permute-start(bf16[4,128,1024]{2,1,0:T(8,128)(2,1)} %get-tuple-element.335), channel_id=1, source_target_pairs={{8,0},{16,8},{24,16},{28,24},{20,28},{12,20},{4,12},{0,4},{9,1},{1... | collective-permute-start | bytes 3145736 | tf_op jit(solution)/shard_map/ppermute | solution.py:867
  305.9 26.0 %collective-permute-start.47 = (bf16[4,128,1024]{2,1,0:T(8,128)(2,1)}, bf16[4,128,1024]{2,1,0:T(8,128)(2,1)S(1)}, u32[]{:S(2)}, u32[]{:S(2)}) collective-permute-start(bf16[4,128,1024]{2,1,0:T(8,128)(2,1)} %get-tuple-element.333), channel_id=1, source_target_pairs={{0,8},{8,16},{16,24},{24,28},{28,20},{20,12},{12,4},{4,0},{1,9},{9... | collective-permute-start | bytes 3145736 | tf_op jit(solution)/shard_map/ppermute | solution.py:867
  307.0 24.7 %collective-permute-start.46 = (bf16[4,128,256]{2,1,0:T(8,128)(2,1)S(1)}, bf16[4,128,256]{2,1,0:T(8,128)(2,1)S(1)}, u32[]{:S(2)}, u32[]{:S(2)}) collective-permute-start(bf16[4,128,256]{2,1,0:T(8,128)(2,1)S(1)} %copy-done.65), channel_id=1, source_target_pairs={{0,3},{1,2},{2,1},{3,0},{4,7},{5,6},{6,5},{7,4},{8,11},{9,10},{10,... | collective-permute-start | bytes 786440 | tf_op jit(solution)/shard_map/ppermute | solution.py:867
  307.0 24.8 %collective-permute-start.45 = (bf16[4,128,256]{2,1,0:T(8,128)(2,1)S(1)}, bf16[4,128,256]{2,1,0:T(8,128)(2,1)S(1)}, u32[]{:S(2)}, u32[]{:S(2)}) collective-permute-start(bf16[4,128,256]{2,1,0:T(8,128)(2,1)S(1)} %copy-done.64), channel_id=1, source_target_pairs={{0,2},{1,3},{2,0},{3,1},{4,6},{5,7},{6,4},{7,5},{8,10},{9,11},{10,... | collective-permute-start | bytes 786440 | tf_op jit(solution)/shard_map/ppermute | solution.py:867
  308.2 23.6 %collective-permute-start.44 = (bf16[4,128,256]{2,1,0:T(8,128)(2,1)S(1)}, bf16[4,128,256]{2,1,0:T(8,128)(2,1)S(1)}, u32[]{:S(2)}, u32[]{:S(2)}) collective-permute-start(bf16[4,128,256]{2,1,0:T(8,128)(2,1)S(1)} %copy-done.63), channel_id=1, source_target_pairs={{0,1},{1,0},{2,3},{3,2},{4,5},{5,4},{6,7},{7,6},{8,9},{9,8},{10,11... | collective-permute-start | bytes 786440 | tf_op jit(solution)/shard_map/ppermute | solution.py:867
  346.3 14.5 %collective-permute-start.51 = (bf16[1,256,1024]{2,1,0:T(8,128)(2,1)}, bf16[1,256,1024]{2,1,0:T(8,128)(2,1)S(1)}, u32[]{:S(2)}, u32[]{:S(2)}) collective-permute-start(bf16[1,256,1024]{2,1,0:T(8,128)(2,1)} %bitcast.89), channel_id=1, source_target_pairs={{0,2},{1,3},{2,0},{3,1},{4,6},{5,7},{6,4},{7,5},{8,10},{9,11},{10,... | collective-permute-start | bytes 1572872 | tf_op jit(solution)/shard_map/ppermute | solution.py:867
  347.1 35.1 %collective-permute-start.53 = (bf16[4,128,1024]{2,1,0:T(8,128)(2,1)}, bf16[4,128,1024]{2,1,0:T(8,128)(2,1)S(1)}, u32[]{:S(2)}, u32[]{:S(2)}) collective-permute-start(bf16[4,128,1024]{2,1,0:T(8,128)(2,1)} %get-tuple-element.362), channel_id=1, source_target_pairs={{8,0},{16,8},{24,16},{28,24},{20,28},{12,20},{4,12},{0,4},{9,1},{1... | collective-permute-start | bytes 3145736 | tf_op jit(solution)/shard_map/ppermute | solution.py:867
  347.9 34.3 %collective-permute-start.52 = (bf16[4,128,1024]{2,1,0:T(8,128)(2,1)}, bf16[4,128,1024]{2,1,0:T(8,128)(2,1)S(1)}, u32[]{:S(2)}, u32[]{:S(2)}) collective-permute-start(bf16[4,128,1024]{2,1,0:T(8,128)(2,1)} %get-tuple-element.360), channel_id=1, source_target_pairs={{0,8},{8,16},{16,24},{24,28},{28,20},{20,12},{12,4},{4,0},{1,9},{9... | collective-permute-start | bytes 3145736 | tf_op jit(solution)/shard_map/ppermute | solution.py:867
  365.6 37.0 %all-to-all-start = ((bf16[8,33,1024]{2,1,0:T(8,128)(2,1)}), bf16[8,33,1024]{2,1,0:T(8,128)(2,1)S(1)}, u32[]{:S(2)}, u32[]{:S(2)}) async-start(bf16[8,33,1024]{2,1,0:T(8,128)(2,1)} %fusion.1), calls=%async_computation | async-start | bytes 1310720 | tf_op jit(solution)/shard_map/all_to_all | solution.py:1099
  387.7 32.0 %collective-permute-start.59 = (bf16[4,128,1024]{2,1,0:T(8,128)(2,1)}, bf16[4,128,1024]{2,1,0:T(8,128)(2,1)}, u32[]{:S(2)}, u32[]{:S(2)}) collective-permute-start(bf16[4,128,1024]{2,1,0:T(8,128)(2,1)} %get-tuple-element.377), channel_id=1, source_target_pairs={{8,0},{16,8},{24,16},{28,24},{20,28},{12,20},{4,12},{0,4},{9,1},{1... | collective-permute-start | bytes 3145736 | tf_op jit(solution)/shard_map/ppermute | solution.py:867
  389.7 30.0 %collective-permute-start.58 = (bf16[4,128,1024]{2,1,0:T(8,128)(2,1)}, bf16[4,128,1024]{2,1,0:T(8,128)(2,1)}, u32[]{:S(2)}, u32[]{:S(2)}) collective-permute-start(bf16[4,128,1024]{2,1,0:T(8,128)(2,1)} %get-tuple-element.375), channel_id=1, source_target_pairs={{0,8},{8,16},{16,24},{24,28},{28,20},{20,12},{12,4},{4,0},{1,9},{9... | collective-permute-start | bytes 3145736 | tf_op jit(solution)/shard_map/ppermute | solution.py:867
  419.4 26.4 %collective-permute-start.62 = (bf16[1,2080,256]{2,1,0:T(8,128)(2,1)S(1)}, bf16[1,2080,256]{2,1,0:T(8,128)(2,1)S(1)}, u32[]{:S(2)}, u32[]{:S(2)}) collective-permute-start(bf16[1,2080,256]{2,1,0:T(8,128)(2,1)S(1)} %copy-done.22), channel_id=1, source_target_pairs={{0,2},{1,3},{2,0},{3,1},{4,6},{5,7},{6,4},{7,5},{8,10},{9,11},{10,... | collective-permute-start | bytes 3194888 | tf_op jit(solution)/shard_map/ppermute | solution.py:867
  431.3 21.4 %collective-permute-start.65 = (bf16[4,128,256]{2,1,0:T(8,128)(2,1)}, bf16[4,128,256]{2,1,0:T(8,128)(2,1)}, u32[]{:S(2)}, u32[]{:S(2)}) collective-permute-start(bf16[4,128,256]{2,1,0:T(8,128)(2,1)} %get-tuple-element.398), channel_id=1, source_target_pairs={{0,3},{1,2},{2,1},{3,0},{4,7},{5,6},{6,5},{7,4},{8,11},{9,10},{10,... | collective-permute-start | bytes 786440 | tf_op jit(solution)/shard_map/ppermute | solution.py:867
  431.4 21.4 %collective-permute-start.64 = (bf16[4,128,256]{2,1,0:T(8,128)(2,1)}, bf16[4,128,256]{2,1,0:T(8,128)(2,1)}, u32[]{:S(2)}, u32[]{:S(2)}) collective-permute-start(bf16[4,128,256]{2,1,0:T(8,128)(2,1)} %get-tuple-element.396), channel_id=1, source_target_pairs={{0,2},{1,3},{2,0},{3,1},{4,6},{5,7},{6,4},{7,5},{8,10},{9,11},{10,... | collective-permute-start | bytes 786440 | tf_op jit(solution)/shard_map/ppermute | solution.py:867
  433.3 19.5 %collective-permute-start.63 = (bf16[4,128,256]{2,1,0:T(8,128)(2,1)}, bf16[4,128,256]{2,1,0:T(8,128)(2,1)}, u32[]{:S(2)}, u32[]{:S(2)}) collective-permute-start(bf16[4,128,256]{2,1,0:T(8,128)(2,1)} %get-tuple-element.394), channel_id=1, source_target_pairs={{0,1},{1,0},{2,3},{3,2},{4,5},{5,4},{6,7},{7,6},{8,9},{9,8},{10,11... | collective-permute-start | bytes 786440 | tf_op jit(solution)/shard_map/ppermute | solution.py:867
  433.3 46.6 %all-to-all-start.1 = ((bf16[8,384,256]{2,1,0:T(8,128)(2,1)}), bf16[8,384,256]{2,1,0:T(8,128)(2,1)}, u32[]{:S(2)}, u32[]{:S(2)}) async-start(bf16[8,384,256]{2,1,0:T(8,128)(2,1)} %get-tuple-element.411), calls=%async_computation.1 | async-start | bytes 3145728 | tf_op jit(solution)/shard_map/all_to_all | solution.py:1135
  455.3 14.8 %collective-permute-start.66 = (bf16[1,8,32,1024]{3,2,1,0:T(8,128)(2,1)S(1)}, bf16[1,8,32,1024]{3,2,1,0:T(8,128)(2,1)S(1)}, u32[]{:S(2)}, u32[]{:S(2)}) collective-permute-start(bf16[1,8,32,1024]{3,2,1,0:T(8,128)(2,1)S(1)} %bitcast.69), channel_id=1, source_target_pairs={{0,2},{1,3},{2,0},{3,1},{4,6},{5,7},{6,4},{7,5},{8,10},{9,11},{10,... | collective-permute-start | bytes 1572872 | tf_op jit(solution)/shard_map/ppermute | solution.py:867
  455.6 14.5 %collective-permute-start.67 = (f32[4,1,256]{2,1,0:T(1,128)S(1)}, f32[4,1,256]{2,1,0:T(1,128)S(1)}, u32[]{:S(2)}, u32[]{:S(2)}) collective-permute-start(f32[4,1,256]{2,1,0:T(1,128)S(1)} %add.23), channel_id=1, source_target_pairs={{0,2},{1,3},{2,0},{3,1},{4,6},{5,7},{6,4},{7,5},{8,10},{9,11},{10,... | collective-permute-start | bytes 12296 | tf_op jit(solution)/shard_map/ppermute | solution.py:867
  (90 other events, 834.6 us)
